TPU v7x, 128 devices: a whole 4x4x4 slice. The times are simulated.
128 devices in a mesh: fsdp: 16 (over y_hi, z, core), rep: 8 (over x, y_lo).
Axes of the slice: x: 4, y: 4 (y_hi: 2, y_lo: 2; y = y_hi * 2 + y_lo), z: 4, core: 2. Of those that a mesh axis runs over, the one named last changes fastest.
Arguments:
- tokens: bfloat16 [32768, 1536], P(('fsdp', 'rep')), may hold values from -6 to 6
- cotangent: bfloat16 [32768, 1536], P(('fsdp', 'rep')), may hold values from -6 to 6
- lengths: int32 [16, 3], replicated, may hold values from 1 to 2046, as said below
- w_in: float32 [1536, 6400], P('fsdp'), may hold values from -0.15625 to 0.15625
- w_dt: float32 [1536, 48], P('fsdp'), may hold values from -0.15625 to 0.15625
- w_out: float32 [3072, 1536], P('fsdp'), may hold values from -0.109375 to 0.109375
- small: float32 [21392], P('fsdp'), may hold values from -6 to 1.5
- first_in: float32 [1536, 6400], P('fsdp'), may hold values from -80 to 80
- first_dt: float32 [1536, 48], P('fsdp'), may hold values from -12 to 12
- first_out: float32 [3072, 1536], P('fsdp'), may hold values from -128 to 128
- first_small: float32 [21392], P('fsdp'), may hold values from -64 to 64
- second_in: float32 [1536, 6400], P('fsdp'), may hold values from 16.384 to 65.536
- second_dt: float32 [1536, 48], P('fsdp'), may hold values from 0.32768 to 1.31072
- second_out: float32 [3072, 1536], P('fsdp'), may hold values from 32.768 to 131.072
- second_small: float32 [21392], P('fsdp'), may hold values from 8.192 to 32.768
Outputs:
- block_out: float32 [32768, 1536], P(('fsdp', 'rep'))
- input_grad: float32 [32768, 1536], P(('fsdp', 'rep'))
- grad_in: float32 [1536, 6400], P('fsdp')
- grad_dt: float32 [1536, 48], P('fsdp')
- grad_out: float32 [3072, 1536], P('fsdp')
- grad_small: float32 [21392], P('fsdp')
- new_first_in: float32 [1536, 6400], P('fsdp')
- new_first_dt: float32 [1536, 48], P('fsdp')
- new_first_out: float32 [3072, 1536], P('fsdp')
- new_first_small: float32 [21392], P('fsdp')
- new_second_in: float32 [1536, 6400], P('fsdp')
- new_second_dt: float32 [1536, 48], P('fsdp')
- new_second_out: float32 [3072, 1536], P('fsdp')
- new_second_small: float32 [21392], P('fsdp')
- new_in: float32 [1536, 6400], P('fsdp')
- new_dt: float32 [1536, 48], P('fsdp')
- new_out: float32 [3072, 1536], P('fsdp')
- new_small: float32 [21392], P('fsdp')
Inputs may be any that keep to these rules, and one draw needn't show every extreme that they name: Row f holds the lengths of the three sequences that fill pack f from its position 0; the rest of its 2048 positions is padding. The first and third are at most 64 long, the padding at most 128, so the second begins within the first 256 positions and ends within the last 256. In every draw some pack has first and third sequences of length 1 and no padding.
All inputs are finite; a program needn't handle non-finite values.
Results may differ from a plain program's by a relative error of at most 0.003.
The roundings to bfloat16 on the way count: a program that leaves them out, or rounds other values in their place, can miss the bound.
Values may be sent and summed in bfloat16 or wider, within the bound.
No kernel may reach another device: no remote copies, remote signals or barrier semaphores. Data moves between devices by JAX's collectives and lax.ppermute only.
A program may use at most 320 MiB of HBM per device.

v0:
```python
from functools import partial

import jax
import jax.numpy as jnp
from jax import lax
from jax.experimental import pallas as pl
from jax.experimental.pallas import tpu as pltpu
from jax.sharding import PartitionSpec as P

D = 1536
H = 48
P_SIZE = 64
N = 128
CONV = 4
STEP = 10
DI = 3072
CHANNELS = DI + 2 * N
SMALL = 21392
N_FSDP = 16
N_REP = 8
ROWS = 256
PACK = 2048
OWN = DI // N_REP
OWN_H = H // N_REP
OWN_BC = 2 * N // N_REP
SHARD_IN = D // N_FSDP
SHARD_OUT = DI // N_FSDP
SHARD_SMALL = SMALL // N_FSDP
WIDE = 384
CHUNK = 128
CHUNKS = PACK // CHUNK
HALF = CHUNKS // 2
TAIL = 512
VMEM_LIMIT = 60 * 1024 * 1024

NORM_EPS = 1e-05
BETA_ONE = 0.9
BETA_TWO = 0.999
ADAM_EPS = 1e-08
WEIGHT_DECAY = 0.1
RATE_MATRIX = 0.04
RATE_SMALL = 0.4
PRECISE = lax.Precision.HIGHEST
BF16 = jnp.bfloat16
F32 = jnp.float32
COST = pl.CostEstimate(flops=1_000_000, bytes_accessed=100_000, transcendentals=0)
FILL = pl.CostEstimate(flops=2_400_000_000, bytes_accessed=20_000_000, transcendentals=0)


def move(value, target):
    pairs = []
    for f in range(N_FSDP):
        for r in range(N_REP):
            yh, z, c, x, yl = target(f // 8, (f // 2) % 4, f % 2, r // 2, r % 2)
            pairs.append((f * N_REP + r, ((yh % 2) * 8 + (z % 4) * 2 + c % 2) * N_REP + (x % 4) * 2 + yl % 2))
    return lax.ppermute(value, ("fsdp", "rep"), pairs)


def along_x(steps):
    return lambda yh, z, c, x, yl: (yh, z, c, x + steps, yl)


def along_z(steps):
    return lambda yh, z, c, x, yl: (yh, z + steps, c, x, yl)


def swap_y(yh, z, c, x, yl):
    return (yh, z, c, x, yl + 1)


def swap_y_hi(yh, z, c, x, yl):
    return (yh + 1, z, c, x, yl)


def swap_core(yh, z, c, x, yl):
    return (yh, z, c + 1, x, yl)


class Place:
    def __init__(self):
        f = lax.axis_index("fsdp")
        r = lax.axis_index("rep")
        self.f, self.r = f, r
        self.yh, self.z, self.c = f // 8, (f // 2) % 4, f % 2
        self.x, self.yl = r // 2, r % 2


def at(value, index, axis=0):
    return lax.dynamic_index_in_dim(value, index, axis, keepdims=False)


def tie(values, *others):
    return lax.optimization_barrier((values, others))[0]


def both(mine, other, second):
    first = jnp.where(second == 0, mine, other)
    last = jnp.where(second == 0, other, mine)
    return jnp.stack([first, last], 0)


def put(out, piece, axis, index):
    starts = [jnp.int32(0)] * out.ndim
    starts[axis] = jnp.int32(index)
    return lax.dynamic_update_slice(out, jnp.expand_dims(piece, axis), tuple(starts))


def swap_shards(value, place):
    other = move(value, lambda yh, z, c, x, yl: (yh + 1, z, c, x, yl + 1))
    return both(value, other, place.yh)


def gather_eight(pair):
    groups = [list(range(8)), list(range(8, 16))]
    out = lax.all_gather(pair, "fsdp", axis=0, tiled=True, axis_index_groups=groups)
    return out.reshape((4, 2) + pair.shape)


def exchange(value, axis):
    return lax.all_to_all(value, axis, 0, 0, tiled=True)


def share_rep(value):
    return exchange(jnp.broadcast_to(value[None], (N_REP,) + value.shape), "rep")


def sum_z(value):
    steps = [move(value, along_z(step)) for step in (1, 3, 2)]
    return value + steps[0] + steps[1] + steps[2]


def scatter_eight(value):
    groups = [list(range(8)), list(range(8, 16))]
    flat = value.reshape(-1, value.shape[-1])
    out = lax.psum_scatter(flat, "fsdp", scatter_dimension=0, tiled=True, axis_index_groups=groups)
    return out.reshape((2,) + value.shape[1:])


def eight_order(f):
    return ((f // 2) % 4 * 2 + f % 2) * 2 + f // 8


def with_rows(block, extra):
    width = block.shape[-1]
    flat = block.reshape(-1, width)
    return flat if extra is None else jnp.concatenate([flat, extra], 0)


def adam_update(weight, gradient, moment_one, moment_two, learn_rate, decay_rate):
    moment_one = BETA_ONE * moment_one + (1.0 - BETA_ONE) * gradient
    moment_two = BETA_TWO * moment_two + (1.0 - BETA_TWO) * gradient * gradient
    scaled = (
        moment_one
        / (1.0 - BETA_ONE**STEP)
        / (jnp.sqrt(moment_two / (1.0 - BETA_TWO**STEP)) + ADAM_EPS)
    )
    return (weight - learn_rate * (scaled + decay_rate * weight), moment_one, moment_two)


def contract_rows(left_side, right_side):
    return lax.dot_general(
        left_side, right_side, (((0,), (0,)), ((), ())), preferred_element_type=F32
    )


def contract_cols(left_side, right_side):
    return lax.dot_general(
        left_side, right_side, (((1,), (1,)), ((), ())), preferred_element_type=F32
    )


def matmul(left_side, right_side):
    return jnp.dot(left_side, right_side, preferred_element_type=F32)


def segment_at(positions, seg_ends):
    counted = jnp.sum((positions[:, None] >= seg_ends[None, :]).astype(jnp.int32), axis=1)
    return jnp.where(positions < 0, jnp.int32(-1), counted)


def split_two(value):
    high = value.astype(BF16)
    return high, (value - high.astype(F32)).astype(BF16)


def split_three(value):
    high = value.astype(BF16)
    rest = value - high.astype(F32)
    middle = rest.astype(BF16)
    return high, middle, (rest - middle.astype(F32)).astype(BF16)


def product(left, right, left_dim, right_dim):
    return lax.dot_general(
        left, right, (((left_dim,), (right_dim,)), ((), ())), preferred_element_type=F32
    )


def joined_product(left_parts, right_parts, left_dim=1, right_dim=0):
    left_high, left_low = left_parts
    right_high, right_low = right_parts
    return product(
        jnp.concatenate([left_high, left_high, left_low], left_dim),
        jnp.concatenate([right_high, right_low, right_high], right_dim),
        left_dim,
        right_dim,
    )


def precise_product(left, right, left_dim=1, right_dim=0):
    return joined_product(split_two(left), split_two(right), left_dim, right_dim)


def ones_product(ones, value):
    return product(jnp.concatenate([ones] * 3, 1), jnp.concatenate(split_three(value), 0), 1, 0)


def spread(per_head, lane):
    return jnp.concatenate(
        [
            jnp.where(lane < P_SIZE, per_head[:, 2 * k : 2 * k + 1], per_head[:, 2 * k + 1 : 2 * k + 2])
            for k in range(OWN_H // 2)
        ],
        1,
    )


def head_sums(value):
    column = lax.broadcasted_iota(jnp.int32, (OWN, N), 0)
    head = lax.broadcasted_iota(jnp.int32, (OWN, N), 1)
    members = ((column >= head * P_SIZE) & (column < (head + 1) * P_SIZE)).astype(F32).astype(BF16)
    high, low = split_two(value)
    return product(jnp.concatenate([high, low], 1), jnp.concatenate([members, members], 0), 1, 0)


def two_heads(pair, lane):
    zero = jnp.zeros_like(pair)
    return jnp.concatenate([jnp.where(lane < P_SIZE, pair, zero), jnp.where(lane < P_SIZE, zero, pair)], 0)


def chunk_facts(ends, chunk, dt_pre, par):
    column = lax.broadcasted_iota(jnp.int32, (CHUNK, 1), 0) + chunk * CHUNK
    row = lax.broadcasted_iota(jnp.int32, (1, CHUNK), 1) + chunk * CHUNK

    def segment(position):
        counted = jnp.zeros_like(position)
        for k in range(3):
            counted = counted + (position >= ends[k]).astype(jnp.int32)
        return jnp.where(position < 0, -1, counted)

    def one_segment(position):
        counted = jnp.int32(0)
        for k in range(3):
            counted = counted + (position >= ends[k]).astype(jnp.int32)
        return jnp.where(position < 0, -1, counted)

    here_column, here_row = segment(column), segment(row)
    prior = one_segment(chunk * CHUNK - 1)
    last = one_segment(chunk * CHUNK + CHUNK - 1)
    lane = lax.broadcasted_iota(jnp.int32, (CHUNK, N), 1)
    shifted = dt_pre + par[6:7, :N]
    soft = jnp.maximum(shifted, 0.0) + jnp.log1p(jnp.exp(-jnp.abs(shifted)))
    step = jnp.where(lane < OWN_H, soft, 0.0)
    decay = step * par[7:8, :N]
    tri_row = lax.broadcasted_iota(jnp.int32, (CHUNK, CHUNK), 0)
    tri_column = lax.broadcasted_iota(jnp.int32, (CHUNK, CHUNK), 1)
    lower = (tri_row >= tri_column).astype(F32).astype(BF16)
    upper = (tri_row <= tri_column).astype(F32).astype(BF16)
    total = ones_product(lower, decay)
    entering = (here_column == prior).astype(F32) * jnp.exp(total)
    end = total[CHUNK - 1 : CHUNK]
    leaving = (here_column == last).astype(F32) * jnp.exp(jnp.minimum(end - total, 0.0))
    passing = jnp.where(last == prior, 1.0, 0.0) * jnp.exp(end)
    return dict(
        column=column,
        segment=segment,
        here_column=here_column,
        here_row=here_row,
        lane=lane,
        shifted=shifted,
        step=step,
        decay=decay,
        total=total,
        entering=entering,
        leaving=leaving,
        passing=passing,
        tri_row=tri_row,
        tri_column=tri_column,
        upper=upper,
    )


def forward_kernel(part, ends, proj, par, *refs):
    if part:
        carry_in, refs = refs[3], refs[4:]
    pre_out, mixed_out, state_out, carry_out, extended, state = refs
    chunk = pl.program_id(0) + part * HALF

    @pl.when(pl.program_id(0) == 0)
    def _():
        if part:
            state[...] = carry_in[:N, :OWN]
            extended[0:8, :] = carry_in[N:, :]
        else:
            state[...] = jnp.zeros_like(state)
            extended[0:8, :] = jnp.zeros((8, 640), F32)

    facts = chunk_facts(ends, chunk, proj[:, 1024:1152], par)
    lane = facts["lane"]
    conv = proj[:, OWN:1024].astype(BF16).astype(F32)
    extended[8 : 8 + CHUNK, :] = conv
    pre = par[4:5] + par[3:4] * conv
    for back in range(1, CONV):
        same = (facts["segment"](facts["column"] - back) == facts["here_column"]).astype(F32)
        pre = pre + par[3 - back : 4 - back] * (extended[8 - back : 8 - back + CHUNK, :] * same)
    extended[0:8, :] = extended[CHUNK : CHUNK + 8, :]
    pre_out[...] = pre
    act = pre * jax.nn.sigmoid(pre)
    own_x, state_b, state_c = act[:, :OWN], act[:, OWN : OWN + N], act[:, OWN + N :]
    stepped = own_x * spread(facts["step"], lane)
    b_parts, c_parts = split_two(state_b), split_two(state_c)
    inside = (facts["tri_row"] >= facts["tri_column"]) & (facts["here_column"] == facts["here_row"])
    scores = jnp.where(inside, joined_product(c_parts, b_parts, 1, 1), 0.0)
    total_rows = facts["total"].T
    state_in = state[...]
    state_out[...] = state_in
    outs = []
    for pair in range(OWN_H // 2):
        mixing = []
        for head in (2 * pair, 2 * pair + 1):
            span = facts["total"][:, head : head + 1] - total_rows[head : head + 1, :]
            mixing.append(jnp.exp(jnp.minimum(span, 0.0)) * scores)
        inner = two_heads(stepped[:, pair * N : pair * N + N], lane)
        outs.append(precise_product(jnp.concatenate(mixing, 1), inner))
    scanned = jnp.concatenate(outs, 1) + spread(facts["entering"], lane) * joined_product(
        c_parts, split_two(state_in)
    )
    state[...] = spread(facts["passing"], lane[:1]) * state_in + precise_product(
        state_b.T, stepped * spread(facts["leaving"], lane)
    )
    mixed_out[...] = scanned + par[5:6, :OWN] * own_x

    @pl.when(pl.program_id(0) == HALF - 1)
    def _():
        carry_out[:N, :OWN] = state[...]
        carry_out[:N, OWN:] = jnp.zeros((N, 640 - OWN), F32)
        carry_out[N:, :] = extended[0:8, :]


def run_forward(part, ends, proj, par, before=()):
    here = lambda i: (i + part * HALF, 0)
    chunked = lambda width: pl.BlockSpec((CHUNK, width), here)
    fixed = lambda shape: pl.BlockSpec(shape, lambda i: (0, 0))
    carry = fixed((N + 8, 640))
    return pl.pallas_call(
        partial(forward_kernel, part),
        grid=(HALF,),
        in_specs=[pl.BlockSpec(memory_space=pltpu.SMEM), chunked(1152), fixed((16, 640))]
        + ([pl.BlockSpec(memory_space=pl.ANY)] * 3 + [carry] if part else []),
        out_specs=[chunked(640), chunked(OWN), pl.BlockSpec((N, OWN), here), carry],
        out_shape=[
            jax.ShapeDtypeStruct((PACK, 640), F32),
            jax.ShapeDtypeStruct((PACK, OWN), F32),
            jax.ShapeDtypeStruct((CHUNKS * N, OWN), F32),
            jax.ShapeDtypeStruct((N + 8, 640), F32),
        ],
        input_output_aliases={3: 0, 4: 1, 5: 2} if part else {},
        scratch_shapes=[pltpu.VMEM((CHUNK + 8, 640), F32), pltpu.VMEM((N, OWN), F32)],
        compiler_params=pltpu.CompilerParams(
            dimension_semantics=("arbitrary",), vmem_limit_bytes=VMEM_LIMIT
        ),
        cost_estimate=COST,
        name="scan_forward",
    )(ends, proj, par, *before)


def backward_kernel(ends, conv_in, dt_in, pre_in, mixed_in, grad_mixed, state_all, par, *refs):
    grad_x, grad_dt, grad_bc, sums, head_acc, carried, extended, end_dot = refs
    step_index = pl.program_id(0)
    chunk = CHUNKS - 1 - step_index

    @pl.when(step_index == 0)
    def _():
        carried[...] = jnp.zeros_like(carried)
        extended[CHUNK : CHUNK + 8, :] = jnp.zeros((8, OWN), F32)
        end_dot[...] = jnp.zeros_like(end_dot)
        sums[...] = jnp.zeros_like(sums)
        head_acc[...] = jnp.zeros_like(head_acc)

    facts = chunk_facts(ends, chunk, dt_in[...], par)
    lane = facts["lane"]
    pre = pre_in[...]
    sig = jax.nn.sigmoid(pre)
    act = pre * sig
    own_x, state_b, state_c = act[:, :OWN], act[:, OWN : OWN + N], act[:, OWN + N :]
    step = facts["step"]
    step_wide = spread(step, lane)
    stepped = own_x * step_wide
    skip = par[5:6, :OWN]
    scanned = mixed_in[...] - skip * own_x
    grad_m = grad_mixed[...]
    sums[6:7] += jnp.sum(grad_m * own_x, 0, keepdims=True)

    b_parts, c_parts = split_two(state_b), split_two(state_c)
    inside = (facts["tri_row"] <= facts["tri_column"]) & (facts["here_column"] == facts["here_row"])
    scores = jnp.where(inside, joined_product(b_parts, c_parts, 1, 1), 0.0)
    total_rows = facts["total"].T
    grad_scores = jnp.zeros((CHUNK, CHUNK), F32)
    grad_stepped = []
    for pair in range(OWN_H // 2):
        columns = slice(pair * N, pair * N + N)
        grad_pair = grad_m[:, columns]
        high, low = split_two(grad_pair)
        stepped_parts = split_two(two_heads(stepped[:, columns], lane))
        grad_mixing = joined_product(stepped_parts, (high, low), 1, 1)
        mixing = []
        for k in range(2):
            head = 2 * pair + k
            span = total_rows[head : head + 1, :] - facts["total"][:, head : head + 1]
            decays = jnp.exp(jnp.minimum(span, 0.0))
            mixing.append(decays * scores)
            grad_scores = grad_scores + decays * grad_mixing[k * CHUNK : (k + 1) * CHUNK]
        grad_stepped.append(
            joined_product(
                split_two(jnp.concatenate(mixing, 1)), (two_heads(high, lane), two_heads(low, lane))
            )
        )
    grad_scores = jnp.where(inside, grad_scores, 0.0)
    carry = carried[...]
    carry_parts = split_two(carry)
    leaving = spread(facts["leaving"], lane)
    grad_stepped = jnp.concatenate(grad_stepped, 1) + leaving * joined_product(b_parts, carry_parts)
    state_in = state_all[...]
    entered = spread(facts["entering"], lane) * grad_m
    entered_parts = split_two(entered)
    grad_b = precise_product(grad_scores, state_c) + joined_product(
        split_two(leaving * stepped), carry_parts, 1, 1
    )
    grad_c = precise_product(grad_scores.T, state_b) + joined_product(
        entered_parts, split_two(state_in), 1, 1
    )
    grad_bc[0:N, :] = grad_b.T.astype(BF16)
    grad_bc[N:, :] = grad_c.T.astype(BF16)
    new_carry = spread(facts["passing"], lane[:1]) * carry + joined_product(
        split_two(state_c.T), entered_parts
    )
    carried[...] = new_carry

    grad_step = head_sums(own_x * grad_stepped)
    last_row = lax.broadcasted_iota(jnp.int32, (CHUNK, N), 0) == CHUNK - 1
    grad_total = head_sums(grad_m * scanned) - step * grad_step
    grad_total = grad_total + jnp.where(last_row, end_dot[0:1, :], 0.0)
    grad_decay = ones_product(facts["upper"], grad_total)
    end_dot[...] = head_sums(
        jnp.broadcast_to(jnp.sum(new_carry * state_in, 0, keepdims=True), (8, OWN))
    )
    grad_pre_dt = (grad_step + grad_decay * par[7:8, :N]) * jax.nn.sigmoid(facts["shifted"])
    grad_pre_dt = jnp.where(lane < OWN_H, grad_pre_dt, 0.0)
    grad_dt[...] = grad_pre_dt.astype(BF16)
    head_acc[0:1] += jnp.sum(grad_pre_dt, 0, keepdims=True)
    head_acc[1:2] += jnp.sum(grad_decay * facts["decay"], 0, keepdims=True)

    sig_x, pre_x = sig[:, :OWN], pre[:, :OWN]
    grad_pre = (step_wide * grad_stepped + skip * grad_m) * (sig_x * (1.0 + pre_x * (1.0 - sig_x)))
    extended[0:CHUNK, :] = grad_pre
    conv = conv_in[...].astype(BF16).astype(F32)
    sums[5:6] += jnp.sum(grad_pre, 0, keepdims=True)
    sums[4:5] += jnp.sum(conv * grad_pre, 0, keepdims=True)
    grad_conv = par[3:4, :OWN] * grad_pre
    for ahead in range(1, CONV):
        same = (facts["segment"](facts["column"] + ahead) == facts["here_column"]).astype(F32)
        later = extended[ahead : ahead + CHUNK, :] * same
        sums[4 - ahead : 5 - ahead] += jnp.sum(conv * later, 0, keepdims=True)
        grad_conv = grad_conv + par[3 - ahead : 4 - ahead, :OWN] * later
    extended[CHUNK : CHUNK + 8, :] = extended[0:8, :]
    grad_x[...] = grad_conv.astype(BF16)


def run_backward(ends, proj, pre, mixed, grad_mixed, states, par):
    last = CHUNKS - 1
    chunked = lambda width, column=0: pl.BlockSpec((CHUNK, width), lambda i: (last - i, column))
    fixed = lambda shape: pl.BlockSpec(shape, lambda i: (0, 0))
    return pl.pallas_call(
        backward_kernel,
        grid=(CHUNKS,),
        in_specs=[
            pl.BlockSpec(memory_space=pltpu.SMEM),
            chunked(OWN, 1),
            chunked(N, 8),
            chunked(640),
            chunked(OWN),
            chunked(OWN),
            pl.BlockSpec((N, OWN), lambda i: (last - i, 0)),
            fixed((16, 640)),
        ],
        out_specs=[
            chunked(OWN),
            chunked(N),
            pl.BlockSpec((2 * N, CHUNK), lambda i: (0, last - i)),
            fixed((8, OWN)),
            fixed((8, N)),
        ],
        out_shape=[
            jax.ShapeDtypeStruct((PACK, OWN), BF16),
            jax.ShapeDtypeStruct((PACK, N), BF16),
            jax.ShapeDtypeStruct((2 * N, PACK), BF16),
            jax.ShapeDtypeStruct((8, OWN), F32),
            jax.ShapeDtypeStruct((8, N), F32),
        ],
        scratch_shapes=[
            pltpu.VMEM((N, OWN), F32),
            pltpu.VMEM((CHUNK + 8, OWN), F32),
            pltpu.VMEM((8, N), F32),
        ],
        compiler_params=pltpu.CompilerParams(
            dimension_semantics=("arbitrary",), vmem_limit_bytes=VMEM_LIMIT
        ),
        cost_estimate=COST,
        name="scan_backward",
    )(ends, proj, proj, pre, mixed, grad_mixed, states, par)


PARTS = (1, 1, 1, 1, 1, 2, 1, 1)


def piece_copies(pieces, parts, blocks, sems):
    copies = []
    taken = 0
    for slot, count in enumerate(parts):
        rows = ROWS // count
        copies.append(
            [
                pltpu.make_async_copy(
                    pieces[taken + k], blocks.at[slot, pl.ds(k * rows, rows)], sems.at[taken + k]
                )
                for k in range(count)
            ]
        )
        taken += count
    return copies


def fetch_block(pieces, parts, blocks, sems):
    copies = piece_copies(pieces, parts, blocks, sems)
    step = pl.program_id(0)

    @pl.when(step == 0)
    def _():
        for group in copies:
            for copy in group:
                copy.start()

    for slot, group in enumerate(copies):

        @pl.when(step == slot)
        def _(group=group):
            for copy in group:
                copy.wait()

    return blocks[step]


def project_kernel(parts, table, *refs):
    pieces = refs[: sum(parts)]
    gain, shards, normed_out, proj, dt_out, blocks, weight, sems = refs[sum(parts) :]
    block = fetch_block(pieces, parts, blocks, sems)

    @pl.when(pl.program_id(0) == 0)
    def _():
        for f in range(N_FSDP):
            weight[f * SHARD_IN : (f + 1) * SHARD_IN, :] = shards[(f // 2) % 4, f % 2, f // 8, :SHARD_IN]
        dt_out[...] = weight[:, 1024:]

    values = block.astype(F32)
    scale = lax.rsqrt(jnp.mean(values * values, axis=1, keepdims=True) + NORM_EPS)
    normed = (values * scale * gain[...]).astype(BF16)
    normed_out[...] = normed
    proj[...] = matmul(normed, weight[...])


def run_project(table, pieces, gain, shards):
    fixed = lambda shape: pl.BlockSpec(shape, lambda i, table: (0,) * len(shape))
    placed = lambda width: pl.BlockSpec((ROWS, width), lambda i, table: (table[i], 0))
    return pl.pallas_call(
        partial(project_kernel, PARTS),
        grid_spec=pltpu.PrefetchScalarGridSpec(
            num_scalar_prefetch=1,
            grid=(N_REP,),
            in_specs=[pl.BlockSpec(memory_space=pl.ANY)] * len(pieces) + [fixed((1, D)), fixed(shards.shape)],
            out_specs=[placed(D), placed(3 * WIDE), fixed((D, N))],
            scratch_shapes=[
                pltpu.VMEM((N_REP, ROWS, D), BF16),
                pltpu.VMEM((D, 3 * WIDE), BF16),
                pltpu.SemaphoreType.DMA((len(pieces),)),
            ],
        ),
        out_shape=[
            jax.ShapeDtypeStruct((PACK, D), BF16),
            jax.ShapeDtypeStruct((PACK, 3 * WIDE), F32),
            jax.ShapeDtypeStruct((D, N), BF16),
        ],
        compiler_params=pltpu.CompilerParams(
            dimension_semantics=("arbitrary",), vmem_limit_bytes=VMEM_LIMIT
        ),
        cost_estimate=COST,
        name="project",
    )(table, *pieces, gain, shards)


def row_sums(value):
    folded = value[:, :N] + value[:, N : 2 * N] + value[:, 2 * N :]
    return jnp.sum(folded.T, 0, keepdims=True)


def out_grad_kernel(table, *refs):
    pieces = refs[: sum(PARTS)]
    w_out, mixed, gate_in, gain, branch_out, grad_out, sums, blocks, turned, sems = refs[sum(PARTS) :]
    branch = fetch_block(pieces, PARTS, blocks, sems)

    @pl.when(pl.program_id(0) == 0)
    def _():
        turned[...] = w_out[...].reshape(OWN, D).T

    branch_out[...] = branch
    total = matmul(branch, turned[...])
    grad_out[...] = total
    gate = gate_in[...]
    gated = mixed[...] * (gate * jax.nn.sigmoid(gate))
    row = lax.broadcasted_iota(jnp.int32, (8, ROWS), 0)
    sums[...] = jnp.where(
        row == 0, row_sums(gated * gated), jnp.where(row == 1, row_sums(total * gain[...] * gated), 0.0)
    )


def run_out_grad(table, pieces, w_out, mixed, proj, gain):
    fixed = lambda shape: pl.BlockSpec(shape, lambda i, table: (0, 0))
    placed = lambda width: pl.BlockSpec((ROWS, width), lambda i, table: (table[i], 0))
    own = pl.BlockSpec(
        (1, 2, 1, SHARD_OUT, D), lambda i, table: (table[N_REP] % 4, 0, table[N_REP] // 4, 0, 0)
    )
    return pl.pallas_call(
        out_grad_kernel,
        grid_spec=pltpu.PrefetchScalarGridSpec(
            num_scalar_prefetch=1,
            grid=(N_REP,),
            in_specs=[pl.BlockSpec(memory_space=pl.ANY)] * len(pieces)
            + [own, placed(OWN), placed(OWN), fixed((1, OWN))],
            out_specs=[placed(D), placed(OWN), pl.BlockSpec((8, ROWS), lambda i, table: (0, table[i]))],
            scratch_shapes=[
                pltpu.VMEM((N_REP, ROWS, D), BF16),
                pltpu.VMEM((D, WIDE), BF16),
                pltpu.SemaphoreType.DMA((len(pieces),)),
            ],
        ),
        out_shape=[
            jax.ShapeDtypeStruct((PACK, D), BF16),
            jax.ShapeDtypeStruct((PACK, OWN), F32),
            jax.ShapeDtypeStruct((8, PACK), F32),
        ],
        compiler_params=pltpu.CompilerParams(
            dimension_semantics=("arbitrary",), vmem_limit_bytes=VMEM_LIMIT
        ),
        cost_estimate=COST,
        name="out_grad",
    )(table, *pieces, w_out, mixed, proj, gain)


def gate_kernel(grad_out, mixed_in, gate_in, sums, gain, low_out, grad_mixed, grad_gain):
    rows = grad_out.shape[0]
    mixed, gate, grad_o = mixed_in[...], gate_in[...], grad_out[...]
    stats = jnp.concatenate([sums[...], jnp.zeros((N - 8, rows), F32)], 0).T
    out_scale = lax.rsqrt(stats[:, 0:1] * (1.0 / DI) + NORM_EPS)
    pull = out_scale * out_scale * out_scale * (stats[:, 1:2] * (1.0 / DI))
    gate_sig = jax.nn.sigmoid(gate)
    silu = gate * gate_sig
    gated = mixed * silu
    unit = gated * out_scale
    grad_gated = out_scale * (grad_o * gain[...]) - gated * pull
    grad_mixed[...] = grad_gated * silu
    low_out[:, :OWN] = (unit * gain[...]).astype(BF16)
    low_out[:, OWN:] = (grad_gated * mixed * (gate_sig * (1.0 + gate * (1.0 - gate_sig)))).astype(BF16)
    gain_part = jnp.sum(grad_o * unit, 0, keepdims=True)

    @pl.when(pl.program_id(0) == 0)
    def _():
        grad_gain[...] = jnp.broadcast_to(gain_part, grad_gain.shape)

    @pl.when(pl.program_id(0) > 0)
    def _():
        grad_gain[...] += gain_part


def run_gate(grad_out, mixed, proj, sums, gain):
    rows = lambda width: pl.BlockSpec((ROWS, width), lambda i: (i, 0))
    fixed = lambda shape: pl.BlockSpec(shape, lambda i: (0, 0))
    return pl.pallas_call(
        gate_kernel,
        grid=(PACK // ROWS,),
        in_specs=[
            rows(OWN),
            rows(OWN),
            rows(OWN),
            pl.BlockSpec((8, ROWS), lambda i: (0, i)),
            fixed((1, OWN)),
        ],
        out_specs=[rows(2 * OWN), rows(OWN), fixed((8, OWN))],
        out_shape=[
            jax.ShapeDtypeStruct((PACK, 2 * OWN), BF16),
            jax.ShapeDtypeStruct((PACK, OWN), F32),
            jax.ShapeDtypeStruct((8, OWN), F32),
        ],
        compiler_params=pltpu.CompilerParams(
            dimension_semantics=("arbitrary",), vmem_limit_bytes=VMEM_LIMIT
        ),
        cost_estimate=COST,
        name="gate_backward",
    )(grad_out, mixed, proj, sums, gain)


def early_grad_kernel(low, grad_branch, normed, out):
    step = pl.program_id(0)

    @pl.when(step == 0)
    def _():
        out[...] = jnp.zeros_like(out)

    for k in range(4):
        part = product(low[:, :OWN], grad_branch[:, k * WIDE : (k + 1) * WIDE], 0, 0)
        for m in range(4):
            out[eight_order(4 * k + m), :SHARD_IN] += part[m * SHARD_IN : (m + 1) * SHARD_IN]
    part = product(normed[...], low[:, OWN:], 0, 0)
    for f in range(N_FSDP):
        out[eight_order(f), SHARD_IN:] += part[f * SHARD_IN : (f + 1) * SHARD_IN]


def run_early_grad(low, grad_branch, normed):
    count = 2 * ROWS
    rows = lambda width: pl.BlockSpec((count, width), lambda i: (i, 0))
    shape = (N_FSDP, 2 * SHARD_IN, WIDE)
    return pl.pallas_call(
        early_grad_kernel,
        grid=(PACK // count,),
        in_specs=[rows(2 * OWN), rows(D), rows(D)],
        out_specs=pl.BlockSpec(shape, lambda i: (0, 0, 0)),
        out_shape=jax.ShapeDtypeStruct(shape, F32),
        compiler_params=pltpu.CompilerParams(
            dimension_semantics=("arbitrary",), vmem_limit_bytes=VMEM_LIMIT
        ),
        cost_estimate=COST,
        name="early_grad",
    )(low, grad_branch, normed)


def block_out_kernel(rows, weight, tokens, live, out):
    step = pl.program_id(0)
    part = matmul(jnp.concatenate([rows[0], rows[1]], 1), weight[...].reshape(2 * OWN, D))

    @pl.when(step == 0)
    def _():
        out[...] = part

    @pl.when(step > 0)
    def _():
        out[...] += part

    @pl.when(step == N_REP // 2 - 1)
    def _():
        out[...] = tokens[...].astype(F32) + live[...] * out[...]


def run_block_out(rows, weight, tokens, live):
    fixed = lambda shape: pl.BlockSpec(shape, lambda i: (0, 0))
    return pl.pallas_call(
        block_out_kernel,
        grid=(N_REP // 2,),
        in_specs=[
            pl.BlockSpec((2, ROWS, OWN), lambda i: (i, 0, 0)),
            pl.BlockSpec((2, 2, 1, SHARD_OUT, D), lambda i: (i % 2, 0, i // 2, 0, 0)),
            fixed((ROWS, D)),
            fixed((ROWS, 1)),
        ],
        out_specs=fixed((ROWS, D)),
        out_shape=jax.ShapeDtypeStruct((ROWS, D), F32),
        compiler_params=pltpu.CompilerParams(
            dimension_semantics=("arbitrary",), vmem_limit_bytes=VMEM_LIMIT
        ),
        cost_estimate=FILL,
        name="block_out",
    )(rows, weight, tokens, live)


def turned_part(weight, rows):
    return product(weight[...].reshape(D, weight.shape[-1]), rows, 1, 1)


def columns_of(full_in, width, index):
    return pl.BlockSpec(full_in.shape[:-1] + (width,), lambda i: (0, 0, 0, 0, index(i)))


def z_grad_kernel(rows, weight, out):
    part = turned_part(weight, jnp.concatenate([rows[0], rows[1]], 1))

    @pl.when(pl.program_id(0) == 0)
    def _():
        out[...] = part

    @pl.when(pl.program_id(0) > 0)
    def _():
        out[...] += part


def run_z_grad(rows, full_in):
    return pl.pallas_call(
        z_grad_kernel,
        grid=(N_REP // 2,),
        in_specs=[
            pl.BlockSpec((2, ROWS, OWN), lambda i: (i, 0, 1)),
            columns_of(full_in, 2 * OWN, lambda i: i),
        ],
        out_specs=pl.BlockSpec((D, ROWS), lambda i: (0, 0)),
        out_shape=jax.ShapeDtypeStruct((D, ROWS), F32),
        compiler_params=pltpu.CompilerParams(
            dimension_semantics=("arbitrary",), vmem_limit_bytes=VMEM_LIMIT
        ),
        cost_estimate=FILL,
        name="z_grad",
    )(rows, full_in)


def input_grad_kernel(
    grad_z, x_rows, rest_rows, w_x, w_bc, low_dt, tokens, cotangent, gain, out, gain_out, total, ordered
):
    step = pl.program_id(0)
    part = turned_part(w_x, jnp.concatenate([x_rows[0], x_rows[1]], 1))

    @pl.when(step == 0)
    def _():
        total[...] = grad_z[...] + part

    @pl.when(step > 0)
    def _():
        total[...] += part

    @pl.when(step == N_REP // 2 - 1)
    def _():
        lane = lax.broadcasted_iota(jnp.int32, (ROWS, N), 1)
        groups = []
        for k in range(2):
            group = jnp.zeros((ROWS, N), F32)
            for m in range(4):
                value = rest_rows[4 * k + m].astype(F32)
                value = value if m == 0 else pltpu.roll(value, m * OWN_BC, 1)
                group = jnp.where((lane >= m * OWN_BC) & (lane < (m + 1) * OWN_BC), value, group)
            groups.append(group.astype(BF16))
        steps = jnp.zeros((ROWS, N), F32)
        for m in range(N_REP):
            start = 8 + m * OWN_H
            value = pltpu.roll(rest_rows[m].astype(F32), (start - OWN_BC) % N, 1)
            steps = jnp.where((lane >= start) & (lane < start + OWN_H), value, steps)
        shared = total[...] + turned_part(w_bc, jnp.concatenate(groups, 1))
        for f in range(N_FSDP):
            start = eight_order(f) * SHARD_IN
            ordered[f * SHARD_IN : (f + 1) * SHARD_IN, :] = shared[start : start + SHARD_IN, :]
        grad_h = (ordered[...] + product(low_dt[...], steps.astype(BF16), 1, 1)).T
        values = tokens[...].astype(F32)
        scale = lax.rsqrt(jnp.mean(values * values, axis=1, keepdims=True) + NORM_EPS)
        unit = values * scale
        gain_sum = jnp.sum(grad_h * unit, 0, keepdims=True)
        gain_out[...] = jnp.zeros_like(gain_out)
        for k in range(D // TAIL):
            gain_out[k : k + 1, :] = gain_sum[:, k * TAIL : (k + 1) * TAIL]
        grad_unit = grad_h * gain[...]
        inner = jnp.mean(grad_unit * unit, axis=1, keepdims=True)
        out[...] = cotangent[...].astype(F32) + scale * (grad_unit - unit * inner)


def run_input_grad(grad_z, tail_rows, full_in, low_dt, tokens, cotangent, gain):
    fixed = lambda shape: pl.BlockSpec(shape, lambda i: (0,) * len(shape))
    return pl.pallas_call(
        input_grad_kernel,
        grid=(N_REP // 2,),
        in_specs=[
            fixed((D, ROWS)),
            pl.BlockSpec((2, ROWS, OWN), lambda i: (i, 0, 0)),
            pl.BlockSpec((N_REP, ROWS, N), lambda i: (0, 0, OWN // N)),
            columns_of(full_in, 2 * OWN, lambda i: N_REP // 2 + i),
            columns_of(full_in, 2 * N, lambda i: DI // N),
            fixed((D, N)),
            fixed((ROWS, D)),
            fixed((ROWS, D)),
            fixed((1, D)),
        ],
        out_specs=[fixed((ROWS, D)), fixed((8, TAIL))],
        out_shape=[jax.ShapeDtypeStruct((ROWS, D), F32), jax.ShapeDtypeStruct((8, TAIL), F32)],
        scratch_shapes=[pltpu.VMEM((D, ROWS), F32), pltpu.VMEM((D, ROWS), F32)],
        compiler_params=pltpu.CompilerParams(
            dimension_semantics=("arbitrary",), vmem_limit_bytes=VMEM_LIMIT
        ),
        cost_estimate=COST,
        name="input_grad",
    )(grad_z, tail_rows, tail_rows, full_in, full_in, low_dt, tokens, cotangent, gain)


def rest_kernel(
    ends, parts, pre_b, pre_c, conv_in, par, grad_x, grad_dt, sums, head_acc, grad_gain, first, tail_out, small_out
):
    own = lax.broadcasted_iota(jnp.int32, (OWN_BC, 2 * N), 0) + first[0]
    chosen = (lax.broadcasted_iota(jnp.int32, (OWN_BC, 2 * N), 1) == own).astype(F32).astype(BF16)

    def pick(value):
        return product(jnp.concatenate([chosen] * 3, 1), jnp.concatenate(split_three(value), 1), 1, 1)

    grad = parts[0].astype(F32)
    for k in range(1, N_REP):
        grad = grad + parts[k].astype(F32)
    own_pre = pick(jnp.concatenate([pre_b[...], pre_c[...]], 1))
    own_conv = product(chosen, conv_in[...].astype(BF16), 1, 1)
    taps = pick(par[:, OWN:])
    sig = jax.nn.sigmoid(own_pre)
    grad_pre = grad * (sig * (1.0 + own_pre * (1.0 - sig)))
    position = lax.broadcasted_iota(jnp.int32, (1, PACK), 1)

    def segment(places):
        counted = jnp.zeros_like(places)
        for k in range(3):
            counted = counted + (places >= ends[k]).astype(jnp.int32)
        return counted

    grad_conv = taps[:, CONV - 1 : CONV] * grad_pre
    column = lax.broadcasted_iota(jnp.int32, (OWN_BC, N), 1)
    found = jnp.where(column == CONV, jnp.sum(grad_pre, 1, keepdims=True), 0.0)
    found = jnp.where(column == CONV - 1, jnp.sum(own_conv * grad_pre, 1, keepdims=True), found)
    for later_by in range(1, CONV):
        same = (segment(position + later_by) == segment(position)) & (position < PACK - later_by)
        later = jnp.where(same, pltpu.roll(grad_pre, PACK - later_by, 1), 0.0)
        tap = CONV - 1 - later_by
        found = jnp.where(column == tap, jnp.sum(own_conv * later, 1, keepdims=True), found)
        grad_conv = grad_conv + taps[:, tap : tap + 1] * later
    lane = lax.broadcasted_iota(jnp.int32, (N, N), 1)
    filler = jnp.zeros((N - OWN_BC, N), F32)
    for k in range(PACK // N):
        rows = slice(k * N, (k + 1) * N)
        columns = jnp.concatenate([grad_conv[:, rows], filler], 0).T
        steps = pltpu.roll(grad_dt[rows, :].astype(F32), OWN_BC, 1)
        tail_out[rows, :OWN] = grad_x[rows, :]
        tail_out[rows, OWN:] = jnp.where(
            lane < OWN_BC, columns, jnp.where(lane < OWN_BC + OWN_H, steps, 0.0)
        ).astype(BF16)
    row = lax.broadcasted_iota(jnp.int32, (8, OWN), 0)
    skip = head_sums(sums[...])
    by_head = jnp.concatenate([skip, jnp.zeros((8, OWN - N), F32)], 1)
    logs = jnp.concatenate([head_acc[...], jnp.zeros((8, OWN - N), F32)], 1)
    wide = jnp.where(row == 0, grad_gain[0:1, :], jnp.where(row < 6, sums[...], 0.0))
    wide = jnp.where(row == 6, logs[1:2, :], jnp.where(row == 7, by_head[6:7, :], wide))
    turned = jnp.concatenate([found, filler], 0).T
    first_row = lax.broadcasted_iota(jnp.int32, (8, N), 0) == 0
    small_out[:, :OWN] = wide
    small_out[:, OWN:] = jnp.where(first_row, head_acc[0:1, :], pltpu.roll(turned[:8], 1, 0))


def run_rest(ends, parts, pre, proj, par, grad_x, grad_dt, sums, head_acc, grad_gain, first):
    fixed = lambda shape: pl.BlockSpec(shape, lambda i: (0,) * len(shape))
    return pl.pallas_call(
        rest_kernel,
        grid=(1,),
        in_specs=[
            pl.BlockSpec(memory_space=pltpu.SMEM),
            fixed((N_REP, OWN_BC, PACK)),
            pl.BlockSpec((PACK, N), lambda i: (0, 3)),
            pl.BlockSpec((PACK, N), lambda i: (0, 4)),
            pl.BlockSpec((PACK, 2 * N), lambda i: (0, 3)),
            fixed((16, 640)),
            fixed((PACK, OWN)),
            fixed((PACK, N)),
            fixed((8, OWN)),
            fixed((8, N)),
            fixed((8, OWN)),
            pl.BlockSpec(memory_space=pltpu.SMEM),
        ],
        out_specs=[fixed((PACK, TAIL)), fixed((8, TAIL))],
        out_shape=[jax.ShapeDtypeStruct((PACK, TAIL), BF16), jax.ShapeDtypeStruct((8, TAIL), F32)],
        compiler_params=pltpu.CompilerParams(
            dimension_semantics=("arbitrary",), vmem_limit_bytes=VMEM_LIMIT
        ),
        cost_estimate=COST,
        name="rest_backward",
    )(ends, parts, pre, pre, proj, par, grad_x, grad_dt, sums, head_acc, grad_gain, first)


def tail_grad_kernel(normed, tail, small, out):
    step = pl.program_id(0)
    part = product(normed[...], tail[...], 0, 0)
    for f in range(N_FSDP):
        rows = part[f * SHARD_IN : (f + 1) * SHARD_IN]

        @pl.when(step == 0)
        def _(f=f, rows=rows):
            out[eight_order(f), :SHARD_IN] = rows
            out[eight_order(f), SHARD_IN:] = small[...]

        @pl.when(step > 0)
        def _(f=f, rows=rows):
            out[eight_order(f), :SHARD_IN] += rows


def run_tail_grad(normed, tail, small):
    count = 2 * ROWS
    shape = (N_FSDP, SHARD_IN + 8, TAIL)
    return pl.pallas_call(
        tail_grad_kernel,
        grid=(PACK // count,),
        in_specs=[
            pl.BlockSpec((count, D), lambda i: (i, 0)),
            pl.BlockSpec((count, TAIL), lambda i: (i, 0)),
            pl.BlockSpec((8, TAIL), lambda i: (0, 0)),
        ],
        out_specs=pl.BlockSpec(shape, lambda i: (0, 0, 0)),
        out_shape=jax.ShapeDtypeStruct(shape, F32),
        compiler_params=pltpu.CompilerParams(
            dimension_semantics=("arbitrary",), vmem_limit_bytes=VMEM_LIMIT
        ),
        cost_estimate=COST,
        name="tail_grad",
    )(normed, tail, small)


def adam_step(grad, weight, first, second, grad_out, first_out, second_out, weight_out):
    new_weight, new_first, new_second = adam_update(
        weight[...], grad, first[...], second[...], RATE_MATRIX, WEIGHT_DECAY
    )
    grad_out[...] = grad
    first_out[...] = new_first
    second_out[...] = new_second
    weight_out[...] = new_weight


def adam_early_kernel(rows, pair, *refs):
    arrays, grad = refs[:-1], refs[-1]
    grad[:, :WIDE] = pair[0, rows, :]
    grad[:, WIDE:] = pair[1, rows, :]
    adam_step(grad[...], *arrays)


def run_adam_early(place_of, rows, parts, weight, first, second):
    part = pl.BlockSpec((SHARD_IN, 2 * WIDE), place_of)
    shape = jax.ShapeDtypeStruct(weight.shape, F32)
    return pl.pallas_call(
        partial(adam_early_kernel, rows),
        grid=(N_REP // 2,),
        in_specs=[pl.BlockSpec((2,) + parts.shape[1:], lambda i: (i, 0, 0))] + [part] * 3,
        out_specs=[part] * 4,
        out_shape=[shape] * 4,
        scratch_shapes=[pltpu.VMEM((SHARD_IN, 2 * WIDE), F32)],
        compiler_params=pltpu.CompilerParams(
            dimension_semantics=("arbitrary",), vmem_limit_bytes=VMEM_LIMIT
        ),
        cost_estimate=FILL,
        name="adam",
    )(parts, weight, first, second)


def adam_tail_kernel(pair, rest, *refs):
    arrays, grad = refs[:3] + refs[-5:-1], refs[-1]
    step = pl.program_id(0)

    @pl.when(step < N_REP // 2)
    def _():
        grad[:, :WIDE] = pair[0, :SHARD_IN]
        grad[:, WIDE:] = pair[1, :SHARD_IN]

    @pl.when(step == N_REP // 2)
    def _():
        lane = lax.broadcasted_iota(jnp.int32, (SHARD_IN, N), 1)
        for k in range(2):
            group = jnp.zeros((SHARD_IN, N), F32)
            for m in range(4):
                value = rest[4 * k + m, :SHARD_IN]
                value = value if m == 0 else pltpu.roll(value, m * OWN_BC, 1)
                group = jnp.where((lane >= m * OWN_BC) & (lane < (m + 1) * OWN_BC), value, group)
            grad[:, k * N : (k + 1) * N] = group

    adam_step(grad[...], *arrays)


def run_adam_tail(parts, weight, first, second, before):
    half = N_REP // 2
    rows = parts.shape[1]
    column = pl.BlockSpec((SHARD_IN, 2 * WIDE), lambda i: (0, half + i))
    shape = jax.ShapeDtypeStruct(weight.shape, F32)
    return pl.pallas_call(
        adam_tail_kernel,
        grid=(half + 1,),
        in_specs=[
            pl.BlockSpec((2, rows, OWN), lambda i: (jnp.minimum(i, half - 1), 0, 0)),
            pl.BlockSpec((N_REP, rows, N), lambda i: (0, 0, OWN // N)),
        ]
        + [column] * 3
        + [pl.BlockSpec(memory_space=pl.ANY)] * 4,
        out_specs=[column] * 4,
        out_shape=[shape] * 4,
        input_output_aliases={5 + k: k for k in range(4)},
        scratch_shapes=[pltpu.VMEM((SHARD_IN, 2 * WIDE), F32)],
        compiler_params=pltpu.CompilerParams(
            dimension_semantics=("arbitrary",), vmem_limit_bytes=VMEM_LIMIT
        ),
        cost_estimate=COST,
        name="adam_tail",
    )(parts, parts, weight, first, second, *before)


def body(
    tokens,
    cotangent,
    lengths,
    w_in,
    w_dt,
    w_out,
    small,
    first_in,
    first_dt,
    first_out,
    first_small,
    second_in,
    second_dt,
    second_out,
    second_small,
):
    place = Place()
    r = place.r
    zero = jnp.int32(0)
    pack_lengths = lax.dynamic_slice_in_dim(lengths, place.f, 1, 0)[0]
    seg_ends = jnp.cumsum(pack_lengths)
    own_positions = r * ROWS + jnp.arange(ROWS, dtype=jnp.int32)
    own_live = (segment_at(own_positions, seg_ends) < 3).astype(F32)[:, None]
    slots = jnp.arange(N_REP, dtype=jnp.int32)
    ahead = ((place.x + slots // 2) % 4) * 2 + (place.yl + slots) % 2
    half = ROWS // 2

    in_low = w_in.astype(BF16)
    dt_low = w_dt.astype(BF16)
    out_low = w_out.astype(BF16)

    small_rows = jnp.pad(small.astype(BF16), (0, 16 * 3 * WIDE - SHARD_SMALL)).reshape(16, 3 * WIDE)

    def own_columns(rep):
        columns = jnp.concatenate(
            [
                lax.dynamic_slice_in_dim(in_low, rep * OWN, OWN, 1),
                lax.dynamic_slice_in_dim(in_low, DI + rep * OWN, OWN, 1),
                in_low[:, 2 * DI :],
                lax.dynamic_slice_in_dim(dt_low, rep * OWN_H, OWN_H, 1),
                jnp.zeros((SHARD_IN, 2), BF16),
                dt_low,
                jnp.zeros((SHARD_IN, N - 8 - H), BF16),
            ],
            1,
        )
        return jnp.concatenate([columns, small_rows], 0)

    other_columns = move(
        own_columns(2 * place.x + 1 - place.yl), lambda yh, z, c, x, yl: (yh + 1, z, c, x, yl + 1)
    )
    from_left = move(tokens, along_x(1))
    from_right = move(tokens, along_x(-1))
    partner = move(tokens, swap_y)

    out_low, other_columns = lax.optimization_barrier((out_low, other_columns))
    out_other = move(out_low, lambda yh, z, c, x, yl: (yh + 1, z, c, x, yl + 1))
    from_left, from_right, partner, other_columns = lax.optimization_barrier(
        (from_left, from_right, partner, other_columns)
    )
    own_shards = gather_eight(both(own_columns(r), other_columns, place.yh))
    far = move(from_left, along_x(1))
    partner_left = move(from_left, swap_y)
    partner_right = move(partner, along_x(-1))

    branch = (cotangent.astype(F32) * own_live).astype(BF16)
    far, partner_left, partner_right, out_other, branch = lax.optimization_barrier(
        (far, partner_left, partner_right, out_other, branch)
    )
    out_pair = both(out_low, out_other, place.yh)
    partner_far_top = move(partner_left[:half], along_x(1))
    partner_far_low = move(partner_right[half:], along_x(-1))

    vector = own_shards[:, :, :, SHARD_IN : SHARD_IN + 2].transpose(2, 0, 1, 3, 4)
    vector = vector.reshape(N_FSDP, 6 * WIDE)[:, :SHARD_SMALL].reshape(-1).astype(F32)
    offset = 0
    gain_in = vector[None, :D]
    offset = D
    gain_row = lax.dynamic_slice_in_dim(vector, offset + r * OWN, OWN, 0)[None, :]
    offset += DI
    taps = vector[offset : offset + (CONV + 1) * CHANNELS].reshape(CONV + 1, CHANNELS)
    offset += (CONV + 1) * CHANNELS
    per_head = vector[offset:].reshape(3, H)
    dt_bias, a_log, d_skip = lax.dynamic_slice_in_dim(per_head, r * OWN_H, OWN_H, 1)
    taps_bc = taps[:, DI:]
    conv_par = jnp.concatenate([lax.dynamic_slice_in_dim(taps, r * OWN, OWN, 1), taps_bc], 1)
    head_par = jnp.stack(
        [
            jnp.pad(jnp.broadcast_to(d_skip[:, None], (OWN_H, P_SIZE)).reshape(-1), (0, 2 * N)),
            jnp.pad(dt_bias, (0, 640 - OWN_H)),
            jnp.pad(-jnp.exp(a_log), (0, 640 - OWN_H)),
        ],
        0,
    )
    par = jnp.concatenate([conv_par, head_par, jnp.zeros((8, 640), F32)], 0)

    in_low, partner_far_top, partner_far_low, own_shards = lax.optimization_barrier(
        (in_low, partner_far_top, partner_far_low, own_shards)
    )
    full_out = gather_eight(tie(out_pair, own_shards))
    in_other = move(in_low, lambda yh, z, c, x, yl: (yh + 1, z, c, x, yl + 1))
    b_left = move(branch, along_x(1))
    b_right = move(branch, along_x(-1))
    b_partner = move(branch, swap_y)
    token_pieces = [
        tokens, partner, from_right, partner_right, far,
        partner_far_top, partner_far_low, from_left, partner_left,
    ]
    normed, proj, low_dt = run_project(ahead, token_pieces, gain_in, own_shards)
    b_left, b_right, b_partner, proj = lax.optimization_barrier((b_left, b_right, b_partner, proj))
    b_far = move(b_left, along_x(1))
    b_partner_left = move(b_left, swap_y)
    b_partner_right = move(b_partner, along_x(-1))
    before = run_forward(0, seg_ends, proj, par)
    b_far, b_partner_left, b_partner_right, before = lax.optimization_barrier(
        (b_far, b_partner_left, b_partner_right, before)
    )
    b_partner_far_top = move(b_partner_left[:half], along_x(1))
    b_partner_far_low = move(b_partner_right[half:], along_x(-1))
    pre, mixed, states, _ = run_forward(1, seg_ends, proj, par, before)
    mixed, in_low, in_other, b_partner_far_top, b_partner_far_low = lax.optimization_barrier(
        (mixed, in_low, in_other, b_partner_far_top, b_partner_far_low)
    )
    full_in = gather_eight(both(in_low, in_other, place.yh))
    branch_pieces = [
        branch, b_partner, b_right, b_partner_right, b_far,
        b_partner_far_top, b_partner_far_low, b_left, b_partner_left,
    ]
    rep_table = jnp.concatenate([ahead, r[None]])
    grad_branch, grad_normed_out, sums = run_out_grad(rep_table, branch_pieces, full_out, mixed, proj, gain_row)
    sums = share_rep(sums[:2].reshape(32, 128)).sum(0).reshape(2, PACK)
    sums = jnp.concatenate([sums, jnp.zeros((6, PACK), F32)], 0)

    low, grad_mixed, grad_gain = run_gate(grad_normed_out, mixed, proj, sums, gain_row)

    low_rows = exchange(low.reshape(N_REP, ROWS, 2 * OWN), "rep")
    grad_x, grad_dtraw, grad_bc, grad_sums, grad_heads = run_backward(
        seg_ends, proj, pre, mixed, grad_mixed, states, par
    )
    low, grad_x = lax.optimization_barrier((low, grad_x))
    early_grad = run_early_grad(low, grad_branch, normed)
    low_rows, early_grad, grad_bc, grad_x = lax.optimization_barrier((low_rows, early_grad, grad_bc, grad_x))

    grad_bc = exchange(grad_bc, "rep").reshape(N_REP, OWN_BC, PACK)
    early = scatter_eight(early_grad)
    grad_rows = run_z_grad(low_rows, full_in)
    grad_bc, grad_rows = lax.optimization_barrier((grad_bc, grad_rows))

    tail, small_own = run_rest(
        seg_ends, grad_bc, pre, proj, par, grad_x, grad_dtraw, grad_sums, grad_heads, grad_gain, (r * OWN_BC)[None]
    )
    grad_tail = run_tail_grad(normed, tail, small_own)
    tail, grad_tail, low_rows = lax.optimization_barrier((tail, grad_tail, low_rows))
    tail_rows = exchange(tail.reshape(N_REP, ROWS, TAIL), "rep")
    tail_part = scatter_eight(grad_tail)
    block_out = run_block_out(low_rows, full_out, tokens, own_live)
    early, block_out = lax.optimization_barrier((early, block_out))
    mine, other = at(early, place.yh), at(early, 1 - place.yh)
    out_mine = move(
        mine[:SHARD_IN], lambda yh, z, c, x, yl: (x // 2, (x % 2) * 2 + yl, z % 2, 2 * c + yh, z // 2)
    )
    out_other = move(
        other[:SHARD_IN], lambda yh, z, c, x, yl: (x // 2, (x % 2) * 2 + yl, z % 2, 2 * c + 1 - yh, z // 2)
    )
    z_other = move(other[SHARD_IN:], swap_y_hi)
    tail_rows, out_mine, out_other, z_other = lax.optimization_barrier((tail_rows, out_mine, out_other, z_other))

    early_parts = share_rep(jnp.concatenate([out_mine + out_other, mine[SHARD_IN:] + z_other], 0))
    input_grad, grad_gain_in = run_input_grad(
        grad_rows, tail_rows, full_in, low_dt, tokens, cotangent, gain_in
    )

    grad_gain_in = sum_z(grad_gain_in + move(grad_gain_in, swap_core))
    tail_part, grad_gain_in = lax.optimization_barrier((tail_part, grad_gain_in))
    gain_rows = grad_gain_in.shape[0]
    tail_other = move(with_rows(at(tail_part, 1 - place.yh), grad_gain_in), swap_y_hi)
    tail_part = with_rows(at(tail_part, place.yh), grad_gain_in) + tail_other

    tail_part, early_parts = lax.optimization_barrier((tail_part, early_parts))
    tail_parts = share_rep(tail_part)

    grad_out, new_first_out, new_second_out, new_out = run_adam_early(
        lambda i: (i // 2, i % 2), slice(0, SHARD_IN), early_parts, w_out, first_out, second_out
    )
    updated = run_adam_early(
        lambda i: (0, i), slice(SHARD_IN, 2 * SHARD_IN), early_parts, w_in, first_in, second_in
    )
    grad_in, new_first_in, new_second_in, new_in = run_adam_tail(tail_parts, w_in, first_in, second_in, updated)

    def columns(parts):
        return parts.transpose(1, 0, 2).reshape(parts.shape[1], -1)

    grad_gain_in = tail_parts[:, -gain_rows : D // TAIL - gain_rows].sum(0).reshape(-1)
    small_parts = tail_parts[:, SHARD_IN:-gain_rows]
    small_x = small_parts[:, :, :OWN].transpose(1, 0, 2).reshape(8, DI)
    small_bc = small_parts[:, :, OWN:].transpose(1, 0, 2)

    def channels(row):
        return jnp.concatenate([small_x[row], small_bc[row, :, :OWN_BC].reshape(-1)])

    grad_small_all = jnp.concatenate(
        [grad_gain_in, small_x[0]]
        + [channels(row) for row in range(1, 6)]
        + [
            small_bc[0, :, :OWN_H].reshape(-1),
            small_parts[:, 6, :OWN_H].reshape(-1),
            small_parts[:, 7, :OWN_H].reshape(-1),
        ]
    )
    grad_small = lax.dynamic_slice_in_dim(grad_small_all, place.f * SHARD_SMALL, SHARD_SMALL, 0)
    grad_dt = columns(tail_parts[:, :SHARD_IN, OWN + OWN_BC : OWN + OWN_BC + OWN_H])
    new_dt, new_first_dt, new_second_dt = adam_update(
        w_dt, grad_dt, first_dt, second_dt, RATE_MATRIX, WEIGHT_DECAY
    )
    new_small, new_first_small, new_second_small = adam_update(
        small, grad_small, first_small, second_small, RATE_SMALL, 0.0
    )
    return (
        block_out,
        input_grad,
        grad_in,
        grad_dt,
        grad_out,
        grad_small,
        new_first_in,
        new_first_dt,
        new_first_out,
        new_first_small,
        new_second_in,
        new_second_dt,
        new_second_out,
        new_second_small,
        new_in,
        new_dt,
        new_out,
        new_small,
    )


def solution(mesh):
    rows = P(("fsdp", "rep"), None)
    matrix = P("fsdp", None)
    vector = P("fsdp")
    group = (matrix, matrix, matrix, vector)
    return jax.shard_map(
        body,
        mesh=mesh,
        in_specs=(rows, rows, P()) + group * 3,
        out_specs=(rows, rows) + group * 4,
        check_vma=False,
    )
```

profile of v0, /device:TPU:0, one launch (start us, length us, event | category | flops | bytes accessed | tf_op | source)
XLA Modules:
  0.0 384.4 jit_solution(2323042524344127474)
XLA Ops:
  19.7 4.9 %collective-permute-done.3 = bf16[112,1152]{1,0:T(8,128)(2,1)} collective-permute-done((bf16[112,1152]{1,0:T(8,128)(2,1)}, bf16[112,1152]{1,0:T(8,128)(2,1)}, u32[]{:S(2)}, u32[]{:S(2)}) %collective-permute-start.3) | collective-permute-done | bytes 258080 | tf_op jit(solution)/shard_map/ppermute | solution.py:56
  39.4 11.6 %collective-permute-done.7 = bf16[192,1536]{1,0:T(8,128)(2,1)S(1)} collective-permute-done((bf16[192,1536]{1,0:T(8,128)(2,1)S(1)}, bf16[192,1536]{1,0:T(8,128)(2,1)S(1)}, u32[]{:S(2)}, u32[]{:S(2)}) %collective-permute-start.7) | collective-permute-done | bytes 589856 | tf_op jit(solution)/shard_map/ppermute | solution.py:56
  58.4 4.6 %collective-permute-done.11.refs_5_ = bf16[128,1536]{1,0:T(8,128)(2,1)} collective-permute-done((bf16[128,1536]{1,0:T(8,128)(2,1)}, bf16[128,1536]{1,0:T(8,128)(2,1)}, u32[]{:S(2)}, u32[]{:S(2)}) %collective-permute-start.11) | collective-permute-done | bytes 393248 | tf_op jit(solution)/shard_map/ppermute | solution.py:56
  74.2 17.4 %project.1 = (bf16[2048,1536]{1,0:T(8,128)(2,1)}, f32[2048,1152]{1,0:T(8,128)}, bf16[1536,128]{1,0:T(8,128)(2,1)}) custom-call(s32[8]{0:T(128)} %fusion.6.table, bf16[256,1536]{1,0:T(8,128)(2,1)} %tokens.3, bf16[256,1536]{1,0:T(8,128)(2,1)} %collective-permute-done.2.refs_1_, bf16[256,1536]{1,0:T(8,128)(2,1)} %collective-permute-done.1.refs_2_, ...), custom_call_target="tpu_custom_call" | custom-call | flops 1000000 | bytes 100000 | tf_op jit(solution)/shard_map/project/pallas_call | solution.py:584
  97.1 12.1 %scan_forward.2 = (f32[2048,640]{1,0:T(8,128)}, f32[2048,384]{1,0:T(8,128)}, f32[2048,384]{1,0:T(8,128)}, f32[136,640]{1,0:T(8,128)}) custom-call(s32[3]{0:T(128)} %bitcast.91, f32[2048,1152]{1,0:T(8,128)} %get-tuple-element.125.proj.refs_11_.gate_in.conv_in.dt_in, f32[16,640]{1,0:T(8,128)} %concatenate.42.par), custom_call_target="tpu_custom_call" | custom-call | flops 1000000 | bytes 100000 | tf_op jit(solution)/shard_map/scan_forward/pallas_call | solution.py:355
  116.5 12.2 %scan_forward.3 = (f32[2048,640]{1,0:T(8,128)}, f32[2048,384]{1,0:T(8,128)}, f32[2048,384]{1,0:T(8,128)}, f32[136,640]{1,0:T(8,128)}) custom-call(s32[3]{0:T(128)} %bitcast.92, f32[2048,1152]{1,0:T(8,128)} %get-tuple-element.125.proj.refs_11_.gate_in.conv_in.dt_in, ...), custom_call_target="tpu_custom_call", output_to_operand_aliasing={{0}: (3, {}), {1}: (4, {}), {2}: (5, {})} | custom-call | flops 1000000 | bytes 100000 | tf_op jit(solution)/shard_map/scan_forward/pallas_call | solution.py:355
  134.0 13.6 %out_grad.1 = (bf16[2048,1536]{1,0:T(8,128)(2,1)}, f32[2048,384]{1,0:T(8,128)}, f32[8,2048]{1,0:T(8,128)}) custom-call(s32[9]{0:T(128)} %pad_add_fusion.table, bf16[256,1536]{1,0:T(8,128)(2,1)} %copy-done.6, bf16[256,1536]{1,0:T(8,128)(2,1)} %collective-permute-done.10.refs_1_, bf16[256,1536]{1,0:T(8,128)(2,1)} %copy-done.12, bf16[256,1536]{1,0:T(8,128)(2,1)} %copy-done.9, ...), custom_call_target="tpu_custom_call" | custom-call | flops 1000000 | bytes 100000 | tf_op jit(solution)/shard_map/out_grad/pallas_call | solution.py:641
  148.5 10.2 %all_to_all.34 = f32[8,32,128]{2,1,0:T(8,128)S(1)} all-to-all(f32[8,32,128]{2,1,0:T(8,128)S(1)} %broadcast_in_dim.59), channel_id=1, replica_groups=mesh['fsdp'=16,'rep'=8] {'rep'}, dimensions={0} | all-to-all | bytes 262144 | tf_op jit(solution)/shard_map/all_to_all | solution.py:120
  159.4 10.5 %gate_backward.1 = (bf16[2048,768]{1,0:T(8,128)(2,1)}, f32[2048,384]{1,0:T(8,128)}, f32[8,384]{1,0:T(8,128)}) custom-call(f32[2048,384]{1,0:T(8,128)} %get-tuple-element.144.grad_out, f32[2048,384]{1,0:T(8,128)} %get-tuple-element.143.refs_10_.mixed_in, f32[2048,1152]{1,0:T(8,128)} %get-tuple-element.125.proj.refs_11_.gate_in.conv_in.dt_in, ...), custom_call_target="tpu_custom_call" | custom-call | flops 1000000 | bytes 100000 | tf_op jit(solution)/shard_map/gate_backward/pallas_call | solution.py:696
  173.6 32.3 %scan_backward.1 = (bf16[2048,384]{1,0:T(8,128)(2,1)}, bf16[2048,128]{1,0:T(8,128)(2,1)}, bf16[256,2048]{1,0:T(8,128)(2,1)}, f32[8,384]{1,0:T(8,128)}, f32[8,128]{1,0:T(8,128)}) custom-call(s32[3]{0:T(128)} %bitcast.93, f32[2048,1152]{1,0:T(8,128)} %get-tuple-element.125.proj.refs_11_.gate_in.conv_in.dt_in, ...), custom_call_target="tpu_custom_call" | custom-call | flops 1000000 | bytes 100000 | tf_op jit(solution)/shard_map/scan_backward/pallas_call | solution.py:483
  206.0 12.6 %early_grad.1 = f32[16,192,384]{2,1,0:T(8,128)} custom-call(bf16[2048,768]{1,0:T(8,128)(2,1)} %get-tuple-element.151.low, bf16[2048,1536]{1,0:T(8,128)(2,1)} %get-tuple-element.152.grad_branch, bf16[2048,1536]{1,0:T(8,128)(2,1)} %get-tuple-element.153.normed), custom_call_target="tpu_custom_call" | custom-call | flops 1000000 | bytes 100000 | tf_op jit(solution)/shard_map/early_grad/pallas_call | solution.py:740
  220.2 5.4 %all-to-all-start.2 = ((bf16[8,32,2048]{2,1,0:T(8,128)(2,1)}), bf16[8,32,2048]{2,1,0:T(8,128)(2,1)S(1)}, u32[]{:S(2)}, u32[]{:S(2)}) async-start(bf16[8,32,2048]{2,1,0:T(8,128)(2,1)} %bitcast.78), calls=%async_computation.3 | async-start | bytes 2097152 | tf_op jit(solution)/shard_map/all_to_all | solution.py:120
  227.1 7.8 %z_grad.1.grad_z = f32[1536,256]{1,0:T(8,128)} custom-call(bf16[8,256,768]{2,1,0:T(8,128)(2,1)} %copy-done.2, bf16[4,2,2,96,6400]{4,3,2,1,0:T(8,128)(2,1)} %bitcast.67), custom_call_target="tpu_custom_call" | custom-call | flops 2400000000 | bytes 20000000 | tf_op jit(solution)/shard_map/z_grad/pallas_call | solution.py:813
  238.0 6.7 %rest_backward.1 = (bf16[2048,512]{1,0:T(8,128)(2,1)}, f32[8,512]{1,0:T(8,128)}) custom-call(s32[3]{0:T(128)} %bitcast.94, bf16[8,32,2048]{2,1,0:T(8,128)(2,1)} %copy-done.5, f32[2048,640]{1,0:T(8,128)} %get-tuple-element.147.pre_in.pre_b.pre_c, f32[2048,640]{1,0:T(8,128)} %get-tuple-element.147.pre_in.pre_b.pre_c, ...), custom_call_target="tpu_custom_call" | custom-call | flops 1000000 | bytes 100000 | tf_op jit(solution)/shard_map/rest_backward/pallas_call | solution.py:963
  244.7 9.0 %tail_grad.1 = f32[16,104,512]{2,1,0:T(8,128)} custom-call(bf16[2048,1536]{1,0:T(8,128)(2,1)} %get-tuple-element.153.normed, bf16[2048,512]{1,0:T(8,128)(2,1)} %get-tuple-element.172.tail, f32[8,512]{1,0:T(8,128)} %get-tuple-element.168.small), custom_call_target="tpu_custom_call" | custom-call | flops 1000000 | bytes 100000 | tf_op jit(solution)/shard_map/tail_grad/pallas_call | solution.py:1009
  258.2 8.3 %block_out.1 = f32[256,1536]{1,0:T(8,128)} custom-call(bf16[8,256,768]{2,1,0:T(8,128)(2,1)} %copy-done.2, bf16[4,2,2,192,1536]{4,3,2,1,0:T(8,128)(2,1)} %bitcast.71, bf16[256,1536]{1,0:T(8,128)(2,1)} %tokens.3, f32[256,1]{1,0:T(8,128)} %fusion.2.live), custom_call_target="tpu_custom_call" | custom-call | flops 2400000000 | bytes 20000000 | tf_op jit(solution)/shard_map/block_out/pallas_call | solution.py:773
  277.1 9.1 %collective-permute-done.20 = f32[96,384]{1,0:T(8,128)S(1)} collective-permute-done((f32[96,384]{1,0:T(8,128)S(1)}, f32[96,384]{1,0:T(8,128)S(1)}, u32[]{:S(2)}, u32[]{:S(2)}) %collective-permute-start.20) | collective-permute-done | bytes 147488 | tf_op jit(solution)/shard_map/ppermute | solution.py:56
  292.2 9.2 %all-to-all-start.4 = ((f32[8,192,384]{2,1,0:T(8,128)}), f32[8,192,384]{2,1,0:T(8,128)}, u32[]{:S(2)}, u32[]{:S(2)}) async-start(f32[8,192,384]{2,1,0:T(8,128)} %broadcast_in_dim.62), calls=%async_computation.6 | async-start | bytes 4718592 | tf_op jit(solution)/shard_map/all_to_all | solution.py:120
  301.5 11.1 %input_grad.1 = (f32[256,1536]{1,0:T(8,128)}, f32[8,512]{1,0:T(8,128)}) custom-call(f32[1536,256]{1,0:T(8,128)} %z_grad.1.grad_z, bf16[8,256,512]{2,1,0:T(8,128)(2,1)} %copy-done.4, bf16[8,256,512]{2,1,0:T(8,128)(2,1)} %copy-done.4, bf16[4,2,2,96,6400]{4,3,2,1,0:T(8,128)(2,1)} %bitcast.68, bf16[4,2,2,96,6400]{4,3,2,1,0:T(8,128)(2,1)} %bitcast.69, ...), custom_call_target="tpu_custom_call" | custom-call | flops 1000000 | bytes 100000 | tf_op jit(solution)/shard_map/input_grad/pallas_call | solution.py:879
  326.8 8.5 %collective-permute-done.26 = f32[112,512]{1,0:T(8,128)S(1)} collective-permute-done((f32[112,512]{1,0:T(8,128)S(1)}, f32[112,512]{1,0:T(8,128)S(1)}, u32[]{:S(2)}, u32[]{:S(2)}) %collective-permute-start.26) | collective-permute-done | bytes 229408 | tf_op jit(solution)/shard_map/ppermute | solution.py:56
  340.6 5.7 %adam.2 = (f32[96,6400]{1,0:T(8,128)}, f32[96,6400]{1,0:T(8,128)}, f32[96,6400]{1,0:T(8,128)}, f32[96,6400]{1,0:T(8,128)}) custom-call(f32[8,192,384]{2,1,0:T(8,128)} %all-to-all-done.4.pair, f32[96,6400]{1,0:T(8,128)} %refs_0_.6, f32[96,6400]{1,0:T(8,128)} %refs_1_.4, f32[96,6400]{1,0:T(8,128)} %refs_2_.4), custom_call_target="tpu_custom_call" | custom-call | flops 2400000000 | bytes 20000000 | tf_op jit(solution)/shard_map/adam/pallas_call | solution.py:1047
  346.3 5.3 %adam.3 = (f32[192,1536]{1,0:T(8,128)}, f32[192,1536]{1,0:T(8,128)}, f32[192,1536]{1,0:T(8,128)}, f32[192,1536]{1,0:T(8,128)}) custom-call(f32[8,192,384]{2,1,0:T(8,128)} %all-to-all-done.4.pair, f32[192,1536]{1,0:T(8,128)} %refs_0_.7, f32[192,1536]{1,0:T(8,128)} %refs_1_.5, f32[192,1536]{1,0:T(8,128)} %refs_2_.5), custom_call_target="tpu_custom_call" | custom-call | flops 2400000000 | bytes 20000000 | tf_op jit(solution)/shard_map/adam/pallas_call | solution.py:1047
  351.7 16.7 %all-to-all-done.5.pair.rest = f32[8,112,512]{2,1,0:T(8,128)S(1)} async-done(((f32[8,112,512]{2,1,0:T(8,128)}), f32[8,112,512]{2,1,0:T(8,128)S(1)}, u32[]{:S(2)}, u32[]{:S(2)}) %all-to-all-start.5) | async-done | bytes 1835040 | tf_op jit(solution)/shard_map/all_to_all | solution.py:120
  371.0 6.9 %adam_tail.1 = (f32[96,6400]{1,0:T(8,128)}, f32[96,6400]{1,0:T(8,128)}, f32[96,6400]{1,0:T(8,128)}, f32[96,6400]{1,0:T(8,128)}) custom-call(f32[8,112,512]{2,1,0:T(8,128)} %copy-done.3, f32[8,112,512]{2,1,0:T(8,128)} %copy-done.3, f32[96,6400]{1,0:T(8,128)} %refs_0_.6, ...), custom_call_target="tpu_custom_call", output_to_operand_aliasing={{0}: (5, {}), {1}: (6, {}), {2}: (7, {}), {3}: (8, {})} | custom-call | flops 1000000 | bytes 100000 | tf_op jit(solution)/shard_map/adam_tail/pallas_call | solution.py:1090
  (221 shorter events, 118.3 us)
Async XLA Ops:
  7.2 57.8 %all-gather.4.cloned.1.call-start = ((), (), s32[]{:S(2)}) async-start(), calls=%async_computation.8 | async-start | bytes 4644864 | tf_op jit(solution)/shard_map/all_gather | solution.py:115
  7.3 20.8 %collective-permute-start = (bf16[256,1536]{1,0:T(8,128)(2,1)}, bf16[256,1536]{1,0:T(8,128)(2,1)}, u32[]{:S(2)}, u32[]{:S(2)}) collective-permute-start(bf16[256,1536]{1,0:T(8,128)(2,1)} %tokens.3), channel_id=1, source_target_pairs={{0,2},{1,3},{2,4},{3,5},{4,6},{5,7},{6,0},{7,1},{8,10},{9,11},{10,... | collective-permute-start | bytes 2359304 | tf_op jit(solution)/shard_map/ppermute | solution.py:56
  8.9 19.3 %collective-permute-start.1 = (bf16[256,1536]{1,0:T(8,128)(2,1)}, bf16[256,1536]{1,0:T(8,128)(2,1)}, u32[]{:S(2)}, u32[]{:S(2)}) collective-permute-start(bf16[256,1536]{1,0:T(8,128)(2,1)} %tokens.3), channel_id=1, source_target_pairs={{0,6},{1,7},{2,0},{3,1},{4,2},{5,3},{6,4},{7,5},{8,14},{9,15},{10,... | collective-permute-start | bytes 2359304 | tf_op jit(solution)/shard_map/ppermute | solution.py:56
  10.6 19.0 %collective-permute-start.2 = (bf16[256,1536]{1,0:T(8,128)(2,1)}, bf16[256,1536]{1,0:T(8,128)(2,1)}, u32[]{:S(2)}, u32[]{:S(2)}) collective-permute-start(bf16[256,1536]{1,0:T(8,128)(2,1)} %tokens.3), channel_id=1, source_target_pairs={{0,1},{1,0},{2,3},{3,2},{4,5},{5,4},{6,7},{7,6},{8,9},{9,8},{10,11... | collective-permute-start | bytes 2359304 | tf_op jit(solution)/shard_map/ppermute | solution.py:56
  31.5 102.5 %all-gather.6.cloned.1.call-start = ((), (), s32[]{:S(2)}) async-start(), calls=%async_computation.9 | async-start | bytes 10616832 | tf_op jit(solution)/shard_map/all_gather | solution.py:115
  31.9 19.2 %collective-permute-start.4 = (bf16[256,1536]{1,0:T(8,128)(2,1)}, bf16[256,1536]{1,0:T(8,128)(2,1)S(1)}, u32[]{:S(2)}, u32[]{:S(2)}) collective-permute-start(bf16[256,1536]{1,0:T(8,128)(2,1)} %collective-permute-done.refs_7_), channel_id=1, source_target_pairs={{0,2},{1,3},{2,4},{3,5},{4,6},{5,7},{6,0},{7,1},{8,10},{9,11},{10,... | collective-permute-start | bytes 2359304 | tf_op jit(solution)/shard_map/ppermute | solution.py:56
  32.3 18.8 %collective-permute-start.5 = (bf16[256,1536]{1,0:T(8,128)(2,1)}, bf16[256,1536]{1,0:T(8,128)(2,1)S(1)}, u32[]{:S(2)}, u32[]{:S(2)}) collective-permute-start(bf16[256,1536]{1,0:T(8,128)(2,1)} %collective-permute-done.refs_7_), channel_id=1, source_target_pairs={{0,1},{1,0},{2,3},{3,2},{4,5},{5,4},{6,7},{7,6},{8,9},{9,8},{10,11... | collective-permute-start | bytes 2359304 | tf_op jit(solution)/shard_map/ppermute | solution.py:56
  33.9 18.0 %collective-permute-start.6 = (bf16[256,1536]{1,0:T(8,128)(2,1)}, bf16[256,1536]{1,0:T(8,128)(2,1)S(1)}, u32[]{:S(2)}, u32[]{:S(2)}) collective-permute-start(bf16[256,1536]{1,0:T(8,128)(2,1)} %collective-permute-done.2.refs_1_), channel_id=1, source_target_pairs={{0,6},{1,7},{2,0},{3,1},{4,2},{5,3},{6,4},{7,5},{8,14},{9,15},{10,... | collective-permute-start | bytes 2359304 | tf_op jit(solution)/shard_map/ppermute | solution.py:56
  65.0 162.1 %all-gather.8.cloned.1.call-start = ((), (), s32[]{:S(2)}) async-start(), calls=%async_computation.11 | async-start | bytes 22118400 | tf_op jit(solution)/shard_map/all_gather | solution.py:115
  65.6 26.1 %collective-permute-start.8 = (bf16[256,1536]{1,0:T(8,128)(2,1)S(1)}, bf16[256,1536]{1,0:T(8,128)(2,1)}, u32[]{:S(2)}, u32[]{:S(2)}) collective-permute-start(bf16[256,1536]{1,0:T(8,128)(2,1)S(1)} %multiply_convert_fusion.refs_0_), channel_id=1, source_target_pairs={{0,2},{1,3},{2,4},{3,5},{4,6},{5,7},{6,0},{7,1},{8,10},{9,11},{10,... | collective-permute-start | bytes 2359304 | tf_op jit(solution)/shard_map/ppermute | solution.py:56
  67.0 24.6 %collective-permute-start.9 = (bf16[256,1536]{1,0:T(8,128)(2,1)S(1)}, bf16[256,1536]{1,0:T(8,128)(2,1)S(1)}, u32[]{:S(2)}, u32[]{:S(2)}) collective-permute-start(bf16[256,1536]{1,0:T(8,128)(2,1)S(1)} %multiply_convert_fusion.refs_0_), channel_id=1, source_target_pairs={{0,6},{1,7},{2,0},{3,1},{4,2},{5,3},{6,4},{7,5},{8,14},{9,15},{10,... | collective-permute-start | bytes 2359304 | tf_op jit(solution)/shard_map/ppermute | solution.py:56
  68.8 22.9 %collective-permute-start.10 = (bf16[256,1536]{1,0:T(8,128)(2,1)S(1)}, bf16[256,1536]{1,0:T(8,128)(2,1)}, u32[]{:S(2)}, u32[]{:S(2)}) collective-permute-start(bf16[256,1536]{1,0:T(8,128)(2,1)S(1)} %multiply_convert_fusion.refs_0_), channel_id=1, source_target_pairs={{0,1},{1,0},{2,3},{3,2},{4,5},{5,4},{6,7},{7,6},{8,9},{9,8},{10,11... | collective-permute-start | bytes 2359304 | tf_op jit(solution)/shard_map/ppermute | solution.py:56
  71.3 57.4 %collective-permute-start.16 = (bf16[96,6400]{1,0:T(8,128)(2,1)S(1)}, bf16[96,6400]{1,0:T(8,128)(2,1)}, u32[]{:S(2)}, u32[]{:S(2)}) collective-permute-start(bf16[96,6400]{1,0:T(8,128)(2,1)S(1)} %convert_element_type.48), channel_id=1, source_target_pairs={{0,65},{1,64},{2,67},{3,66},{4,69},{5,68},{6,71},{7,70},{8,73},{9,... | collective-permute-start | bytes 3686408 | tf_op jit(solution)/shard_map/ppermute | solution.py:56
  91.7 19.9 %collective-permute-start.13 = (bf16[256,1536]{1,0:T(8,128)(2,1)}, bf16[256,1536]{1,0:T(8,128)(2,1)}, u32[]{:S(2)}, u32[]{:S(2)}) collective-permute-start(bf16[256,1536]{1,0:T(8,128)(2,1)} %collective-permute-done.8.refs_7_), channel_id=1, source_target_pairs={{0,2},{1,3},{2,4},{3,5},{4,6},{5,7},{6,0},{7,1},{8,10},{9,11},{10,... | collective-permute-start | bytes 2359304 | tf_op jit(solution)/shard_map/ppermute | solution.py:56
  92.6 19.1 %collective-permute-start.14 = (bf16[256,1536]{1,0:T(8,128)(2,1)}, bf16[256,1536]{1,0:T(8,128)(2,1)S(1)}, u32[]{:S(2)}, u32[]{:S(2)}) collective-permute-start(bf16[256,1536]{1,0:T(8,128)(2,1)} %collective-permute-done.8.refs_7_), channel_id=1, source_target_pairs={{0,1},{1,0},{2,3},{3,2},{4,5},{5,4},{6,7},{7,6},{8,9},{9,8},{10,11... | collective-permute-start | bytes 2359304 | tf_op jit(solution)/shard_map/ppermute | solution.py:56
  92.9 18.7 %collective-permute-start.15 = (bf16[256,1536]{1,0:T(8,128)(2,1)}, bf16[256,1536]{1,0:T(8,128)(2,1)S(1)}, u32[]{:S(2)}, u32[]{:S(2)}) collective-permute-start(bf16[256,1536]{1,0:T(8,128)(2,1)} %collective-permute-done.10.refs_1_), channel_id=1, source_target_pairs={{0,6},{1,7},{2,0},{3,1},{4,2},{5,3},{6,4},{7,5},{8,14},{9,15},{10,... | collective-permute-start | bytes 2359304 | tf_op jit(solution)/shard_map/ppermute | solution.py:56
  112.5 16.2 %collective-permute-start.17 = (bf16[128,1536]{1,0:T(8,128)(2,1)}, bf16[128,1536]{1,0:T(8,128)(2,1)S(1)}, u32[]{:S(2)}, u32[]{:S(2)}) collective-permute-start(bf16[128,1536]{1,0:T(8,128)(2,1)} %slice.135), channel_id=1, source_target_pairs={{0,2},{1,3},{2,4},{3,5},{4,6},{5,7},{6,0},{7,1},{8,10},{9,11},{10,... | collective-permute-start | bytes 1179656 | tf_op jit(solution)/shard_map/ppermute | solution.py:56
  169.9 48.6 %all-to-all-start.1 = ((bf16[8,256,768]{2,1,0:T(8,128)(2,1)}), bf16[8,256,768]{2,1,0:T(8,128)(2,1)S(1)}, u32[]{:S(2)}, u32[]{:S(2)}) async-start(bf16[8,256,768]{2,1,0:T(8,128)(2,1)} %bitcast.74), calls=%async_computation.1 | async-start | bytes 6291456 | tf_op jit(solution)/shard_map/all_to_all | solution.py:120
  173.6 95.9 %reduce-scatter.3.cloned.1.call-start = ((), (), s32[]{:S(2)}) async-start(), calls=%async_computation.10 | async-start | bytes 5308416 | tf_op jit(solution)/shard_map/reduce_scatter | solution.py:135
  220.2 16.8 %all-to-all-start.2 = ((bf16[8,32,2048]{2,1,0:T(8,128)(2,1)}), bf16[8,32,2048]{2,1,0:T(8,128)(2,1)S(1)}, u32[]{:S(2)}, u32[]{:S(2)}) async-start(bf16[8,32,2048]{2,1,0:T(8,128)(2,1)} %bitcast.78), calls=%async_computation.3 | async-start | bytes 2097152 | tf_op jit(solution)/shard_map/all_to_all | solution.py:120
  225.6 96.2 %reduce-scatter.5.cloned.1.call-start = ((), (), s32[]{:S(2)}) async-start(), calls=%async_computation.12 | async-start | bytes 3833856 | tf_op jit(solution)/shard_map/reduce_scatter | solution.py:135
  253.7 35.8 %all-to-all-start.3 = ((bf16[8,256,512]{2,1,0:T(8,128)(2,1)}), bf16[8,256,512]{2,1,0:T(8,128)(2,1)S(1)}, u32[]{:S(2)}, u32[]{:S(2)}) async-start(bf16[8,256,512]{2,1,0:T(8,128)(2,1)} %bitcast.75), calls=%async_computation.4 | async-start | bytes 4194304 | tf_op jit(solution)/shard_map/all_to_all | solution.py:120
  292.2 43.0 %all-to-all-start.4 = ((f32[8,192,384]{2,1,0:T(8,128)}), f32[8,192,384]{2,1,0:T(8,128)}, u32[]{:S(2)}, u32[]{:S(2)}) async-start(f32[8,192,384]{2,1,0:T(8,128)} %broadcast_in_dim.62), calls=%async_computation.6 | async-start | bytes 4718592 | tf_op jit(solution)/shard_map/all_to_all | solution.py:120
  336.8 31.5 %all-to-all-start.5 = ((f32[8,112,512]{2,1,0:T(8,128)}), f32[8,112,512]{2,1,0:T(8,128)S(1)}, u32[]{:S(2)}, u32[]{:S(2)}) async-start(f32[8,112,512]{2,1,0:T(8,128)} %broadcast_in_dim.63), calls=%async_computation.7 | async-start | bytes 3670016 | tf_op jit(solution)/shard_map/all_to_all | solution.py:120
  (38 other events, 408.6 us)
Sparse Core Ops, SparseCore 0:
  31.6 33.3 all-gather.3
  67.2 54.1 all-gather.5
  132.3 94.7 all-gather.7
  229.4 40.0 reduce-scatter.2
  271.7 41.7 reduce-scatter.4
where the time goes:
time: 387 us; the launch traced here: 384 us
  Pallas kernels  172 us (44%)
  waiting for transfers between devices  80.2 us (21%)
  starting transfers between devices  71.1 us (18%)
  local copies, waits for them, and re-layouts  20.2 us (5%)
  other arithmetic  16.7 us (4%)
  between operations  14.5 us (4%)
  blocking collectives  10.2 us (3%)
    ppermute x27, waiting for transfers between devices, move(): return lax.ppermute(value, ('fsdp', 'rep'), pairs)  54.4 us
    ppermute x27, starting transfers between devices, move(): return lax.ppermute(value, ('fsdp', 'rep'), pairs)  45 us
    pallas_call x1, Pallas kernels, run_backward(): pl.pallas_call(backward_kernel, grid=(CHUNKS,), in_specs=[pl.BlockSpec(me...  32.3 us
    all_to_all x5, starting transfers between devices, exchange(): return lax.all_to_all(value, axis, 0, 0, tiled=True)  25.7 us
    pallas_call x2, Pallas kernels, run_forward(): pl.pallas_call(partial(forward_kernel, part), grid=(HALF,), in_specs=[pl....  24.2 us
    all_to_all x5, waiting for transfers between devices, exchange(): return lax.all_to_all(value, axis, 0, 0, tiled=True)  19.4 us
    pallas_call x1, Pallas kernels, run_project(): pl.pallas_call(partial(project_kernel, PARTS), grid_spec=pltpu.PrefetchSc...  17.4 us
    pallas_call x1, Pallas kernels, run_out_grad(): pl.pallas_call(out_grad_kernel, grid_spec=pltpu.PrefetchScalarGridSpec(nu...  13.6 us
  transfers between devices with their start and end apart: 37, of which 22 were waited for; matrix products, arithmetic and copies ran while one was open for 7% of the time, Pallas kernels for 43%

commit v1 on v0

--- a/solution.py
+++ b/solution.py
@@ -439,8 +439,8 @@
     grad_c = precise_product(grad_scores.T, state_b) + joined_product(
         entered_parts, split_two(state_in), 1, 1
     )
-    grad_bc[0:N, :] = grad_b.T.astype(BF16)
-    grad_bc[N:, :] = grad_c.T.astype(BF16)
+    grad_bc[0:N, :] = grad_b.T
+    grad_bc[N:, :] = grad_c.T
     new_carry = spread(facts["passing"], lane[:1]) * carry + joined_product(
         split_two(state_c.T), entered_parts
     )
@@ -503,7 +503,7 @@
         out_shape=[
             jax.ShapeDtypeStruct((PACK, OWN), BF16),
             jax.ShapeDtypeStruct((PACK, N), BF16),
-            jax.ShapeDtypeStruct((2 * N, PACK), BF16),
+            jax.ShapeDtypeStruct((2 * N, PACK), F32),
             jax.ShapeDtypeStruct((8, OWN), F32),
             jax.ShapeDtypeStruct((8, N), F32),
         ],
@@ -828,7 +828,7 @@
 
 
 def input_grad_kernel(
-    grad_z, x_rows, rest_rows, w_x, w_bc, low_dt, tokens, cotangent, gain, out, gain_out, total, ordered
+    own_half, grad_z, x_rows, rest_rows, w_x, w_bc, low_dt, tokens, cotangent, gain, out, gain_out, total, ordered
 ):
     step = pl.program_id(0)
     part = turned_part(w_x, jnp.concatenate([x_rows[0], x_rows[1]], 1))
@@ -857,10 +857,11 @@
             start = 8 + m * OWN_H
             value = pltpu.roll(rest_rows[m].astype(F32), (start - OWN_BC) % N, 1)
             steps = jnp.where((lane >= start) & (lane < start + OWN_H), value, steps)
-        shared = total[...] + turned_part(w_bc, jnp.concatenate(groups, 1))
+        total[...] += turned_part(w_bc, jnp.concatenate(groups, 1))
         for f in range(N_FSDP):
-            start = eight_order(f) * SHARD_IN
-            ordered[f * SHARD_IN : (f + 1) * SHARD_IN, :] = shared[start : start + SHARD_IN, :]
+            place = eight_order(f) - f // 8 + (f // 8 + own_half[0]) % 2
+            start = pl.multiple_of(place * SHARD_IN, SHARD_IN)
+            ordered[f * SHARD_IN : (f + 1) * SHARD_IN, :] = total[pl.ds(start, SHARD_IN), :]
         grad_h = (ordered[...] + product(low_dt[...], steps.astype(BF16), 1, 1)).T
         values = tokens[...].astype(F32)
         scale = lax.rsqrt(jnp.mean(values * values, axis=1, keepdims=True) + NORM_EPS)
@@ -874,12 +875,13 @@
         out[...] = cotangent[...].astype(F32) + scale * (grad_unit - unit * inner)
 
 
-def run_input_grad(grad_z, tail_rows, full_in, low_dt, tokens, cotangent, gain):
+def run_input_grad(own_half, grad_z, tail_rows, full_in, low_dt, tokens, cotangent, gain):
     fixed = lambda shape: pl.BlockSpec(shape, lambda i: (0,) * len(shape))
     return pl.pallas_call(
         input_grad_kernel,
         grid=(N_REP // 2,),
         in_specs=[
+            pl.BlockSpec(memory_space=pltpu.SMEM),
             fixed((D, ROWS)),
             pl.BlockSpec((2, ROWS, OWN), lambda i: (i, 0, 0)),
             pl.BlockSpec((N_REP, ROWS, N), lambda i: (0, 0, OWN // N)),
@@ -898,7 +900,7 @@
         ),
         cost_estimate=COST,
         name="input_grad",
-    )(grad_z, tail_rows, tail_rows, full_in, full_in, low_dt, tokens, cotangent, gain)
+    )(own_half, grad_z, tail_rows, tail_rows, full_in, full_in, low_dt, tokens, cotangent, gain)
 
 
 def rest_kernel(
@@ -910,9 +912,9 @@
     def pick(value):
         return product(jnp.concatenate([chosen] * 3, 1), jnp.concatenate(split_three(value), 1), 1, 1)
 
-    grad = parts[0].astype(F32)
+    grad = parts[0]
     for k in range(1, N_REP):
-        grad = grad + parts[k].astype(F32)
+        grad = grad + parts[k]
     own_pre = pick(jnp.concatenate([pre_b[...], pre_c[...]], 1))
     own_conv = product(chosen, conv_in[...].astype(BF16), 1, 1)
     taps = pick(par[:, OWN:])
@@ -1166,18 +1168,20 @@
 
     out_low, other_columns = lax.optimization_barrier((out_low, other_columns))
     out_other = move(out_low, lambda yh, z, c, x, yl: (yh + 1, z, c, x, yl + 1))
-    from_left, from_right, partner, other_columns = lax.optimization_barrier(
-        (from_left, from_right, partner, other_columns)
+    branch = (cotangent.astype(F32) * own_live).astype(BF16)
+    from_left, from_right, partner, other_columns, branch = lax.optimization_barrier(
+        (from_left, from_right, partner, other_columns, branch)
     )
     own_shards = gather_eight(both(own_columns(r), other_columns, place.yh))
     far = move(from_left, along_x(1))
     partner_left = move(from_left, swap_y)
     partner_right = move(partner, along_x(-1))
 
-    branch = (cotangent.astype(F32) * own_live).astype(BF16)
-    far, partner_left, partner_right, out_other, branch = lax.optimization_barrier(
-        (far, partner_left, partner_right, out_other, branch)
-    )
+    b_partner = move(branch, swap_y)
+    far, partner_left, partner_right, out_other, branch, in_low = lax.optimization_barrier(
+        (far, partner_left, partner_right, out_other, branch, in_low)
+    )
+    in_other = move(in_low, lambda yh, z, c, x, yl: (yh + 1, z, c, x, yl + 1))
     out_pair = both(out_low, out_other, place.yh)
     partner_far_top = move(partner_left[:half], along_x(1))
     partner_far_low = move(partner_right[half:], along_x(-1))
@@ -1205,14 +1209,12 @@
     )
     par = jnp.concatenate([conv_par, head_par, jnp.zeros((8, 640), F32)], 0)
 
-    in_low, partner_far_top, partner_far_low, own_shards = lax.optimization_barrier(
-        (in_low, partner_far_top, partner_far_low, own_shards)
+    partner_far_top, partner_far_low, own_shards, b_partner = lax.optimization_barrier(
+        (partner_far_top, partner_far_low, own_shards, b_partner)
     )
     full_out = gather_eight(tie(out_pair, own_shards))
-    in_other = move(in_low, lambda yh, z, c, x, yl: (yh + 1, z, c, x, yl + 1))
     b_left = move(branch, along_x(1))
     b_right = move(branch, along_x(-1))
-    b_partner = move(branch, swap_y)
     token_pieces = [
         tokens, partner, from_right, partner_right, far,
         partner_far_top, partner_far_low, from_left, partner_left,
@@ -1232,7 +1234,7 @@
     mixed, in_low, in_other, b_partner_far_top, b_partner_far_low = lax.optimization_barrier(
         (mixed, in_low, in_other, b_partner_far_top, b_partner_far_low)
     )
-    full_in = gather_eight(both(in_low, in_other, place.yh))
+    full_in = gather_eight(jnp.stack([in_low, in_other], 0))
     branch_pieces = [
         branch, b_partner, b_right, b_partner_right, b_far,
         b_partner_far_top, b_partner_far_low, b_left, b_partner_left,
@@ -1276,14 +1278,15 @@
     z_other = move(other[SHARD_IN:], swap_y_hi)
     tail_rows, out_mine, out_other, z_other = lax.optimization_barrier((tail_rows, out_mine, out_other, z_other))
 
-    early_parts = share_rep(jnp.concatenate([out_mine + out_other, mine[SHARD_IN:] + z_other], 0))
     input_grad, grad_gain_in = run_input_grad(
-        grad_rows, tail_rows, full_in, low_dt, tokens, cotangent, gain_in
-    )
-
+        place.yh[None], grad_rows, tail_rows, full_in, low_dt, tokens, cotangent, gain_in
+    )
+    early = jnp.concatenate([out_mine + out_other, mine[SHARD_IN:] + z_other], 0)
+    early, grad_gain_in = lax.optimization_barrier((early, grad_gain_in))
+
+    early_parts = share_rep(early)
     grad_gain_in = sum_z(grad_gain_in + move(grad_gain_in, swap_core))
     tail_part, grad_gain_in = lax.optimization_barrier((tail_part, grad_gain_in))
-    gain_rows = grad_gain_in.shape[0]
     tail_other = move(with_rows(at(tail_part, 1 - place.yh), grad_gain_in), swap_y_hi)
     tail_part = with_rows(at(tail_part, place.yh), grad_gain_in) + tail_other
 
@@ -1301,8 +1304,8 @@
     def columns(parts):
         return parts.transpose(1, 0, 2).reshape(parts.shape[1], -1)
 
-    grad_gain_in = tail_parts[:, -gain_rows : D // TAIL - gain_rows].sum(0).reshape(-1)
-    small_parts = tail_parts[:, SHARD_IN:-gain_rows]
+    small_parts = tail_parts[:, SHARD_IN : SHARD_IN + 8]
+    grad_gain_in = tail_parts[:, SHARD_IN + 8 : SHARD_IN + 8 + D // TAIL].sum(0).reshape(-1)
     small_x = small_parts[:, :, :OWN].transpose(1, 0, 2).reshape(8, DI)
     small_bc = small_parts[:, :, OWN:].transpose(1, 0, 2)
 

time: 387 us -> 403 us (1.041)
  waiting for transfers between devices: 80.2 us -> 99.1 us
    ppermute x27, waiting for transfers between devices: 54.4 us -> 67.2 us  [move(): return lax.ppermute(value, ('fsdp', 'rep'), pairs)]
    all_to_all x5, waiting for transfers between devices: 19.4 us -> 28.9 us  [exchange(): return lax.all_to_all(value, axis, 0, 0, tiled=True)]
  transfers between devices with their start and end apart: 37 -> 37, of which waited for: 22 -> 19; matrix products, arithmetic and copies ran while one was open for 7% -> 6% of each run, Pallas kernels for 43% -> 41%
where the time goes in v1:
time: 403 us; the launch traced here: 401 us
  Pallas kernels  170 us (42%)
  waiting for transfers between devices  99.1 us (25%)
  starting transfers between devices  68.8 us (17%)
  local copies, waits for them, and re-layouts  22.5 us (6%)
  other arithmetic  15.6 us (4%)
  between operations  14.5 us (4%)
  blocking collectives  10.2 us (3%)
    ppermute x27, waiting for transfers between devices, move(): return lax.ppermute(value, ('fsdp', 'rep'), pairs)  67.2 us
    ppermute x27, starting transfers between devices, move(): return lax.ppermute(value, ('fsdp', 'rep'), pairs)  44.3 us
    pallas_call x1, Pallas kernels, run_backward(): pl.pallas_call(backward_kernel, grid=(CHUNKS,), in_specs=[pl.BlockSpec(me...  32.1 us
    all_to_all x5, waiting for transfers between devices, exchange(): return lax.all_to_all(value, axis, 0, 0, tiled=True)  28.9 us
    pallas_call x2, Pallas kernels, run_forward(): pl.pallas_call(partial(forward_kernel, part), grid=(HALF,), in_specs=[pl....  24.4 us
    all_to_all x5, starting transfers between devices, exchange(): return lax.all_to_all(value, axis, 0, 0, tiled=True)  24.4 us
    pallas_call x1, Pallas kernels, run_project(): pl.pallas_call(partial(project_kernel, PARTS), grid_spec=pltpu.PrefetchSc...  17.2 us
    pallas_call x1, Pallas kernels, run_out_grad(): pl.pallas_call(out_grad_kernel, grid_spec=pltpu.PrefetchScalarGridSpec(nu...  13.6 us
  transfers between devices with their start and end apart: 37, of which 19 were waited for; matrix products, arithmetic and copies ran while one was open for 6% of the time, Pallas kernels for 41%

profile of v1, /device:TPU:0, one launch (start us, length us, event | category | flops | bytes accessed | tf_op | source)
XLA Modules:
  0.0 401.0 jit_solution(12195991086004010896)
XLA Ops:
  39.5 11.1 %collective-permute-done.7 = bf16[192,1536]{1,0:T(8,128)(2,1)S(1)} collective-permute-done((bf16[192,1536]{1,0:T(8,128)(2,1)S(1)}, bf16[192,1536]{1,0:T(8,128)(2,1)S(1)}, u32[]{:S(2)}, u32[]{:S(2)}) %collective-permute-start.7) | collective-permute-done | bytes 589856 | tf_op jit(solution)/shard_map/ppermute | solution.py:56
  58.9 8.0 %collective-permute-done.12.refs_1_ = bf16[256,1536]{1,0:T(8,128)(2,1)} collective-permute-done((bf16[256,1536]{1,0:T(8,128)(2,1)S(1)}, bf16[256,1536]{1,0:T(8,128)(2,1)}, u32[]{:S(2)}, u32[]{:S(2)}) %collective-permute-start.12) | collective-permute-done | bytes 786464 | tf_op jit(solution)/shard_map/ppermute | solution.py:56
  75.5 17.2 %project.1 = (bf16[2048,1536]{1,0:T(8,128)(2,1)}, f32[2048,1152]{1,0:T(8,128)}, bf16[1536,128]{1,0:T(8,128)(2,1)}) custom-call(s32[8]{0:T(128)} %fusion.6.table, bf16[256,1536]{1,0:T(8,128)(2,1)} %tokens.3, bf16[256,1536]{1,0:T(8,128)(2,1)} %collective-permute-done.2.refs_1_, bf16[256,1536]{1,0:T(8,128)(2,1)} %collective-permute-done.1.refs_2_, ...), custom_call_target="tpu_custom_call" | custom-call | flops 1000000 | bytes 100000 | tf_op jit(solution)/shard_map/project/pallas_call | solution.py:584
  97.7 12.2 %scan_forward.2 = (f32[2048,640]{1,0:T(8,128)}, f32[2048,384]{1,0:T(8,128)}, f32[2048,384]{1,0:T(8,128)}, f32[136,640]{1,0:T(8,128)}) custom-call(s32[3]{0:T(128)} %bitcast.91, f32[2048,1152]{1,0:T(8,128)} %get-tuple-element.131.proj.refs_11_.gate_in.conv_in.dt_in, f32[16,640]{1,0:T(8,128)} %concatenate.42.par), custom_call_target="tpu_custom_call" | custom-call | flops 1000000 | bytes 100000 | tf_op jit(solution)/shard_map/scan_forward/pallas_call | solution.py:355
  115.0 12.2 %scan_forward.3 = (f32[2048,640]{1,0:T(8,128)}, f32[2048,384]{1,0:T(8,128)}, f32[2048,384]{1,0:T(8,128)}, f32[136,640]{1,0:T(8,128)}) custom-call(s32[3]{0:T(128)} %bitcast.92, f32[2048,1152]{1,0:T(8,128)} %get-tuple-element.131.proj.refs_11_.gate_in.conv_in.dt_in, ...), custom_call_target="tpu_custom_call", output_to_operand_aliasing={{0}: (3, {}), {1}: (4, {}), {2}: (5, {})} | custom-call | flops 1000000 | bytes 100000 | tf_op jit(solution)/shard_map/scan_forward/pallas_call | solution.py:355
  132.2 13.6 %out_grad.1 = (bf16[2048,1536]{1,0:T(8,128)(2,1)}, f32[2048,384]{1,0:T(8,128)}, f32[8,2048]{1,0:T(8,128)}) custom-call(s32[9]{0:T(128)} %pad_add_fusion.table, bf16[256,1536]{1,0:T(8,128)(2,1)} %copy-done.7, bf16[256,1536]{1,0:T(8,128)(2,1)} %collective-permute-done.12.refs_1_, bf16[256,1536]{1,0:T(8,128)(2,1)} %copy-done.13, bf16[256,1536]{1,0:T(8,128)(2,1)} %copy-done.10, ...), custom_call_target="tpu_custom_call" | custom-call | flops 1000000 | bytes 100000 | tf_op jit(solution)/shard_map/out_grad/pallas_call | solution.py:641
  146.7 10.2 %all_to_all.34 = f32[8,32,128]{2,1,0:T(8,128)S(1)} all-to-all(f32[8,32,128]{2,1,0:T(8,128)S(1)} %broadcast_in_dim.62), channel_id=1, replica_groups=mesh['fsdp'=16,'rep'=8] {'rep'}, dimensions={0} | all-to-all | bytes 262144 | tf_op jit(solution)/shard_map/all_to_all | solution.py:120
  157.5 10.2 %gate_backward.1 = (bf16[2048,768]{1,0:T(8,128)(2,1)}, f32[2048,384]{1,0:T(8,128)}, f32[8,384]{1,0:T(8,128)}) custom-call(f32[2048,384]{1,0:T(8,128)} %get-tuple-element.150.grad_out, f32[2048,384]{1,0:T(8,128)} %get-tuple-element.149.refs_10_.mixed_in, f32[2048,1152]{1,0:T(8,128)} %get-tuple-element.131.proj.refs_11_.gate_in.conv_in.dt_in, ...), custom_call_target="tpu_custom_call" | custom-call | flops 1000000 | bytes 100000 | tf_op jit(solution)/shard_map/gate_backward/pallas_call | solution.py:696
  171.5 32.1 %scan_backward.1 = (bf16[2048,384]{1,0:T(8,128)(2,1)}, bf16[2048,128]{1,0:T(8,128)(2,1)}, f32[256,2048]{1,0:T(8,128)}, f32[8,384]{1,0:T(8,128)}, f32[8,128]{1,0:T(8,128)}) custom-call(s32[3]{0:T(128)} %bitcast.93, f32[2048,1152]{1,0:T(8,128)} %get-tuple-element.131.proj.refs_11_.gate_in.conv_in.dt_in, ...), custom_call_target="tpu_custom_call" | custom-call | flops 1000000 | bytes 100000 | tf_op jit(solution)/shard_map/scan_backward/pallas_call | solution.py:483
  203.5 12.3 %early_grad.1 = f32[16,192,384]{2,1,0:T(8,128)} custom-call(bf16[2048,768]{1,0:T(8,128)(2,1)} %get-tuple-element.157.low, bf16[2048,1536]{1,0:T(8,128)(2,1)} %get-tuple-element.158.grad_branch, bf16[2048,1536]{1,0:T(8,128)(2,1)} %get-tuple-element.159.normed), custom_call_target="tpu_custom_call" | custom-call | flops 1000000 | bytes 100000 | tf_op jit(solution)/shard_map/early_grad/pallas_call | solution.py:740
  217.5 6.1 %all-to-all-start.2 = ((f32[8,32,2048]{2,1,0:T(8,128)}), f32[8,32,2048]{2,1,0:T(8,128)S(1)}, u32[]{:S(2)}, u32[]{:S(2)}) async-start(f32[8,32,2048]{2,1,0:T(8,128)} %bitcast.78), calls=%async_computation.3 | async-start | bytes 4194304 | tf_op jit(solution)/shard_map/all_to_all | solution.py:120
  226.4 7.8 %z_grad.1.grad_z = f32[1536,256]{1,0:T(8,128)} custom-call(bf16[8,256,768]{2,1,0:T(8,128)(2,1)} %copy-done.2, bf16[4,2,2,96,6400]{4,3,2,1,0:T(8,128)(2,1)} %bitcast.66), custom_call_target="tpu_custom_call" | custom-call | flops 2400000000 | bytes 20000000 | tf_op jit(solution)/shard_map/z_grad/pallas_call | solution.py:813
  234.2 12.9 %all-to-all-done.2.parts = f32[8,32,2048]{2,1,0:T(8,128)S(1)} async-done(((f32[8,32,2048]{2,1,0:T(8,128)}), f32[8,32,2048]{2,1,0:T(8,128)S(1)}, u32[]{:S(2)}, u32[]{:S(2)}) %all-to-all-start.2) | async-done | bytes 2097184 | tf_op jit(solution)/shard_map/all_to_all | solution.py:120
  248.4 6.7 %rest_backward.1 = (bf16[2048,512]{1,0:T(8,128)(2,1)}, f32[8,512]{1,0:T(8,128)}) custom-call(s32[3]{0:T(128)} %bitcast.94, f32[8,32,2048]{2,1,0:T(8,128)} %copy-done.6, f32[2048,640]{1,0:T(8,128)} %get-tuple-element.153.pre_in.pre_b.pre_c, f32[2048,640]{1,0:T(8,128)} %get-tuple-element.153.pre_in.pre_b.pre_c, ...), custom_call_target="tpu_custom_call" | custom-call | flops 1000000 | bytes 100000 | tf_op jit(solution)/shard_map/rest_backward/pallas_call | solution.py:965
  255.1 9.0 %tail_grad.1 = f32[16,104,512]{2,1,0:T(8,128)} custom-call(bf16[2048,1536]{1,0:T(8,128)(2,1)} %get-tuple-element.159.normed, bf16[2048,512]{1,0:T(8,128)(2,1)} %get-tuple-element.178.tail, f32[8,512]{1,0:T(8,128)} %get-tuple-element.174.small), custom_call_target="tpu_custom_call" | custom-call | flops 1000000 | bytes 100000 | tf_op jit(solution)/shard_map/tail_grad/pallas_call | solution.py:1011
  268.8 8.1 %block_out.1 = f32[256,1536]{1,0:T(8,128)} custom-call(bf16[8,256,768]{2,1,0:T(8,128)(2,1)} %copy-done.2, bf16[4,2,2,192,1536]{4,3,2,1,0:T(8,128)(2,1)} %bitcast.70, bf16[256,1536]{1,0:T(8,128)(2,1)} %tokens.3, f32[256,1]{1,0:T(8,128)} %fusion.2.live), custom_call_target="tpu_custom_call" | custom-call | flops 2400000000 | bytes 20000000 | tf_op jit(solution)/shard_map/block_out/pallas_call | solution.py:773
  284.8 5.2 %collective-permute-done.20 = f32[96,384]{1,0:T(8,128)S(1)} collective-permute-done((f32[96,384]{1,0:T(8,128)S(1)}, f32[96,384]{1,0:T(8,128)S(1)}, u32[]{:S(2)}, u32[]{:S(2)}) %collective-permute-start.20) | collective-permute-done | bytes 147488 | tf_op jit(solution)/shard_map/ppermute | solution.py:56
  296.4 11.2 %input_grad.1 = (f32[256,1536]{1,0:T(8,128)}, f32[8,512]{1,0:T(8,128)}) custom-call(s32[1]{0:T(128)} %bitcast.21.own_half, f32[1536,256]{1,0:T(8,128)} %z_grad.1.grad_z, bf16[8,256,512]{2,1,0:T(8,128)(2,1)} %copy-done.4, bf16[8,256,512]{2,1,0:T(8,128)(2,1)} %copy-done.4, bf16[4,2,2,96,6400]{4,3,2,1,0:T(8,128)(2,1)} %bitcast.67, ...), custom_call_target="tpu_custom_call" | custom-call | flops 1000000 | bytes 100000 | tf_op jit(solution)/shard_map/input_grad/pallas_call | solution.py:880
  310.1 6.0 %all-to-all-start.4 = ((f32[8,192,384]{2,1,0:T(8,128)}), f32[8,192,384]{2,1,0:T(8,128)S(1)}, u32[]{:S(2)}, u32[]{:S(2)}) async-start(f32[8,192,384]{2,1,0:T(8,128)} %broadcast_in_dim.66), calls=%async_computation.6 | async-start | bytes 4718592 | tf_op jit(solution)/shard_map/all_to_all | solution.py:120
  329.7 21.2 %collective-permute-done.26 = f32[112,512]{1,0:T(8,128)S(1)} collective-permute-done((f32[112,512]{1,0:T(8,128)S(1)}, f32[112,512]{1,0:T(8,128)S(1)}, u32[]{:S(2)}, u32[]{:S(2)}) %collective-permute-start.26) | collective-permute-done | bytes 229408 | tf_op jit(solution)/shard_map/ppermute | solution.py:56
  357.8 5.7 %adam.2 = (f32[96,6400]{1,0:T(8,128)}, f32[96,6400]{1,0:T(8,128)}, f32[96,6400]{1,0:T(8,128)}, f32[96,6400]{1,0:T(8,128)}) custom-call(f32[8,192,384]{2,1,0:T(8,128)} %copy-done.5, f32[96,6400]{1,0:T(8,128)} %refs_0_.6, f32[96,6400]{1,0:T(8,128)} %refs_1_.4, f32[96,6400]{1,0:T(8,128)} %refs_2_.4), custom_call_target="tpu_custom_call" | custom-call | flops 2400000000 | bytes 20000000 | tf_op jit(solution)/shard_map/adam/pallas_call | solution.py:1049
  363.5 5.3 %adam.3 = (f32[192,1536]{1,0:T(8,128)}, f32[192,1536]{1,0:T(8,128)}, f32[192,1536]{1,0:T(8,128)}, f32[192,1536]{1,0:T(8,128)}) custom-call(f32[8,192,384]{2,1,0:T(8,128)} %copy-done.5, f32[192,1536]{1,0:T(8,128)} %refs_0_.7, f32[192,1536]{1,0:T(8,128)} %refs_1_.5, f32[192,1536]{1,0:T(8,128)} %refs_2_.5), custom_call_target="tpu_custom_call" | custom-call | flops 2400000000 | bytes 20000000 | tf_op jit(solution)/shard_map/adam/pallas_call | solution.py:1049
  368.9 16.0 %all-to-all-done.5.pair.rest = f32[8,112,512]{2,1,0:T(8,128)S(1)} async-done(((f32[8,112,512]{2,1,0:T(8,128)}), f32[8,112,512]{2,1,0:T(8,128)S(1)}, u32[]{:S(2)}, u32[]{:S(2)}) %all-to-all-start.5) | async-done | bytes 1835040 | tf_op jit(solution)/shard_map/all_to_all | solution.py:120
  387.6 6.9 %adam_tail.1 = (f32[96,6400]{1,0:T(8,128)}, f32[96,6400]{1,0:T(8,128)}, f32[96,6400]{1,0:T(8,128)}, f32[96,6400]{1,0:T(8,128)}) custom-call(f32[8,112,512]{2,1,0:T(8,128)} %copy-done.3, f32[8,112,512]{2,1,0:T(8,128)} %copy-done.3, f32[96,6400]{1,0:T(8,128)} %refs_0_.6, ...), custom_call_target="tpu_custom_call", output_to_operand_aliasing={{0}: (5, {}), {1}: (6, {}), {2}: (7, {}), {3}: (8, {})} | custom-call | flops 1000000 | bytes 100000 | tf_op jit(solution)/shard_map/adam_tail/pallas_call | solution.py:1092
  (222 shorter events, 119.5 us)
Async XLA Ops:
  7.2 59.6 %all-gather.4.cloned.1.call-start = ((), (), s32[]{:S(2)}) async-start(), calls=%async_computation.8 | async-start | bytes 4644864 | tf_op jit(solution)/shard_map/all_gather | solution.py:115
  7.3 20.8 %collective-permute-start = (bf16[256,1536]{1,0:T(8,128)(2,1)}, bf16[256,1536]{1,0:T(8,128)(2,1)}, u32[]{:S(2)}, u32[]{:S(2)}) collective-permute-start(bf16[256,1536]{1,0:T(8,128)(2,1)} %tokens.3), channel_id=1, source_target_pairs={{0,2},{1,3},{2,4},{3,5},{4,6},{5,7},{6,0},{7,1},{8,10},{9,11},{10,... | collective-permute-start | bytes 2359304 | tf_op jit(solution)/shard_map/ppermute | solution.py:56
  8.9 19.3 %collective-permute-start.1 = (bf16[256,1536]{1,0:T(8,128)(2,1)}, bf16[256,1536]{1,0:T(8,128)(2,1)}, u32[]{:S(2)}, u32[]{:S(2)}) collective-permute-start(bf16[256,1536]{1,0:T(8,128)(2,1)} %tokens.3), channel_id=1, source_target_pairs={{0,6},{1,7},{2,0},{3,1},{4,2},{5,3},{6,4},{7,5},{8,14},{9,15},{10,... | collective-permute-start | bytes 2359304 | tf_op jit(solution)/shard_map/ppermute | solution.py:56
  10.6 19.0 %collective-permute-start.2 = (bf16[256,1536]{1,0:T(8,128)(2,1)}, bf16[256,1536]{1,0:T(8,128)(2,1)}, u32[]{:S(2)}, u32[]{:S(2)}) collective-permute-start(bf16[256,1536]{1,0:T(8,128)(2,1)} %tokens.3), channel_id=1, source_target_pairs={{0,1},{1,0},{2,3},{3,2},{4,5},{5,4},{6,7},{7,6},{8,9},{9,8},{10,11... | collective-permute-start | bytes 2359304 | tf_op jit(solution)/shard_map/ppermute | solution.py:56
  31.6 100.6 %all-gather.6.cloned.1.call-start = ((), (), s32[]{:S(2)}) async-start(), calls=%async_computation.9 | async-start | bytes 10616832 | tf_op jit(solution)/shard_map/all_gather | solution.py:115
  31.7 19.3 %collective-permute-start.4 = (bf16[256,1536]{1,0:T(8,128)(2,1)}, bf16[256,1536]{1,0:T(8,128)(2,1)S(1)}, u32[]{:S(2)}, u32[]{:S(2)}) collective-permute-start(bf16[256,1536]{1,0:T(8,128)(2,1)} %collective-permute-done.refs_7_), channel_id=1, source_target_pairs={{0,2},{1,3},{2,4},{3,5},{4,6},{5,7},{6,0},{7,1},{8,10},{9,11},{10,... | collective-permute-start | bytes 2359304 | tf_op jit(solution)/shard_map/ppermute | solution.py:56
  32.1 20.7 %collective-permute-start.5 = (bf16[256,1536]{1,0:T(8,128)(2,1)}, bf16[256,1536]{1,0:T(8,128)(2,1)S(1)}, u32[]{:S(2)}, u32[]{:S(2)}) collective-permute-start(bf16[256,1536]{1,0:T(8,128)(2,1)} %collective-permute-done.refs_7_), channel_id=1, source_target_pairs={{0,1},{1,0},{2,3},{3,2},{4,5},{5,4},{6,7},{7,6},{8,9},{9,8},{10,11... | collective-permute-start | bytes 2359304 | tf_op jit(solution)/shard_map/ppermute | solution.py:56
  33.7 19.1 %collective-permute-start.6 = (bf16[256,1536]{1,0:T(8,128)(2,1)}, bf16[256,1536]{1,0:T(8,128)(2,1)S(1)}, u32[]{:S(2)}, u32[]{:S(2)}) collective-permute-start(bf16[256,1536]{1,0:T(8,128)(2,1)} %collective-permute-done.2.refs_1_), channel_id=1, source_target_pairs={{0,6},{1,7},{2,0},{3,1},{4,2},{5,3},{6,4},{7,5},{8,14},{9,15},{10,... | collective-permute-start | bytes 2359304 | tf_op jit(solution)/shard_map/ppermute | solution.py:56
  38.8 28.0 %collective-permute-start.12 = (bf16[256,1536]{1,0:T(8,128)(2,1)S(1)}, bf16[256,1536]{1,0:T(8,128)(2,1)}, u32[]{:S(2)}, u32[]{:S(2)}) collective-permute-start(bf16[256,1536]{1,0:T(8,128)(2,1)S(1)} %multiply_convert_fusion.refs_0_), channel_id=1, source_target_pairs={{0,1},{1,0},{2,3},{3,2},{4,5},{5,4},{6,7},{7,6},{8,9},{9,8},{10,11... | collective-permute-start | bytes 2359304 | tf_op jit(solution)/shard_map/ppermute | solution.py:56
  66.9 159.5 %all-gather.8.cloned.1.call-start = ((), (), s32[]{:S(2)}) async-start(), calls=%async_computation.11 | async-start | bytes 22118400 | tf_op jit(solution)/shard_map/all_gather | solution.py:115
  67.5 25.2 %collective-permute-start.8 = (bf16[256,1536]{1,0:T(8,128)(2,1)S(1)}, bf16[256,1536]{1,0:T(8,128)(2,1)}, u32[]{:S(2)}, u32[]{:S(2)}) collective-permute-start(bf16[256,1536]{1,0:T(8,128)(2,1)S(1)} %multiply_convert_fusion.refs_0_), channel_id=1, source_target_pairs={{0,2},{1,3},{2,4},{3,5},{4,6},{5,7},{6,0},{7,1},{8,10},{9,11},{10,... | collective-permute-start | bytes 2359304 | tf_op jit(solution)/shard_map/ppermute | solution.py:56
  68.9 23.8 %collective-permute-start.9 = (bf16[256,1536]{1,0:T(8,128)(2,1)S(1)}, bf16[256,1536]{1,0:T(8,128)(2,1)S(1)}, u32[]{:S(2)}, u32[]{:S(2)}) collective-permute-start(bf16[256,1536]{1,0:T(8,128)(2,1)S(1)} %multiply_convert_fusion.refs_0_), channel_id=1, source_target_pairs={{0,6},{1,7},{2,0},{3,1},{4,2},{5,3},{6,4},{7,5},{8,14},{9,15},{10,... | collective-permute-start | bytes 2359304 | tf_op jit(solution)/shard_map/ppermute | solution.py:56
  70.7 56.5 %collective-permute-start.16 = (bf16[96,6400]{1,0:T(8,128)(2,1)S(1)}, bf16[96,6400]{1,0:T(8,128)(2,1)}, u32[]{:S(2)}, u32[]{:S(2)}) collective-permute-start(bf16[96,6400]{1,0:T(8,128)(2,1)S(1)} %convert_element_type.48), channel_id=1, source_target_pairs={{0,65},{1,64},{2,67},{3,66},{4,69},{5,68},{6,71},{7,70},{8,73},{9,... | collective-permute-start | bytes 3686408 | tf_op jit(solution)/shard_map/ppermute | solution.py:56
  92.7 18.1 %collective-permute-start.13 = (bf16[256,1536]{1,0:T(8,128)(2,1)}, bf16[256,1536]{1,0:T(8,128)(2,1)}, u32[]{:S(2)}, u32[]{:S(2)}) collective-permute-start(bf16[256,1536]{1,0:T(8,128)(2,1)} %collective-permute-done.8.refs_7_), channel_id=1, source_target_pairs={{0,2},{1,3},{2,4},{3,5},{4,6},{5,7},{6,0},{7,1},{8,10},{9,11},{10,... | collective-permute-start | bytes 2359304 | tf_op jit(solution)/shard_map/ppermute | solution.py:56
  93.6 17.3 %collective-permute-start.14 = (bf16[256,1536]{1,0:T(8,128)(2,1)}, bf16[256,1536]{1,0:T(8,128)(2,1)S(1)}, u32[]{:S(2)}, u32[]{:S(2)}) collective-permute-start(bf16[256,1536]{1,0:T(8,128)(2,1)} %collective-permute-done.8.refs_7_), channel_id=1, source_target_pairs={{0,1},{1,0},{2,3},{3,2},{4,5},{5,4},{6,7},{7,6},{8,9},{9,8},{10,11... | collective-permute-start | bytes 2359304 | tf_op jit(solution)/shard_map/ppermute | solution.py:56
  93.6 17.3 %collective-permute-start.15 = (bf16[256,1536]{1,0:T(8,128)(2,1)}, bf16[256,1536]{1,0:T(8,128)(2,1)S(1)}, u32[]{:S(2)}, u32[]{:S(2)}) collective-permute-start(bf16[256,1536]{1,0:T(8,128)(2,1)} %collective-permute-done.12.refs_1_), channel_id=1, source_target_pairs={{0,6},{1,7},{2,0},{3,1},{4,2},{5,3},{6,4},{7,5},{8,14},{9,15},{10,... | collective-permute-start | bytes 2359304 | tf_op jit(solution)/shard_map/ppermute | solution.py:56
  167.8 48.0 %all-to-all-start.1 = ((bf16[8,256,768]{2,1,0:T(8,128)(2,1)}), bf16[8,256,768]{2,1,0:T(8,128)(2,1)S(1)}, u32[]{:S(2)}, u32[]{:S(2)}) async-start(bf16[8,256,768]{2,1,0:T(8,128)(2,1)} %bitcast.73), calls=%async_computation.1 | async-start | bytes 6291456 | tf_op jit(solution)/shard_map/all_to_all | solution.py:120
  171.4 105.5 %reduce-scatter.3.cloned.1.call-start = ((), (), s32[]{:S(2)}) async-start(), calls=%async_computation.10 | async-start | bytes 5308416 | tf_op jit(solution)/shard_map/reduce_scatter | solution.py:135
  217.5 29.6 %all-to-all-start.2 = ((f32[8,32,2048]{2,1,0:T(8,128)}), f32[8,32,2048]{2,1,0:T(8,128)S(1)}, u32[]{:S(2)}, u32[]{:S(2)}) async-start(f32[8,32,2048]{2,1,0:T(8,128)} %bitcast.78), calls=%async_computation.3 | async-start | bytes 4194304 | tf_op jit(solution)/shard_map/all_to_all | solution.py:120
  223.6 101.4 %reduce-scatter.5.cloned.1.call-start = ((), (), s32[]{:S(2)}) async-start(), calls=%async_computation.12 | async-start | bytes 3833856 | tf_op jit(solution)/shard_map/reduce_scatter | solution.py:135
  264.1 30.9 %all-to-all-start.3 = ((bf16[8,256,512]{2,1,0:T(8,128)(2,1)}), bf16[8,256,512]{2,1,0:T(8,128)(2,1)S(1)}, u32[]{:S(2)}, u32[]{:S(2)}) async-start(bf16[8,256,512]{2,1,0:T(8,128)(2,1)} %bitcast.74), calls=%async_computation.4 | async-start | bytes 4194304 | tf_op jit(solution)/shard_map/all_to_all | solution.py:120
  310.1 40.9 %all-to-all-start.4 = ((f32[8,192,384]{2,1,0:T(8,128)}), f32[8,192,384]{2,1,0:T(8,128)S(1)}, u32[]{:S(2)}, u32[]{:S(2)}) async-start(f32[8,192,384]{2,1,0:T(8,128)} %broadcast_in_dim.66), calls=%async_computation.6 | async-start | bytes 4718592 | tf_op jit(solution)/shard_map/all_to_all | solution.py:120
  326.1 24.9 %collective-permute-start.26 = (f32[112,512]{1,0:T(8,128)S(1)}, f32[112,512]{1,0:T(8,128)S(1)}, u32[]{:S(2)}, u32[]{:S(2)}) collective-permute-start(f32[112,512]{1,0:T(8,128)S(1)} %pad_maximum_fusion.5), channel_id=1, source_target_pairs={{0,64},{1,65},{2,66},{3,67},{4,68},{5,69},{6,70},{7,71},{8,72},{9,... | collective-permute-start | bytes 688136 | tf_op jit(solution)/shard_map/ppermute | solution.py:56
  353.0 32.0 %all-to-all-start.5 = ((f32[8,112,512]{2,1,0:T(8,128)}), f32[8,112,512]{2,1,0:T(8,128)S(1)}, u32[]{:S(2)}, u32[]{:S(2)}) async-start(f32[8,112,512]{2,1,0:T(8,128)} %broadcast_in_dim.67), calls=%async_computation.7 | async-start | bytes 3670016 | tf_op jit(solution)/shard_map/all_to_all | solution.py:120
  (39 other events, 423.3 us)
Sparse Core Ops, SparseCore 0:
  31.7 33.3 all-gather.3
  67.4 56.2 all-gather.5
  130.5 95.8 all-gather.7
  228.7 39.8 reduce-scatter.2
  270.9 39.4 reduce-scatter.4

commit v2 on v1

--- a/solution.py
+++ b/solution.py
@@ -717,7 +717,7 @@
     )(grad_out, mixed, proj, sums, gain)
 
 
-def early_grad_kernel(low, grad_branch, normed, out):
+def early_grad_kernel(low, grad_x, grad_branch, normed, out):
     step = pl.program_id(0)
 
     @pl.when(step == 0)
@@ -728,19 +728,21 @@
         part = product(low[:, :OWN], grad_branch[:, k * WIDE : (k + 1) * WIDE], 0, 0)
         for m in range(4):
             out[eight_order(4 * k + m), :SHARD_IN] += part[m * SHARD_IN : (m + 1) * SHARD_IN]
-    part = product(normed[...], low[:, OWN:], 0, 0)
+    part = product(normed[...], jnp.concatenate([low[:, OWN:], grad_x[...]], 1), 0, 0)
     for f in range(N_FSDP):
-        out[eight_order(f), SHARD_IN:] += part[f * SHARD_IN : (f + 1) * SHARD_IN]
-
-
-def run_early_grad(low, grad_branch, normed):
+        rows = part[f * SHARD_IN : (f + 1) * SHARD_IN]
+        out[eight_order(f), SHARD_IN : 2 * SHARD_IN] += rows[:, :OWN]
+        out[eight_order(f), 2 * SHARD_IN :] += rows[:, OWN:]
+
+
+def run_early_grad(low, grad_x, grad_branch, normed):
     count = 2 * ROWS
     rows = lambda width: pl.BlockSpec((count, width), lambda i: (i, 0))
-    shape = (N_FSDP, 2 * SHARD_IN, WIDE)
+    shape = (N_FSDP, 3 * SHARD_IN, WIDE)
     return pl.pallas_call(
         early_grad_kernel,
         grid=(PACK // count,),
-        in_specs=[rows(2 * OWN), rows(D), rows(D)],
+        in_specs=[rows(2 * OWN), rows(OWN), rows(D), rows(D)],
         out_specs=pl.BlockSpec(shape, lambda i: (0, 0, 0)),
         out_shape=jax.ShapeDtypeStruct(shape, F32),
         compiler_params=pltpu.CompilerParams(
@@ -748,7 +750,7 @@
         ),
         cost_estimate=COST,
         name="early_grad",
-    )(low, grad_branch, normed)
+    )(low, grad_x, grad_branch, normed)
 
 
 def block_out_kernel(rows, weight, tokens, live, out):
@@ -868,8 +870,8 @@
         unit = values * scale
         gain_sum = jnp.sum(grad_h * unit, 0, keepdims=True)
         gain_out[...] = jnp.zeros_like(gain_out)
-        for k in range(D // TAIL):
-            gain_out[k : k + 1, :] = gain_sum[:, k * TAIL : (k + 1) * TAIL]
+        for k in range(D // N):
+            gain_out[k : k + 1, :] = gain_sum[:, k * N : (k + 1) * N]
         grad_unit = grad_h * gain[...]
         inner = jnp.mean(grad_unit * unit, axis=1, keepdims=True)
         out[...] = cotangent[...].astype(F32) + scale * (grad_unit - unit * inner)
@@ -892,8 +894,8 @@
             fixed((ROWS, D)),
             fixed((1, D)),
         ],
-        out_specs=[fixed((ROWS, D)), fixed((8, TAIL))],
-        out_shape=[jax.ShapeDtypeStruct((ROWS, D), F32), jax.ShapeDtypeStruct((8, TAIL), F32)],
+        out_specs=[fixed((ROWS, D)), fixed((16, N))],
+        out_shape=[jax.ShapeDtypeStruct((ROWS, D), F32), jax.ShapeDtypeStruct((16, N), F32)],
         scratch_shapes=[pltpu.VMEM((D, ROWS), F32), pltpu.VMEM((D, ROWS), F32)],
         compiler_params=pltpu.CompilerParams(
             dimension_semantics=("arbitrary",), vmem_limit_bytes=VMEM_LIMIT
@@ -956,8 +958,9 @@
     wide = jnp.where(row == 6, logs[1:2, :], jnp.where(row == 7, by_head[6:7, :], wide))
     turned = jnp.concatenate([found, filler], 0).T
     first_row = lax.broadcasted_iota(jnp.int32, (8, N), 0) == 0
-    small_out[:, :OWN] = wide
-    small_out[:, OWN:] = jnp.where(first_row, head_acc[0:1, :], pltpu.roll(turned[:8], 1, 0))
+    for k in range(3):
+        small_out[8 * k : 8 * k + 8, :] = wide[:, k * N : (k + 1) * N]
+    small_out[24:, :] = jnp.where(first_row, head_acc[0:1, :], pltpu.roll(turned[:8], 1, 0))
 
 
 def run_rest(ends, parts, pre, proj, par, grad_x, grad_dt, sums, head_acc, grad_gain, first):
@@ -979,8 +982,8 @@
             fixed((8, OWN)),
             pl.BlockSpec(memory_space=pltpu.SMEM),
         ],
-        out_specs=[fixed((PACK, TAIL)), fixed((8, TAIL))],
-        out_shape=[jax.ShapeDtypeStruct((PACK, TAIL), BF16), jax.ShapeDtypeStruct((8, TAIL), F32)],
+        out_specs=[fixed((PACK, TAIL)), fixed((32, N))],
+        out_shape=[jax.ShapeDtypeStruct((PACK, TAIL), BF16), jax.ShapeDtypeStruct((32, N), F32)],
         compiler_params=pltpu.CompilerParams(
             dimension_semantics=("arbitrary",), vmem_limit_bytes=VMEM_LIMIT
         ),
@@ -1007,14 +1010,14 @@
 
 def run_tail_grad(normed, tail, small):
     count = 2 * ROWS
-    shape = (N_FSDP, SHARD_IN + 8, TAIL)
+    shape = (N_FSDP, SHARD_IN + 32, N)
     return pl.pallas_call(
         tail_grad_kernel,
         grid=(PACK // count,),
         in_specs=[
             pl.BlockSpec((count, D), lambda i: (i, 0)),
-            pl.BlockSpec((count, TAIL), lambda i: (i, 0)),
-            pl.BlockSpec((8, TAIL), lambda i: (0, 0)),
+            pl.BlockSpec((count, N), lambda i: (i, OWN // N)),
+            pl.BlockSpec((32, N), lambda i: (0, 0)),
         ],
         out_specs=pl.BlockSpec(shape, lambda i: (0, 0, 0)),
         out_shape=jax.ShapeDtypeStruct(shape, F32),
@@ -1037,77 +1040,64 @@
 
 
 def adam_early_kernel(rows, pair, *refs):
-    arrays, grad = refs[:-1], refs[-1]
+    arrays, grad = refs[:3] + refs[-5:-1], refs[-1]
     grad[:, :WIDE] = pair[0, rows, :]
     grad[:, WIDE:] = pair[1, rows, :]
     adam_step(grad[...], *arrays)
 
 
-def run_adam_early(place_of, rows, parts, weight, first, second):
+def run_adam_early(place_of, rows, parts, weight, first, second, before=()):
     part = pl.BlockSpec((SHARD_IN, 2 * WIDE), place_of)
     shape = jax.ShapeDtypeStruct(weight.shape, F32)
     return pl.pallas_call(
         partial(adam_early_kernel, rows),
         grid=(N_REP // 2,),
-        in_specs=[pl.BlockSpec((2,) + parts.shape[1:], lambda i: (i, 0, 0))] + [part] * 3,
+        in_specs=[pl.BlockSpec((2,) + parts.shape[1:], lambda i: (i, 0, 0))]
+        + [part] * 3
+        + [pl.BlockSpec(memory_space=pl.ANY)] * len(before),
         out_specs=[part] * 4,
         out_shape=[shape] * 4,
+        input_output_aliases={4 + k: k for k in range(len(before))},
         scratch_shapes=[pltpu.VMEM((SHARD_IN, 2 * WIDE), F32)],
         compiler_params=pltpu.CompilerParams(
             dimension_semantics=("arbitrary",), vmem_limit_bytes=VMEM_LIMIT
         ),
         cost_estimate=FILL,
         name="adam",
-    )(parts, weight, first, second)
-
-
-def adam_tail_kernel(pair, rest, *refs):
-    arrays, grad = refs[:3] + refs[-5:-1], refs[-1]
-    step = pl.program_id(0)
-
-    @pl.when(step < N_REP // 2)
-    def _():
-        grad[:, :WIDE] = pair[0, :SHARD_IN]
-        grad[:, WIDE:] = pair[1, :SHARD_IN]
-
-    @pl.when(step == N_REP // 2)
-    def _():
-        lane = lax.broadcasted_iota(jnp.int32, (SHARD_IN, N), 1)
-        for k in range(2):
-            group = jnp.zeros((SHARD_IN, N), F32)
-            for m in range(4):
-                value = rest[4 * k + m, :SHARD_IN]
-                value = value if m == 0 else pltpu.roll(value, m * OWN_BC, 1)
-                group = jnp.where((lane >= m * OWN_BC) & (lane < (m + 1) * OWN_BC), value, group)
-            grad[:, k * N : (k + 1) * N] = group
-
-    adam_step(grad[...], *arrays)
-
-
-def run_adam_tail(parts, weight, first, second, before):
-    half = N_REP // 2
-    rows = parts.shape[1]
-    column = pl.BlockSpec((SHARD_IN, 2 * WIDE), lambda i: (0, half + i))
+    )(parts, weight, first, second, *before)
+
+
+def adam_rest_kernel(parts, weight, first, second, *refs):
+    lane = lax.broadcasted_iota(jnp.int32, (SHARD_IN, N), 1)
+    groups = []
+    for k in range(2):
+        group = jnp.zeros((SHARD_IN, N), F32)
+        for m in range(4):
+            value = parts[4 * k + m, :SHARD_IN]
+            value = value if m == 0 else pltpu.roll(value, m * OWN_BC, 1)
+            group = jnp.where((lane >= m * OWN_BC) & (lane < (m + 1) * OWN_BC), value, group)
+        groups.append(group)
+    adam_step(jnp.concatenate(groups, 1), weight, first, second, *refs[-4:])
+
+
+def run_adam_rest(parts, weight, first, second, before):
+    column = pl.BlockSpec((SHARD_IN, 2 * N), lambda i: (0, DI // N))
     shape = jax.ShapeDtypeStruct(weight.shape, F32)
     return pl.pallas_call(
-        adam_tail_kernel,
-        grid=(half + 1,),
-        in_specs=[
-            pl.BlockSpec((2, rows, OWN), lambda i: (jnp.minimum(i, half - 1), 0, 0)),
-            pl.BlockSpec((N_REP, rows, N), lambda i: (0, 0, OWN // N)),
-        ]
+        adam_rest_kernel,
+        grid=(1,),
+        in_specs=[pl.BlockSpec(parts.shape, lambda i: (0, 0, 0))]
         + [column] * 3
         + [pl.BlockSpec(memory_space=pl.ANY)] * 4,
         out_specs=[column] * 4,
         out_shape=[shape] * 4,
-        input_output_aliases={5 + k: k for k in range(4)},
-        scratch_shapes=[pltpu.VMEM((SHARD_IN, 2 * WIDE), F32)],
+        input_output_aliases={4 + k: k for k in range(4)},
         compiler_params=pltpu.CompilerParams(
             dimension_semantics=("arbitrary",), vmem_limit_bytes=VMEM_LIMIT
         ),
         cost_estimate=COST,
-        name="adam_tail",
-    )(parts, parts, weight, first, second, *before)
+        name="adam_rest",
+    )(parts, weight, first, second, *before)
 
 
 def body(
@@ -1251,7 +1241,7 @@
         seg_ends, proj, pre, mixed, grad_mixed, states, par
     )
     low, grad_x = lax.optimization_barrier((low, grad_x))
-    early_grad = run_early_grad(low, grad_branch, normed)
+    early_grad = run_early_grad(low, grad_x, grad_branch, normed)
     low_rows, early_grad, grad_bc, grad_x = lax.optimization_barrier((low_rows, early_grad, grad_bc, grad_x))
 
     grad_bc = exchange(grad_bc, "rep").reshape(N_REP, OWN_BC, PACK)
@@ -1263,11 +1253,10 @@
         seg_ends, grad_bc, pre, proj, par, grad_x, grad_dtraw, grad_sums, grad_heads, grad_gain, (r * OWN_BC)[None]
     )
     grad_tail = run_tail_grad(normed, tail, small_own)
-    tail, grad_tail, low_rows = lax.optimization_barrier((tail, grad_tail, low_rows))
+    tail, grad_tail = lax.optimization_barrier((tail, grad_tail))
     tail_rows = exchange(tail.reshape(N_REP, ROWS, TAIL), "rep")
+    early, grad_tail = lax.optimization_barrier((early, grad_tail))
     tail_part = scatter_eight(grad_tail)
-    block_out = run_block_out(low_rows, full_out, tokens, own_live)
-    early, block_out = lax.optimization_barrier((early, block_out))
     mine, other = at(early, place.yh), at(early, 1 - place.yh)
     out_mine = move(
         mine[:SHARD_IN], lambda yh, z, c, x, yl: (x // 2, (x % 2) * 2 + yl, z % 2, 2 * c + yh, z // 2)
@@ -1275,23 +1264,22 @@
     out_other = move(
         other[:SHARD_IN], lambda yh, z, c, x, yl: (x // 2, (x % 2) * 2 + yl, z % 2, 2 * c + 1 - yh, z // 2)
     )
-    z_other = move(other[SHARD_IN:], swap_y_hi)
-    tail_rows, out_mine, out_other, z_other = lax.optimization_barrier((tail_rows, out_mine, out_other, z_other))
-
+    in_other = move(other[SHARD_IN:], swap_y_hi)
+    tail_rows, out_mine, out_other, in_other = lax.optimization_barrier((tail_rows, out_mine, out_other, in_other))
+
+    early_parts = share_rep(jnp.concatenate([out_mine + out_other, mine[SHARD_IN:] + in_other], 0))
     input_grad, grad_gain_in = run_input_grad(
         place.yh[None], grad_rows, tail_rows, full_in, low_dt, tokens, cotangent, gain_in
     )
-    early = jnp.concatenate([out_mine + out_other, mine[SHARD_IN:] + z_other], 0)
-    early, grad_gain_in = lax.optimization_barrier((early, grad_gain_in))
-
-    early_parts = share_rep(early)
+
     grad_gain_in = sum_z(grad_gain_in + move(grad_gain_in, swap_core))
     tail_part, grad_gain_in = lax.optimization_barrier((tail_part, grad_gain_in))
     tail_other = move(with_rows(at(tail_part, 1 - place.yh), grad_gain_in), swap_y_hi)
     tail_part = with_rows(at(tail_part, place.yh), grad_gain_in) + tail_other
 
-    tail_part, early_parts = lax.optimization_barrier((tail_part, early_parts))
+    tail_part, early_parts, low_rows = lax.optimization_barrier((tail_part, early_parts, low_rows))
     tail_parts = share_rep(tail_part)
+    block_out = run_block_out(low_rows, full_out, tokens, own_live)
 
     grad_out, new_first_out, new_second_out, new_out = run_adam_early(
         lambda i: (i // 2, i % 2), slice(0, SHARD_IN), early_parts, w_out, first_out, second_out
@@ -1299,15 +1287,18 @@
     updated = run_adam_early(
         lambda i: (0, i), slice(SHARD_IN, 2 * SHARD_IN), early_parts, w_in, first_in, second_in
     )
-    grad_in, new_first_in, new_second_in, new_in = run_adam_tail(tail_parts, w_in, first_in, second_in, updated)
+    updated = run_adam_early(
+        lambda i: (0, 4 + i), slice(2 * SHARD_IN, 3 * SHARD_IN), early_parts, w_in, first_in, second_in, updated
+    )
+    grad_in, new_first_in, new_second_in, new_in = run_adam_rest(tail_parts, w_in, first_in, second_in, updated)
 
     def columns(parts):
         return parts.transpose(1, 0, 2).reshape(parts.shape[1], -1)
 
-    small_parts = tail_parts[:, SHARD_IN : SHARD_IN + 8]
-    grad_gain_in = tail_parts[:, SHARD_IN + 8 : SHARD_IN + 8 + D // TAIL].sum(0).reshape(-1)
-    small_x = small_parts[:, :, :OWN].transpose(1, 0, 2).reshape(8, DI)
-    small_bc = small_parts[:, :, OWN:].transpose(1, 0, 2)
+    grad_gain_in = tail_parts[:, SHARD_IN + 32 : SHARD_IN + 32 + D // N].sum(0).reshape(-1)
+    small_parts = tail_parts[:, SHARD_IN : SHARD_IN + 32].reshape(N_REP, 4, 8, N)
+    small_x = small_parts[:, :3].transpose(2, 0, 1, 3).reshape(8, DI)
+    small_bc = small_parts[:, 3].transpose(1, 0, 2)
 
     def channels(row):
         return jnp.concatenate([small_x[row], small_bc[row, :, :OWN_BC].reshape(-1)])
@@ -1317,12 +1308,12 @@
         + [channels(row) for row in range(1, 6)]
         + [
             small_bc[0, :, :OWN_H].reshape(-1),
-            small_parts[:, 6, :OWN_H].reshape(-1),
-            small_parts[:, 7, :OWN_H].reshape(-1),
+            small_parts[:, 0, 6, :OWN_H].reshape(-1),
+            small_parts[:, 0, 7, :OWN_H].reshape(-1),
         ]
     )
     grad_small = lax.dynamic_slice_in_dim(grad_small_all, place.f * SHARD_SMALL, SHARD_SMALL, 0)
-    grad_dt = columns(tail_parts[:, :SHARD_IN, OWN + OWN_BC : OWN + OWN_BC + OWN_H])
+    grad_dt = columns(tail_parts[:, :SHARD_IN, OWN_BC : OWN_BC + OWN_H])
     new_dt, new_first_dt, new_second_dt = adam_update(
         w_dt, grad_dt, first_dt, second_dt, RATE_MATRIX, WEIGHT_DECAY
     )

time: 403 us -> 408 us (1.012)
  waiting for transfers between devices: 99.1 us -> 92.4 us
  other arithmetic: 15.6 us -> 21.2 us
    reduce_scatter x2, waiting for transfers between devices: 0.01 us -> 23.5 us  [scatter_eight(): lax.psum_scatter(flat, 'fsdp', scatter_dimension=0, tiled=True, axis_inde...]
    ppermute x27, waiting for transfers between devices: 67.2 us -> 48.2 us  [move(): return lax.ppermute(value, ('fsdp', 'rep'), pairs)]
    all_to_all x5, waiting for transfers between devices: 28.9 us -> 19.6 us  [exchange(): return lax.all_to_all(value, axis, 0, 0, tiled=True)]
    pallas_call x2 -> x3, Pallas kernels: 11.1 us -> 17.6 us  [run_adam_early(): pl.pallas_call(partial(adam_early_kernel, rows), grid=(N_REP // 2,), in_s...]
    pallas_call x1, Pallas kernels: 6.87 us -> 2.09 us  [run_adam_rest(): pl.pallas_call(adam_rest_kernel, grid=(1,), in_specs=[pl.BlockSpec(parts....]
  transfers between devices with their start and end apart: 37 -> 37, of which waited for: 19 -> 19; matrix products, arithmetic and copies ran while one was open for 6% -> 7% of each run, Pallas kernels for 41% -> 42%
where the time goes in v2:
time: 408 us; the launch traced here: 405 us
  Pallas kernels  172 us (42%)
  waiting for transfers between devices  92.4 us (23%)
  starting transfers between devices  69.2 us (17%)
  local copies, waits for them, and re-layouts  25.4 us (6%)
  other arithmetic  21.2 us (5%)
  between operations  14.5 us (4%)
  blocking collectives  10.2 us (2%)
    ppermute x27, waiting for transfers between devices, move(): return lax.ppermute(value, ('fsdp', 'rep'), pairs)  48.2 us
    ppermute x27, starting transfers between devices, move(): return lax.ppermute(value, ('fsdp', 'rep'), pairs)  43.6 us
    pallas_call x1, Pallas kernels, run_backward(): pl.pallas_call(backward_kernel, grid=(CHUNKS,), in_specs=[pl.BlockSpec(me...  32.1 us
    all_to_all x5, starting transfers between devices, exchange(): return lax.all_to_all(value, axis, 0, 0, tiled=True)  25.3 us
    pallas_call x2, Pallas kernels, run_forward(): pl.pallas_call(partial(forward_kernel, part), grid=(HALF,), in_specs=[pl....  24.4 us
    reduce_scatter x2, waiting for transfers between devices, scatter_eight(): lax.psum_scatter(flat, 'fsdp', scatter_dimension=0, tiled=True, axis_inde...  23.5 us
    all_to_all x5, waiting for transfers between devices, exchange(): return lax.all_to_all(value, axis, 0, 0, tiled=True)  19.6 us
    pallas_call x3, Pallas kernels, run_adam_early(): pl.pallas_call(partial(adam_early_kernel, rows), grid=(N_REP // 2,), in_s...  17.6 us
  transfers between devices with their start and end apart: 37, of which 19 were waited for; matrix products, arithmetic and copies ran while one was open for 7% of the time, Pallas kernels for 42%

profile of v2, /device:TPU:0, one launch (start us, length us, event | category | flops | bytes accessed | tf_op | source)
XLA Modules:
  0.0 404.8 jit_solution(12119744031106355837)
XLA Ops:
  39.5 11.1 %collective-permute-done.7 = bf16[192,1536]{1,0:T(8,128)(2,1)S(1)} collective-permute-done((bf16[192,1536]{1,0:T(8,128)(2,1)S(1)}, bf16[192,1536]{1,0:T(8,128)(2,1)S(1)}, u32[]{:S(2)}, u32[]{:S(2)}) %collective-permute-start.7) | collective-permute-done | bytes 589856 | tf_op jit(solution)/shard_map/ppermute | solution.py:56
  58.9 8.0 %collective-permute-done.12.refs_1_ = bf16[256,1536]{1,0:T(8,128)(2,1)} collective-permute-done((bf16[256,1536]{1,0:T(8,128)(2,1)S(1)}, bf16[256,1536]{1,0:T(8,128)(2,1)}, u32[]{:S(2)}, u32[]{:S(2)}) %collective-permute-start.12) | collective-permute-done | bytes 786464 | tf_op jit(solution)/shard_map/ppermute | solution.py:56
  75.5 17.2 %project.1 = (bf16[2048,1536]{1,0:T(8,128)(2,1)}, f32[2048,1152]{1,0:T(8,128)}, bf16[1536,128]{1,0:T(8,128)(2,1)}) custom-call(s32[8]{0:T(128)} %fusion.6.table, bf16[256,1536]{1,0:T(8,128)(2,1)} %tokens.3, bf16[256,1536]{1,0:T(8,128)(2,1)} %collective-permute-done.2.refs_1_, bf16[256,1536]{1,0:T(8,128)(2,1)} %collective-permute-done.1.refs_2_, ...), custom_call_target="tpu_custom_call" | custom-call | flops 1000000 | bytes 100000 | tf_op jit(solution)/shard_map/project/pallas_call | solution.py:584
  97.8 12.2 %scan_forward.2 = (f32[2048,640]{1,0:T(8,128)}, f32[2048,384]{1,0:T(8,128)}, f32[2048,384]{1,0:T(8,128)}, f32[136,640]{1,0:T(8,128)}) custom-call(s32[3]{0:T(128)} %bitcast.113, f32[2048,1152]{1,0:T(8,128)} %get-tuple-element.133.proj.refs_11_.gate_in.conv_in.dt_in, f32[16,640]{1,0:T(8,128)} %concatenate.42.par), custom_call_target="tpu_custom_call" | custom-call | flops 1000000 | bytes 100000 | tf_op jit(solution)/shard_map/scan_forward/pallas_call | solution.py:355
  115.0 12.2 %scan_forward.3 = (f32[2048,640]{1,0:T(8,128)}, f32[2048,384]{1,0:T(8,128)}, f32[2048,384]{1,0:T(8,128)}, f32[136,640]{1,0:T(8,128)}) custom-call(s32[3]{0:T(128)} %bitcast.114, f32[2048,1152]{1,0:T(8,128)} %get-tuple-element.133.proj.refs_11_.gate_in.conv_in.dt_in, ...), custom_call_target="tpu_custom_call", output_to_operand_aliasing={{0}: (3, {}), {1}: (4, {}), {2}: (5, {})} | custom-call | flops 1000000 | bytes 100000 | tf_op jit(solution)/shard_map/scan_forward/pallas_call | solution.py:355
  132.2 13.6 %out_grad.1 = (bf16[2048,1536]{1,0:T(8,128)(2,1)}, f32[2048,384]{1,0:T(8,128)}, f32[8,2048]{1,0:T(8,128)}) custom-call(s32[9]{0:T(128)} %pad_add_fusion.table, bf16[256,1536]{1,0:T(8,128)(2,1)} %copy-done.6, bf16[256,1536]{1,0:T(8,128)(2,1)} %collective-permute-done.12.refs_1_, bf16[256,1536]{1,0:T(8,128)(2,1)} %copy-done.12, bf16[256,1536]{1,0:T(8,128)(2,1)} %copy-done.9, ...), custom_call_target="tpu_custom_call" | custom-call | flops 1000000 | bytes 100000 | tf_op jit(solution)/shard_map/out_grad/pallas_call | solution.py:641
  146.7 10.2 %all_to_all.34 = f32[8,32,128]{2,1,0:T(8,128)S(1)} all-to-all(f32[8,32,128]{2,1,0:T(8,128)S(1)} %broadcast_in_dim.62), channel_id=1, replica_groups=mesh['fsdp'=16,'rep'=8] {'rep'}, dimensions={0} | all-to-all | bytes 262144 | tf_op jit(solution)/shard_map/all_to_all | solution.py:120
  157.6 10.1 %gate_backward.1 = (bf16[2048,768]{1,0:T(8,128)(2,1)}, f32[2048,384]{1,0:T(8,128)}, f32[8,384]{1,0:T(8,128)}) custom-call(f32[2048,384]{1,0:T(8,128)} %get-tuple-element.152.grad_out, f32[2048,384]{1,0:T(8,128)} %get-tuple-element.151.refs_10_.mixed_in, f32[2048,1152]{1,0:T(8,128)} %get-tuple-element.133.proj.refs_11_.gate_in.conv_in.dt_in, ...), custom_call_target="tpu_custom_call" | custom-call | flops 1000000 | bytes 100000 | tf_op jit(solution)/shard_map/gate_backward/pallas_call | solution.py:696
  171.4 32.1 %scan_backward.1 = (bf16[2048,384]{1,0:T(8,128)(2,1)}, bf16[2048,128]{1,0:T(8,128)(2,1)}, f32[256,2048]{1,0:T(8,128)}, f32[8,384]{1,0:T(8,128)}, f32[8,128]{1,0:T(8,128)}) custom-call(s32[3]{0:T(128)} %bitcast.115, f32[2048,1152]{1,0:T(8,128)} %get-tuple-element.133.proj.refs_11_.gate_in.conv_in.dt_in, ...), custom_call_target="tpu_custom_call" | custom-call | flops 1000000 | bytes 100000 | tf_op jit(solution)/shard_map/scan_backward/pallas_call | solution.py:483
  203.5 14.8 %early_grad.1 = f32[16,288,384]{2,1,0:T(8,128)} custom-call(bf16[2048,768]{1,0:T(8,128)(2,1)} %get-tuple-element.159.low, bf16[2048,384]{1,0:T(8,128)(2,1)} %get-tuple-element.170.grad_x, bf16[2048,1536]{1,0:T(8,128)(2,1)} %get-tuple-element.161.grad_branch, bf16[2048,1536]{1,0:T(8,128)(2,1)} %get-tuple-element.162.normed), custom_call_target="tpu_custom_call" | custom-call | flops 1000000 | bytes 100000 | tf_op jit(solution)/shard_map/early_grad/pallas_call | solution.py:742
  219.9 6.0 %all-to-all-start.2 = ((f32[8,32,2048]{2,1,0:T(8,128)}), f32[8,32,2048]{2,1,0:T(8,128)S(1)}, u32[]{:S(2)}, u32[]{:S(2)}) async-start(f32[8,32,2048]{2,1,0:T(8,128)} %bitcast.94), calls=%async_computation.3 | async-start | bytes 4194304 | tf_op jit(solution)/shard_map/all_to_all | solution.py:120
  226.4 7.8 %z_grad.1.grad_z = f32[1536,256]{1,0:T(8,128)} custom-call(bf16[8,256,768]{2,1,0:T(8,128)(2,1)} %copy-done.3, bf16[4,2,2,96,6400]{4,3,2,1,0:T(8,128)(2,1)} %bitcast.82), custom_call_target="tpu_custom_call" | custom-call | flops 2400000000 | bytes 20000000 | tf_op jit(solution)/shard_map/z_grad/pallas_call | solution.py:815
  234.2 14.9 %all-to-all-done.2.parts = f32[8,32,2048]{2,1,0:T(8,128)S(1)} async-done(((f32[8,32,2048]{2,1,0:T(8,128)}), f32[8,32,2048]{2,1,0:T(8,128)S(1)}, u32[]{:S(2)}, u32[]{:S(2)}) %all-to-all-start.2) | async-done | bytes 2097184 | tf_op jit(solution)/shard_map/all_to_all | solution.py:120
  250.4 6.9 %rest_backward.1 = (bf16[2048,512]{1,0:T(8,128)(2,1)}, f32[32,128]{1,0:T(8,128)}) custom-call(s32[3]{0:T(128)} %bitcast.116, f32[8,32,2048]{2,1,0:T(8,128)} %copy-done.5, f32[2048,640]{1,0:T(8,128)} %get-tuple-element.155.pre_in.pre_b.pre_c, f32[2048,640]{1,0:T(8,128)} %get-tuple-element.155.pre_in.pre_b.pre_c, ...), custom_call_target="tpu_custom_call" | custom-call | flops 1000000 | bytes 100000 | tf_op jit(solution)/shard_map/rest_backward/pallas_call | solution.py:968
  257.3 6.3 %tail_grad.1 = f32[16,128,128]{2,1,0:T(8,128)} custom-call(bf16[2048,1536]{1,0:T(8,128)(2,1)} %get-tuple-element.162.normed, bf16[2048,512]{1,0:T(8,128)(2,1)} %get-tuple-element.180.tail, f32[32,128]{1,0:T(8,128)} %get-tuple-element.176.small), custom_call_target="tpu_custom_call" | custom-call | flops 1000000 | bytes 100000 | tf_op jit(solution)/shard_map/tail_grad/pallas_call | solution.py:1014
  267.3 8.5 %reduce-scatter.3.cloned.1.call-done = f32[576,384]{1,0:T(8,128)} async-done(((f32[4608,384]{1,0:T(8,128)}), f32[576,384]{1,0:T(8,128)}) %reduce-scatter.3.cloned.1.call-update) | async-done | bytes 884752 | tf_op jit(solution)/shard_map/reduce_scatter | solution.py:135
  285.2 11.7 %collective-permute-done.20 = f32[96,384]{1,0:T(8,128)S(1)} collective-permute-done((f32[96,384]{1,0:T(8,128)S(1)}, f32[96,384]{1,0:T(8,128)S(1)}, u32[]{:S(2)}, u32[]{:S(2)}) %collective-permute-start.20) | collective-permute-done | bytes 147488 | tf_op jit(solution)/shard_map/ppermute | solution.py:56
  300.1 7.9 %all-to-all-start.4 = ((f32[8,288,384]{2,1,0:T(8,128)}), f32[8,288,384]{2,1,0:T(8,128)S(1)}, u32[]{:S(2)}, u32[]{:S(2)}) async-start(f32[8,288,384]{2,1,0:T(8,128)} %broadcast_in_dim.65), calls=%async_computation.6 | async-start | bytes 7077888 | tf_op jit(solution)/shard_map/all_to_all | solution.py:120
  308.6 11.2 %input_grad.1 = (f32[256,1536]{1,0:T(8,128)}, f32[16,128]{1,0:T(8,128)}) custom-call(s32[1]{0:T(128)} %bitcast.22.own_half, f32[1536,256]{1,0:T(8,128)} %z_grad.1.grad_z, bf16[8,256,512]{2,1,0:T(8,128)(2,1)} %copy-done.4, bf16[8,256,512]{2,1,0:T(8,128)(2,1)} %copy-done.4, bf16[4,2,2,96,6400]{4,3,2,1,0:T(8,128)(2,1)} %bitcast.83, ...), custom_call_target="tpu_custom_call" | custom-call | flops 1000000 | bytes 100000 | tf_op jit(solution)/shard_map/input_grad/pallas_call | solution.py:882
  328.8 15.0 %reduce-scatter.5.cloned.1.call-done = f32[256,128]{1,0:T(8,128)} async-done(((f32[2048,128]{1,0:T(8,128)}), f32[256,128]{1,0:T(8,128)}) %reduce-scatter.5.cloned.1.call-update) | async-done | bytes 131088 | tf_op jit(solution)/shard_map/reduce_scatter | solution.py:135
  365.1 8.2 %block_out.1 = f32[256,1536]{1,0:T(8,128)} custom-call(bf16[8,256,768]{2,1,0:T(8,128)(2,1)} %copy-done.3, bf16[4,2,2,192,1536]{4,3,2,1,0:T(8,128)(2,1)} %bitcast.86, bf16[256,1536]{1,0:T(8,128)(2,1)} %tokens.3, f32[256,1]{1,0:T(8,128)} %fusion.1.live), custom_call_target="tpu_custom_call" | custom-call | flops 2400000000 | bytes 20000000 | tf_op jit(solution)/shard_map/block_out/pallas_call | solution.py:775
  373.2 6.0 %adam.3 = (f32[96,6400]{1,0:T(8,128)}, f32[96,6400]{1,0:T(8,128)}, f32[96,6400]{1,0:T(8,128)}, f32[96,6400]{1,0:T(8,128)}) custom-call(f32[8,288,384]{2,1,0:T(8,128)} %copy-done.2, f32[96,6400]{1,0:T(8,128)} %weight.1, f32[96,6400]{1,0:T(8,128)} %first.1, f32[96,6400]{1,0:T(8,128)} %second.1), custom_call_target="tpu_custom_call" | custom-call | flops 2400000000 | bytes 20000000 | tf_op jit(solution)/shard_map/adam/pallas_call | solution.py:1052
  379.2 5.6 %adam.5 = (f32[192,1536]{1,0:T(8,128)}, f32[192,1536]{1,0:T(8,128)}, f32[192,1536]{1,0:T(8,128)}, f32[192,1536]{1,0:T(8,128)}) custom-call(f32[8,288,384]{2,1,0:T(8,128)} %copy-done.2, f32[192,1536]{1,0:T(8,128)} %refs_0_.7, f32[192,1536]{1,0:T(8,128)} %refs_1_.5, f32[192,1536]{1,0:T(8,128)} %refs_2_.5), custom_call_target="tpu_custom_call" | custom-call | flops 2400000000 | bytes 20000000 | tf_op jit(solution)/shard_map/adam/pallas_call | solution.py:1052
  384.8 6.0 %adam.4 = (f32[96,6400]{1,0:T(8,128)}, f32[96,6400]{1,0:T(8,128)}, f32[96,6400]{1,0:T(8,128)}, f32[96,6400]{1,0:T(8,128)}) custom-call(f32[8,288,384]{2,1,0:T(8,128)} %copy-done.2, f32[96,6400]{1,0:T(8,128)} %weight.1, f32[96,6400]{1,0:T(8,128)} %first.1, ...), custom_call_target="tpu_custom_call", output_to_operand_aliasing={{0}: (4, {}), {1}: (5, {}), {2}: (6, {}), {3}: (7, {})} | custom-call | flops 2400000000 | bytes 20000000 | tf_op jit(solution)/shard_map/adam/pallas_call | solution.py:1052
  (225 shorter events, 127.2 us)
Async XLA Ops:
  7.2 59.6 %all-gather.4.cloned.1.call-start = ((), (), s32[]{:S(2)}) async-start(), calls=%async_computation.8 | async-start | bytes 4644864 | tf_op jit(solution)/shard_map/all_gather | solution.py:115
  7.3 20.8 %collective-permute-start = (bf16[256,1536]{1,0:T(8,128)(2,1)}, bf16[256,1536]{1,0:T(8,128)(2,1)}, u32[]{:S(2)}, u32[]{:S(2)}) collective-permute-start(bf16[256,1536]{1,0:T(8,128)(2,1)} %tokens.3), channel_id=1, source_target_pairs={{0,2},{1,3},{2,4},{3,5},{4,6},{5,7},{6,0},{7,1},{8,10},{9,11},{10,... | collective-permute-start | bytes 2359304 | tf_op jit(solution)/shard_map/ppermute | solution.py:56
  8.9 19.3 %collective-permute-start.1 = (bf16[256,1536]{1,0:T(8,128)(2,1)}, bf16[256,1536]{1,0:T(8,128)(2,1)}, u32[]{:S(2)}, u32[]{:S(2)}) collective-permute-start(bf16[256,1536]{1,0:T(8,128)(2,1)} %tokens.3), channel_id=1, source_target_pairs={{0,6},{1,7},{2,0},{3,1},{4,2},{5,3},{6,4},{7,5},{8,14},{9,15},{10,... | collective-permute-start | bytes 2359304 | tf_op jit(solution)/shard_map/ppermute | solution.py:56
  10.6 19.0 %collective-permute-start.2 = (bf16[256,1536]{1,0:T(8,128)(2,1)}, bf16[256,1536]{1,0:T(8,128)(2,1)}, u32[]{:S(2)}, u32[]{:S(2)}) collective-permute-start(bf16[256,1536]{1,0:T(8,128)(2,1)} %tokens.3), channel_id=1, source_target_pairs={{0,1},{1,0},{2,3},{3,2},{4,5},{5,4},{6,7},{7,6},{8,9},{9,8},{10,11... | collective-permute-start | bytes 2359304 | tf_op jit(solution)/shard_map/ppermute | solution.py:56
  31.6 100.6 %all-gather.6.cloned.1.call-start = ((), (), s32[]{:S(2)}) async-start(), calls=%async_computation.9 | async-start | bytes 10616832 | tf_op jit(solution)/shard_map/all_gather | solution.py:115
  31.7 19.3 %collective-permute-start.4 = (bf16[256,1536]{1,0:T(8,128)(2,1)}, bf16[256,1536]{1,0:T(8,128)(2,1)S(1)}, u32[]{:S(2)}, u32[]{:S(2)}) collective-permute-start(bf16[256,1536]{1,0:T(8,128)(2,1)} %collective-permute-done.refs_7_), channel_id=1, source_target_pairs={{0,2},{1,3},{2,4},{3,5},{4,6},{5,7},{6,0},{7,1},{8,10},{9,11},{10,... | collective-permute-start | bytes 2359304 | tf_op jit(solution)/shard_map/ppermute | solution.py:56
  32.1 20.7 %collective-permute-start.5 = (bf16[256,1536]{1,0:T(8,128)(2,1)}, bf16[256,1536]{1,0:T(8,128)(2,1)S(1)}, u32[]{:S(2)}, u32[]{:S(2)}) collective-permute-start(bf16[256,1536]{1,0:T(8,128)(2,1)} %collective-permute-done.refs_7_), channel_id=1, source_target_pairs={{0,1},{1,0},{2,3},{3,2},{4,5},{5,4},{6,7},{7,6},{8,9},{9,8},{10,11... | collective-permute-start | bytes 2359304 | tf_op jit(solution)/shard_map/ppermute | solution.py:56
  33.7 19.1 %collective-permute-start.6 = (bf16[256,1536]{1,0:T(8,128)(2,1)}, bf16[256,1536]{1,0:T(8,128)(2,1)S(1)}, u32[]{:S(2)}, u32[]{:S(2)}) collective-permute-start(bf16[256,1536]{1,0:T(8,128)(2,1)} %collective-permute-done.2.refs_1_), channel_id=1, source_target_pairs={{0,6},{1,7},{2,0},{3,1},{4,2},{5,3},{6,4},{7,5},{8,14},{9,15},{10,... | collective-permute-start | bytes 2359304 | tf_op jit(solution)/shard_map/ppermute | solution.py:56
  38.8 28.0 %collective-permute-start.12 = (bf16[256,1536]{1,0:T(8,128)(2,1)S(1)}, bf16[256,1536]{1,0:T(8,128)(2,1)}, u32[]{:S(2)}, u32[]{:S(2)}) collective-permute-start(bf16[256,1536]{1,0:T(8,128)(2,1)S(1)} %multiply_convert_fusion.refs_0_), channel_id=1, source_target_pairs={{0,1},{1,0},{2,3},{3,2},{4,5},{5,4},{6,7},{7,6},{8,9},{9,8},{10,11... | collective-permute-start | bytes 2359304 | tf_op jit(solution)/shard_map/ppermute | solution.py:56
  66.9 159.5 %all-gather.8.cloned.1.call-start = ((), (), s32[]{:S(2)}) async-start(), calls=%async_computation.11 | async-start | bytes 22118400 | tf_op jit(solution)/shard_map/all_gather | solution.py:115
  67.5 25.3 %collective-permute-start.8 = (bf16[256,1536]{1,0:T(8,128)(2,1)S(1)}, bf16[256,1536]{1,0:T(8,128)(2,1)}, u32[]{:S(2)}, u32[]{:S(2)}) collective-permute-start(bf16[256,1536]{1,0:T(8,128)(2,1)S(1)} %multiply_convert_fusion.refs_0_), channel_id=1, source_target_pairs={{0,2},{1,3},{2,4},{3,5},{4,6},{5,7},{6,0},{7,1},{8,10},{9,11},{10,... | collective-permute-start | bytes 2359304 | tf_op jit(solution)/shard_map/ppermute | solution.py:56
  68.9 23.8 %collective-permute-start.9 = (bf16[256,1536]{1,0:T(8,128)(2,1)S(1)}, bf16[256,1536]{1,0:T(8,128)(2,1)S(1)}, u32[]{:S(2)}, u32[]{:S(2)}) collective-permute-start(bf16[256,1536]{1,0:T(8,128)(2,1)S(1)} %multiply_convert_fusion.refs_0_), channel_id=1, source_target_pairs={{0,6},{1,7},{2,0},{3,1},{4,2},{5,3},{6,4},{7,5},{8,14},{9,15},{10,... | collective-permute-start | bytes 2359304 | tf_op jit(solution)/shard_map/ppermute | solution.py:56
  70.7 56.5 %collective-permute-start.16 = (bf16[96,6400]{1,0:T(8,128)(2,1)S(1)}, bf16[96,6400]{1,0:T(8,128)(2,1)}, u32[]{:S(2)}, u32[]{:S(2)}) collective-permute-start(bf16[96,6400]{1,0:T(8,128)(2,1)S(1)} %convert_element_type.48), channel_id=1, source_target_pairs={{0,65},{1,64},{2,67},{3,66},{4,69},{5,68},{6,71},{7,70},{8,73},{9,... | collective-permute-start | bytes 3686408 | tf_op jit(solution)/shard_map/ppermute | solution.py:56
  92.7 18.1 %collective-permute-start.13 = (bf16[256,1536]{1,0:T(8,128)(2,1)}, bf16[256,1536]{1,0:T(8,128)(2,1)}, u32[]{:S(2)}, u32[]{:S(2)}) collective-permute-start(bf16[256,1536]{1,0:T(8,128)(2,1)} %collective-permute-done.8.refs_7_), channel_id=1, source_target_pairs={{0,2},{1,3},{2,4},{3,5},{4,6},{5,7},{6,0},{7,1},{8,10},{9,11},{10,... | collective-permute-start | bytes 2359304 | tf_op jit(solution)/shard_map/ppermute | solution.py:56
  93.6 17.2 %collective-permute-start.14 = (bf16[256,1536]{1,0:T(8,128)(2,1)}, bf16[256,1536]{1,0:T(8,128)(2,1)S(1)}, u32[]{:S(2)}, u32[]{:S(2)}) collective-permute-start(bf16[256,1536]{1,0:T(8,128)(2,1)} %collective-permute-done.8.refs_7_), channel_id=1, source_target_pairs={{0,1},{1,0},{2,3},{3,2},{4,5},{5,4},{6,7},{7,6},{8,9},{9,8},{10,11... | collective-permute-start | bytes 2359304 | tf_op jit(solution)/shard_map/ppermute | solution.py:56
  93.6 17.2 %collective-permute-start.15 = (bf16[256,1536]{1,0:T(8,128)(2,1)}, bf16[256,1536]{1,0:T(8,128)(2,1)S(1)}, u32[]{:S(2)}, u32[]{:S(2)}) collective-permute-start(bf16[256,1536]{1,0:T(8,128)(2,1)} %collective-permute-done.12.refs_1_), channel_id=1, source_target_pairs={{0,6},{1,7},{2,0},{3,1},{4,2},{5,3},{6,4},{7,5},{8,14},{9,15},{10,... | collective-permute-start | bytes 2359304 | tf_op jit(solution)/shard_map/ppermute | solution.py:56
  167.7 50.6 %all-to-all-start.1 = ((bf16[8,256,768]{2,1,0:T(8,128)(2,1)}), bf16[8,256,768]{2,1,0:T(8,128)(2,1)S(1)}, u32[]{:S(2)}, u32[]{:S(2)}) async-start(bf16[8,256,768]{2,1,0:T(8,128)(2,1)} %bitcast.88), calls=%async_computation.1 | async-start | bytes 6291456 | tf_op jit(solution)/shard_map/all_to_all | solution.py:120
  171.4 104.4 %reduce-scatter.3.cloned.1.call-start = ((), (), s32[]{:S(2)}) async-start(), calls=%async_computation.10 | async-start | bytes 7962624 | tf_op jit(solution)/shard_map/reduce_scatter | solution.py:135
  219.9 29.2 %all-to-all-start.2 = ((f32[8,32,2048]{2,1,0:T(8,128)}), f32[8,32,2048]{2,1,0:T(8,128)S(1)}, u32[]{:S(2)}, u32[]{:S(2)}) async-start(f32[8,32,2048]{2,1,0:T(8,128)} %bitcast.94), calls=%async_computation.3 | async-start | bytes 4194304 | tf_op jit(solution)/shard_map/all_to_all | solution.py:120
  263.6 33.2 %all-to-all-start.3 = ((bf16[8,256,512]{2,1,0:T(8,128)(2,1)}), bf16[8,256,512]{2,1,0:T(8,128)(2,1)S(1)}, u32[]{:S(2)}, u32[]{:S(2)}) async-start(bf16[8,256,512]{2,1,0:T(8,128)(2,1)} %bitcast.89), calls=%async_computation.5 | async-start | bytes 4194304 | tf_op jit(solution)/shard_map/all_to_all | solution.py:120
  276.7 20.1 %collective-permute-start.21 = (f32[192,384]{1,0:T(8,128)S(1)}, f32[192,384]{1,0:T(8,128)S(1)}, u32[]{:S(2)}, u32[]{:S(2)}) collective-permute-start(f32[192,384]{1,0:T(8,128)S(1)} %dynamic-slice_bitcast_fusion.1), channel_id=1, source_target_pairs={{0,64},{1,65},{2,66},{3,67},{4,68},{5,69},{6,70},{7,71},{8,72},{9,... | collective-permute-start | bytes 884744 | tf_op jit(solution)/shard_map/ppermute | solution.py:56
  300.1 58.8 %all-to-all-start.4 = ((f32[8,288,384]{2,1,0:T(8,128)}), f32[8,288,384]{2,1,0:T(8,128)S(1)}, u32[]{:S(2)}, u32[]{:S(2)}) async-start(f32[8,288,384]{2,1,0:T(8,128)} %broadcast_in_dim.65), calls=%async_computation.6 | async-start | bytes 7077888 | tf_op jit(solution)/shard_map/all_to_all | solution.py:120
  308.0 35.8 %reduce-scatter.5.cloned.1.call-start = ((), (), s32[]{:S(2)}) async-start(), calls=%async_computation.12 | async-start | bytes 1179648 | tf_op jit(solution)/shard_map/reduce_scatter | solution.py:135
  360.9 30.0 %all-to-all-start.5 = ((f32[8,144,128]{2,1,0:T(8,128)}), f32[8,144,128]{2,1,0:T(8,128)}, u32[]{:S(2)}, u32[]{:S(2)}) async-start(f32[8,144,128]{2,1,0:T(8,128)} %broadcast_in_dim.67), calls=%async_computation.7 | async-start | bytes 1179648 | tf_op jit(solution)/shard_map/all_to_all | solution.py:120
  (39 other events, 347.3 us)
Sparse Core Ops, SparseCore 0:
  31.7 33.3 all-gather.3
  67.4 56.2 all-gather.5
  130.5 95.8 all-gather.7
  228.7 47.0 reduce-scatter.2
  311.5 32.2 reduce-scatter.4

commit v3 on v1

--- a/solution.py
+++ b/solution.py
@@ -138,12 +138,6 @@
 
 def eight_order(f):
     return ((f // 2) % 4 * 2 + f % 2) * 2 + f // 8
-
-
-def with_rows(block, extra):
-    width = block.shape[-1]
-    flat = block.reshape(-1, width)
-    return flat if extra is None else jnp.concatenate([flat, extra], 0)
 
 
 def adam_update(weight, gradient, moment_one, moment_two, learn_rate, decay_rate):
@@ -1177,7 +1171,6 @@
     partner_left = move(from_left, swap_y)
     partner_right = move(partner, along_x(-1))
 
-    b_partner = move(branch, swap_y)
     far, partner_left, partner_right, out_other, branch, in_low = lax.optimization_barrier(
         (far, partner_left, partner_right, out_other, branch, in_low)
     )
@@ -1209,12 +1202,13 @@
     )
     par = jnp.concatenate([conv_par, head_par, jnp.zeros((8, 640), F32)], 0)
 
-    partner_far_top, partner_far_low, own_shards, b_partner = lax.optimization_barrier(
-        (partner_far_top, partner_far_low, own_shards, b_partner)
+    partner_far_top, partner_far_low, own_shards = lax.optimization_barrier(
+        (partner_far_top, partner_far_low, own_shards)
     )
     full_out = gather_eight(tie(out_pair, own_shards))
     b_left = move(branch, along_x(1))
     b_right = move(branch, along_x(-1))
+    b_partner = move(branch, swap_y)
     token_pieces = [
         tokens, partner, from_right, partner_right, far,
         partner_far_top, partner_far_low, from_left, partner_left,
@@ -1278,17 +1272,17 @@
     z_other = move(other[SHARD_IN:], swap_y_hi)
     tail_rows, out_mine, out_other, z_other = lax.optimization_barrier((tail_rows, out_mine, out_other, z_other))
 
+    early_parts = share_rep(jnp.concatenate([out_mine + out_other, mine[SHARD_IN:] + z_other], 0))
     input_grad, grad_gain_in = run_input_grad(
         place.yh[None], grad_rows, tail_rows, full_in, low_dt, tokens, cotangent, gain_in
     )
-    early = jnp.concatenate([out_mine + out_other, mine[SHARD_IN:] + z_other], 0)
-    early, grad_gain_in = lax.optimization_barrier((early, grad_gain_in))
-
-    early_parts = share_rep(early)
+    tail_part, grad_gain_in = lax.optimization_barrier((tail_part, grad_gain_in))
+
+    tail_other = move(at(tail_part, 1 - place.yh), swap_y_hi)
     grad_gain_in = sum_z(grad_gain_in + move(grad_gain_in, swap_core))
-    tail_part, grad_gain_in = lax.optimization_barrier((tail_part, grad_gain_in))
-    tail_other = move(with_rows(at(tail_part, 1 - place.yh), grad_gain_in), swap_y_hi)
-    tail_part = with_rows(at(tail_part, place.yh), grad_gain_in) + tail_other
+    tail_part = at(tail_part, place.yh) + tail_other
+    grad_gain_in = grad_gain_in + move(grad_gain_in, swap_y_hi)
+    tail_part = jnp.concatenate([tail_part, grad_gain_in], 0)
 
     tail_part, early_parts = lax.optimization_barrier((tail_part, early_parts))
     tail_parts = share_rep(tail_part)

time: 403 us -> 393 us (0.975)
  waiting for transfers between devices: 99.1 us -> 85.8 us
    ppermute x27 -> x28, waiting for transfers between devices: 67.2 us -> 49.8 us  [move(): return lax.ppermute(value, ('fsdp', 'rep'), pairs)]
    ppermute x27 -> x28, starting transfers between devices: 44.3 us -> 48.5 us  [move(): return lax.ppermute(value, ('fsdp', 'rep'), pairs)]
  transfers between devices with their start and end apart: 37 -> 38, of which waited for: 19 -> 18; matrix products, arithmetic and copies ran while one was open for 6% -> 7% of each run, Pallas kernels for 41% -> 42%
where the time goes in v3:
time: 393 us; the launch traced here: 391 us
  Pallas kernels  171 us (44%)
  waiting for transfers between devices  85.8 us (22%)
  starting transfers between devices  69.8 us (18%)
  local copies, waits for them, and re-layouts  21.4 us (5%)
  other arithmetic  17.4 us (4%)
  between operations  14.5 us (4%)
  blocking collectives  10.3 us (3%)
    ppermute x28, waiting for transfers between devices, move(): return lax.ppermute(value, ('fsdp', 'rep'), pairs)  49.8 us
    ppermute x28, starting transfers between devices, move(): return lax.ppermute(value, ('fsdp', 'rep'), pairs)  48.5 us
    pallas_call x1, Pallas kernels, run_backward(): pl.pallas_call(backward_kernel, grid=(CHUNKS,), in_specs=[pl.BlockSpec(me...  32.1 us
    all_to_all x5, waiting for transfers between devices, exchange(): return lax.all_to_all(value, axis, 0, 0, tiled=True)  31.9 us
    pallas_call x2, Pallas kernels, run_forward(): pl.pallas_call(partial(forward_kernel, part), grid=(HALF,), in_specs=[pl....  24.3 us
    all_to_all x5, starting transfers between devices, exchange(): return lax.all_to_all(value, axis, 0, 0, tiled=True)  21.2 us
    pallas_call x1, Pallas kernels, run_project(): pl.pallas_call(partial(project_kernel, PARTS), grid_spec=pltpu.PrefetchSc...  17.4 us
    pallas_call x1, Pallas kernels, run_out_grad(): pl.pallas_call(out_grad_kernel, grid_spec=pltpu.PrefetchScalarGridSpec(nu...  13.6 us
  transfers between devices with their start and end apart: 38, of which 18 were waited for; matrix products, arithmetic and copies ran while one was open for 7% of the time, Pallas kernels for 42%

profile of v3, /device:TPU:0, one launch (start us, length us, event | category | flops | bytes accessed | tf_op | source)
XLA Modules:
  0.0 390.6 jit_solution(9820859114189624135)
XLA Ops:
  38.8 11.8 %collective-permute-done.7 = bf16[192,1536]{1,0:T(8,128)(2,1)S(1)} collective-permute-done((bf16[192,1536]{1,0:T(8,128)(2,1)S(1)}, bf16[192,1536]{1,0:T(8,128)(2,1)S(1)}, u32[]{:S(2)}, u32[]{:S(2)}) %collective-permute-start.7) | collective-permute-done | bytes 589856 | tf_op jit(solution)/shard_map/ppermute | solution.py:56
  58.1 4.6 %collective-permute-done.11.refs_5_ = bf16[128,1536]{1,0:T(8,128)(2,1)} collective-permute-done((bf16[128,1536]{1,0:T(8,128)(2,1)}, bf16[128,1536]{1,0:T(8,128)(2,1)}, u32[]{:S(2)}, u32[]{:S(2)}) %collective-permute-start.11) | collective-permute-done | bytes 393248 | tf_op jit(solution)/shard_map/ppermute | solution.py:56
  74.3 17.4 %project.1 = (bf16[2048,1536]{1,0:T(8,128)(2,1)}, f32[2048,1152]{1,0:T(8,128)}, bf16[1536,128]{1,0:T(8,128)(2,1)}) custom-call(s32[8]{0:T(128)} %fusion.5.table, bf16[256,1536]{1,0:T(8,128)(2,1)} %tokens.3, bf16[256,1536]{1,0:T(8,128)(2,1)} %collective-permute-done.2.refs_1_, bf16[256,1536]{1,0:T(8,128)(2,1)} %collective-permute-done.1.refs_2_, ...), custom_call_target="tpu_custom_call" | custom-call | flops 1000000 | bytes 100000 | tf_op jit(solution)/shard_map/project/pallas_call | solution.py:578
  97.1 12.1 %scan_forward.2 = (f32[2048,640]{1,0:T(8,128)}, f32[2048,384]{1,0:T(8,128)}, f32[2048,384]{1,0:T(8,128)}, f32[136,640]{1,0:T(8,128)}) custom-call(s32[3]{0:T(128)} %bitcast.92, f32[2048,1152]{1,0:T(8,128)} %get-tuple-element.127.proj.refs_11_.gate_in.conv_in.dt_in, f32[16,640]{1,0:T(8,128)} %concatenate.39.par), custom_call_target="tpu_custom_call" | custom-call | flops 1000000 | bytes 100000 | tf_op jit(solution)/shard_map/scan_forward/pallas_call | solution.py:349
  115.8 12.2 %scan_forward.3 = (f32[2048,640]{1,0:T(8,128)}, f32[2048,384]{1,0:T(8,128)}, f32[2048,384]{1,0:T(8,128)}, f32[136,640]{1,0:T(8,128)}) custom-call(s32[3]{0:T(128)} %bitcast.93, f32[2048,1152]{1,0:T(8,128)} %get-tuple-element.127.proj.refs_11_.gate_in.conv_in.dt_in, ...), custom_call_target="tpu_custom_call", output_to_operand_aliasing={{0}: (3, {}), {1}: (4, {}), {2}: (5, {})} | custom-call | flops 1000000 | bytes 100000 | tf_op jit(solution)/shard_map/scan_forward/pallas_call | solution.py:349
  133.0 13.6 %out_grad.1 = (bf16[2048,1536]{1,0:T(8,128)(2,1)}, f32[2048,384]{1,0:T(8,128)}, f32[8,2048]{1,0:T(8,128)}) custom-call(s32[9]{0:T(128)} %pad_add_fusion.table, bf16[256,1536]{1,0:T(8,128)(2,1)} %copy-done.6, bf16[256,1536]{1,0:T(8,128)(2,1)} %collective-permute-done.10.refs_1_, bf16[256,1536]{1,0:T(8,128)(2,1)} %copy-done.12, bf16[256,1536]{1,0:T(8,128)(2,1)} %copy-done.9, ...), custom_call_target="tpu_custom_call" | custom-call | flops 1000000 | bytes 100000 | tf_op jit(solution)/shard_map/out_grad/pallas_call | solution.py:635
  147.5 10.3 %all_to_all.34 = f32[8,32,128]{2,1,0:T(8,128)S(1)} all-to-all(f32[8,32,128]{2,1,0:T(8,128)S(1)} %broadcast_in_dim.62), channel_id=1, replica_groups=mesh['fsdp'=16,'rep'=8] {'rep'}, dimensions={0} | all-to-all | bytes 262144 | tf_op jit(solution)/shard_map/all_to_all | solution.py:120
  158.5 10.5 %gate_backward.1 = (bf16[2048,768]{1,0:T(8,128)(2,1)}, f32[2048,384]{1,0:T(8,128)}, f32[8,384]{1,0:T(8,128)}) custom-call(f32[2048,384]{1,0:T(8,128)} %get-tuple-element.146.grad_out, f32[2048,384]{1,0:T(8,128)} %get-tuple-element.145.refs_10_.mixed_in, f32[2048,1152]{1,0:T(8,128)} %get-tuple-element.127.proj.refs_11_.gate_in.conv_in.dt_in, ...), custom_call_target="tpu_custom_call" | custom-call | flops 1000000 | bytes 100000 | tf_op jit(solution)/shard_map/gate_backward/pallas_call | solution.py:690
  172.7 32.1 %scan_backward.1 = (bf16[2048,384]{1,0:T(8,128)(2,1)}, bf16[2048,128]{1,0:T(8,128)(2,1)}, f32[256,2048]{1,0:T(8,128)}, f32[8,384]{1,0:T(8,128)}, f32[8,128]{1,0:T(8,128)}) custom-call(s32[3]{0:T(128)} %bitcast.94, f32[2048,1152]{1,0:T(8,128)} %get-tuple-element.127.proj.refs_11_.gate_in.conv_in.dt_in, ...), custom_call_target="tpu_custom_call" | custom-call | flops 1000000 | bytes 100000 | tf_op jit(solution)/shard_map/scan_backward/pallas_call | solution.py:477
  204.7 12.7 %early_grad.1 = f32[16,192,384]{2,1,0:T(8,128)} custom-call(bf16[2048,768]{1,0:T(8,128)(2,1)} %get-tuple-element.153.low, bf16[2048,1536]{1,0:T(8,128)(2,1)} %get-tuple-element.154.grad_branch, bf16[2048,1536]{1,0:T(8,128)(2,1)} %get-tuple-element.155.normed), custom_call_target="tpu_custom_call" | custom-call | flops 1000000 | bytes 100000 | tf_op jit(solution)/shard_map/early_grad/pallas_call | solution.py:734
  219.1 5.4 %all-to-all-start.2 = ((f32[8,32,2048]{2,1,0:T(8,128)}), f32[8,32,2048]{2,1,0:T(8,128)S(1)}, u32[]{:S(2)}, u32[]{:S(2)}) async-start(f32[8,32,2048]{2,1,0:T(8,128)} %bitcast.78), calls=%async_computation.3 | async-start | bytes 4194304 | tf_op jit(solution)/shard_map/all_to_all | solution.py:120
  226.1 7.8 %z_grad.1.grad_z = f32[1536,256]{1,0:T(8,128)} custom-call(bf16[8,256,768]{2,1,0:T(8,128)(2,1)} %copy-done.2, bf16[4,2,2,96,6400]{4,3,2,1,0:T(8,128)(2,1)} %bitcast.66), custom_call_target="tpu_custom_call" | custom-call | flops 2400000000 | bytes 20000000 | tf_op jit(solution)/shard_map/z_grad/pallas_call | solution.py:807
  233.9 14.6 %all-to-all-done.2.parts = f32[8,32,2048]{2,1,0:T(8,128)S(1)} async-done(((f32[8,32,2048]{2,1,0:T(8,128)}), f32[8,32,2048]{2,1,0:T(8,128)S(1)}, u32[]{:S(2)}, u32[]{:S(2)}) %all-to-all-start.2) | async-done | bytes 2097184 | tf_op jit(solution)/shard_map/all_to_all | solution.py:120
  249.8 6.8 %rest_backward.1 = (bf16[2048,512]{1,0:T(8,128)(2,1)}, f32[8,512]{1,0:T(8,128)}) custom-call(s32[3]{0:T(128)} %bitcast.95, f32[8,32,2048]{2,1,0:T(8,128)} %copy-done.5, f32[2048,640]{1,0:T(8,128)} %get-tuple-element.149.pre_in.pre_b.pre_c, f32[2048,640]{1,0:T(8,128)} %get-tuple-element.149.pre_in.pre_b.pre_c, ...), custom_call_target="tpu_custom_call" | custom-call | flops 1000000 | bytes 100000 | tf_op jit(solution)/shard_map/rest_backward/pallas_call | solution.py:959
  256.6 8.9 %tail_grad.1 = f32[16,104,512]{2,1,0:T(8,128)} custom-call(bf16[2048,1536]{1,0:T(8,128)(2,1)} %get-tuple-element.155.normed, bf16[2048,512]{1,0:T(8,128)(2,1)} %get-tuple-element.174.tail, f32[8,512]{1,0:T(8,128)} %get-tuple-element.170.small), custom_call_target="tpu_custom_call" | custom-call | flops 1000000 | bytes 100000 | tf_op jit(solution)/shard_map/tail_grad/pallas_call | solution.py:1005
  270.3 8.1 %block_out.1 = f32[256,1536]{1,0:T(8,128)} custom-call(bf16[8,256,768]{2,1,0:T(8,128)(2,1)} %copy-done.2, bf16[4,2,2,192,1536]{4,3,2,1,0:T(8,128)(2,1)} %bitcast.70, bf16[256,1536]{1,0:T(8,128)(2,1)} %tokens.3, f32[256,1]{1,0:T(8,128)} %fusion.1.live), custom_call_target="tpu_custom_call" | custom-call | flops 2400000000 | bytes 20000000 | tf_op jit(solution)/shard_map/block_out/pallas_call | solution.py:767
  286.3 6.2 %collective-permute-done.20 = f32[96,384]{1,0:T(8,128)S(1)} collective-permute-done((f32[96,384]{1,0:T(8,128)S(1)}, f32[96,384]{1,0:T(8,128)S(1)}, u32[]{:S(2)}, u32[]{:S(2)}) %collective-permute-start.20) | collective-permute-done | bytes 147488 | tf_op jit(solution)/shard_map/ppermute | solution.py:56
  292.5 5.7 %collective-permute-done.21 = f32[96,384]{1,0:T(8,128)S(1)} collective-permute-done((f32[96,384]{1,0:T(8,128)S(1)}, f32[96,384]{1,0:T(8,128)S(1)}, u32[]{:S(2)}, u32[]{:S(2)}) %collective-permute-start.21) | collective-permute-done | bytes 147488 | tf_op jit(solution)/shard_map/ppermute | solution.py:56
  305.3 11.4 %input_grad.1 = (f32[256,1536]{1,0:T(8,128)}, f32[8,512]{1,0:T(8,128)}) custom-call(s32[1]{0:T(128)} %bitcast.21.own_half, f32[1536,256]{1,0:T(8,128)} %z_grad.1.grad_z, bf16[8,256,512]{2,1,0:T(8,128)(2,1)} %copy-done.4, bf16[8,256,512]{2,1,0:T(8,128)(2,1)} %copy-done.4, bf16[4,2,2,96,6400]{4,3,2,1,0:T(8,128)(2,1)} %bitcast.67, ...), custom_call_target="tpu_custom_call" | custom-call | flops 1000000 | bytes 100000 | tf_op jit(solution)/shard_map/input_grad/pallas_call | solution.py:874
  331.2 8.4 %collective-permute-done.27 = f32[8,512]{1,0:T(8,128)S(1)} collective-permute-done((f32[8,512]{1,0:T(8,128)S(1)}, f32[8,512]{1,0:T(8,128)S(1)}, u32[]{:S(2)}, u32[]{:S(2)}) %collective-permute-start.27) | collective-permute-done | bytes 16416 | tf_op jit(solution)/shard_map/ppermute | solution.py:56
  346.8 5.7 %adam.2 = (f32[96,6400]{1,0:T(8,128)}, f32[96,6400]{1,0:T(8,128)}, f32[96,6400]{1,0:T(8,128)}, f32[96,6400]{1,0:T(8,128)}) custom-call(f32[8,192,384]{2,1,0:T(8,128)} %all-to-all-done.4.pair, f32[96,6400]{1,0:T(8,128)} %refs_0_.6, f32[96,6400]{1,0:T(8,128)} %refs_1_.4, f32[96,6400]{1,0:T(8,128)} %refs_2_.4), custom_call_target="tpu_custom_call" | custom-call | flops 2400000000 | bytes 20000000 | tf_op jit(solution)/shard_map/adam/pallas_call | solution.py:1043
  352.6 5.3 %adam.3 = (f32[192,1536]{1,0:T(8,128)}, f32[192,1536]{1,0:T(8,128)}, f32[192,1536]{1,0:T(8,128)}, f32[192,1536]{1,0:T(8,128)}) custom-call(f32[8,192,384]{2,1,0:T(8,128)} %all-to-all-done.4.pair, f32[192,1536]{1,0:T(8,128)} %refs_0_.7, f32[192,1536]{1,0:T(8,128)} %refs_1_.5, f32[192,1536]{1,0:T(8,128)} %refs_2_.5), custom_call_target="tpu_custom_call" | custom-call | flops 2400000000 | bytes 20000000 | tf_op jit(solution)/shard_map/adam/pallas_call | solution.py:1043
  358.0 16.5 %all-to-all-done.5.pair.rest = f32[8,112,512]{2,1,0:T(8,128)S(1)} async-done(((f32[8,112,512]{2,1,0:T(8,128)}), f32[8,112,512]{2,1,0:T(8,128)S(1)}, u32[]{:S(2)}, u32[]{:S(2)}) %all-to-all-start.5) | async-done | bytes 1835040 | tf_op jit(solution)/shard_map/all_to_all | solution.py:120
  377.2 6.9 %adam_tail.1 = (f32[96,6400]{1,0:T(8,128)}, f32[96,6400]{1,0:T(8,128)}, f32[96,6400]{1,0:T(8,128)}, f32[96,6400]{1,0:T(8,128)}) custom-call(f32[8,112,512]{2,1,0:T(8,128)} %copy-done.3, f32[8,112,512]{2,1,0:T(8,128)} %copy-done.3, f32[96,6400]{1,0:T(8,128)} %refs_0_.6, ...), custom_call_target="tpu_custom_call", output_to_operand_aliasing={{0}: (5, {}), {1}: (6, {}), {2}: (7, {}), {3}: (8, {})} | custom-call | flops 1000000 | bytes 100000 | tf_op jit(solution)/shard_map/adam_tail/pallas_call | solution.py:1086
  (221 shorter events, 121.2 us)
Async XLA Ops:
  7.2 57.9 %all-gather.4.cloned.1.call-start = ((), (), s32[]{:S(2)}) async-start(), calls=%async_computation.8 | async-start | bytes 4644864 | tf_op jit(solution)/shard_map/all_gather | solution.py:115
  7.3 20.8 %collective-permute-start = (bf16[256,1536]{1,0:T(8,128)(2,1)}, bf16[256,1536]{1,0:T(8,128)(2,1)}, u32[]{:S(2)}, u32[]{:S(2)}) collective-permute-start(bf16[256,1536]{1,0:T(8,128)(2,1)} %tokens.3), channel_id=1, source_target_pairs={{0,2},{1,3},{2,4},{3,5},{4,6},{5,7},{6,0},{7,1},{8,10},{9,11},{10,... | collective-permute-start | bytes 2359304 | tf_op jit(solution)/shard_map/ppermute | solution.py:56
  8.9 19.3 %collective-permute-start.1 = (bf16[256,1536]{1,0:T(8,128)(2,1)}, bf16[256,1536]{1,0:T(8,128)(2,1)}, u32[]{:S(2)}, u32[]{:S(2)}) collective-permute-start(bf16[256,1536]{1,0:T(8,128)(2,1)} %tokens.3), channel_id=1, source_target_pairs={{0,6},{1,7},{2,0},{3,1},{4,2},{5,3},{6,4},{7,5},{8,14},{9,15},{10,... | collective-permute-start | bytes 2359304 | tf_op jit(solution)/shard_map/ppermute | solution.py:56
  10.6 19.0 %collective-permute-start.2 = (bf16[256,1536]{1,0:T(8,128)(2,1)}, bf16[256,1536]{1,0:T(8,128)(2,1)}, u32[]{:S(2)}, u32[]{:S(2)}) collective-permute-start(bf16[256,1536]{1,0:T(8,128)(2,1)} %tokens.3), channel_id=1, source_target_pairs={{0,1},{1,0},{2,3},{3,2},{4,5},{5,4},{6,7},{7,6},{8,9},{9,8},{10,11... | collective-permute-start | bytes 2359304 | tf_op jit(solution)/shard_map/ppermute | solution.py:56
  31.6 101.4 %all-gather.6.cloned.1.call-start = ((), (), s32[]{:S(2)}) async-start(), calls=%async_computation.9 | async-start | bytes 10616832 | tf_op jit(solution)/shard_map/all_gather | solution.py:115
  31.7 19.3 %collective-permute-start.4 = (bf16[256,1536]{1,0:T(8,128)(2,1)}, bf16[256,1536]{1,0:T(8,128)(2,1)S(1)}, u32[]{:S(2)}, u32[]{:S(2)}) collective-permute-start(bf16[256,1536]{1,0:T(8,128)(2,1)} %collective-permute-done.refs_7_), channel_id=1, source_target_pairs={{0,2},{1,3},{2,4},{3,5},{4,6},{5,7},{6,0},{7,1},{8,10},{9,11},{10,... | collective-permute-start | bytes 2359304 | tf_op jit(solution)/shard_map/ppermute | solution.py:56
  32.1 18.8 %collective-permute-start.5 = (bf16[256,1536]{1,0:T(8,128)(2,1)}, bf16[256,1536]{1,0:T(8,128)(2,1)S(1)}, u32[]{:S(2)}, u32[]{:S(2)}) collective-permute-start(bf16[256,1536]{1,0:T(8,128)(2,1)} %collective-permute-done.refs_7_), channel_id=1, source_target_pairs={{0,1},{1,0},{2,3},{3,2},{4,5},{5,4},{6,7},{7,6},{8,9},{9,8},{10,11... | collective-permute-start | bytes 2359304 | tf_op jit(solution)/shard_map/ppermute | solution.py:56
  33.7 18.1 %collective-permute-start.6 = (bf16[256,1536]{1,0:T(8,128)(2,1)}, bf16[256,1536]{1,0:T(8,128)(2,1)S(1)}, u32[]{:S(2)}, u32[]{:S(2)}) collective-permute-start(bf16[256,1536]{1,0:T(8,128)(2,1)} %collective-permute-done.2.refs_1_), channel_id=1, source_target_pairs={{0,6},{1,7},{2,0},{3,1},{4,2},{5,3},{6,4},{7,5},{8,14},{9,15},{10,... | collective-permute-start | bytes 2359304 | tf_op jit(solution)/shard_map/ppermute | solution.py:56
  65.1 161.0 %all-gather.8.cloned.1.call-start = ((), (), s32[]{:S(2)}) async-start(), calls=%async_computation.11 | async-start | bytes 22118400 | tf_op jit(solution)/shard_map/all_gather | solution.py:115
  65.7 26.0 %collective-permute-start.8 = (bf16[256,1536]{1,0:T(8,128)(2,1)S(1)}, bf16[256,1536]{1,0:T(8,128)(2,1)}, u32[]{:S(2)}, u32[]{:S(2)}) collective-permute-start(bf16[256,1536]{1,0:T(8,128)(2,1)S(1)} %multiply_convert_fusion.refs_0_), channel_id=1, source_target_pairs={{0,2},{1,3},{2,4},{3,5},{4,6},{5,7},{6,0},{7,1},{8,10},{9,11},{10,... | collective-permute-start | bytes 2359304 | tf_op jit(solution)/shard_map/ppermute | solution.py:56
  67.2 24.5 %collective-permute-start.9 = (bf16[256,1536]{1,0:T(8,128)(2,1)S(1)}, bf16[256,1536]{1,0:T(8,128)(2,1)S(1)}, u32[]{:S(2)}, u32[]{:S(2)}) collective-permute-start(bf16[256,1536]{1,0:T(8,128)(2,1)S(1)} %multiply_convert_fusion.refs_0_), channel_id=1, source_target_pairs={{0,6},{1,7},{2,0},{3,1},{4,2},{5,3},{6,4},{7,5},{8,14},{9,15},{10,... | collective-permute-start | bytes 2359304 | tf_op jit(solution)/shard_map/ppermute | solution.py:56
  68.9 22.8 %collective-permute-start.10 = (bf16[256,1536]{1,0:T(8,128)(2,1)S(1)}, bf16[256,1536]{1,0:T(8,128)(2,1)}, u32[]{:S(2)}, u32[]{:S(2)}) collective-permute-start(bf16[256,1536]{1,0:T(8,128)(2,1)S(1)} %multiply_convert_fusion.refs_0_), channel_id=1, source_target_pairs={{0,1},{1,0},{2,3},{3,2},{4,5},{5,4},{6,7},{7,6},{8,9},{9,8},{10,11... | collective-permute-start | bytes 2359304 | tf_op jit(solution)/shard_map/ppermute | solution.py:56
  70.4 57.6 %collective-permute-start.16 = (bf16[96,6400]{1,0:T(8,128)(2,1)S(1)}, bf16[96,6400]{1,0:T(8,128)(2,1)}, u32[]{:S(2)}, u32[]{:S(2)}) collective-permute-start(bf16[96,6400]{1,0:T(8,128)(2,1)S(1)} %convert_element_type.48), channel_id=1, source_target_pairs={{0,65},{1,64},{2,67},{3,66},{4,69},{5,68},{6,71},{7,70},{8,73},{9,... | collective-permute-start | bytes 3686408 | tf_op jit(solution)/shard_map/ppermute | solution.py:56
  91.7 19.9 %collective-permute-start.13 = (bf16[256,1536]{1,0:T(8,128)(2,1)}, bf16[256,1536]{1,0:T(8,128)(2,1)}, u32[]{:S(2)}, u32[]{:S(2)}) collective-permute-start(bf16[256,1536]{1,0:T(8,128)(2,1)} %collective-permute-done.8.refs_7_), channel_id=1, source_target_pairs={{0,2},{1,3},{2,4},{3,5},{4,6},{5,7},{6,0},{7,1},{8,10},{9,11},{10,... | collective-permute-start | bytes 2359304 | tf_op jit(solution)/shard_map/ppermute | solution.py:56
  92.6 19.1 %collective-permute-start.14 = (bf16[256,1536]{1,0:T(8,128)(2,1)}, bf16[256,1536]{1,0:T(8,128)(2,1)S(1)}, u32[]{:S(2)}, u32[]{:S(2)}) collective-permute-start(bf16[256,1536]{1,0:T(8,128)(2,1)} %collective-permute-done.8.refs_7_), channel_id=1, source_target_pairs={{0,1},{1,0},{2,3},{3,2},{4,5},{5,4},{6,7},{7,6},{8,9},{9,8},{10,11... | collective-permute-start | bytes 2359304 | tf_op jit(solution)/shard_map/ppermute | solution.py:56
  93.0 18.7 %collective-permute-start.15 = (bf16[256,1536]{1,0:T(8,128)(2,1)}, bf16[256,1536]{1,0:T(8,128)(2,1)S(1)}, u32[]{:S(2)}, u32[]{:S(2)}) collective-permute-start(bf16[256,1536]{1,0:T(8,128)(2,1)} %collective-permute-done.10.refs_1_), channel_id=1, source_target_pairs={{0,6},{1,7},{2,0},{3,1},{4,2},{5,3},{6,4},{7,5},{8,14},{9,15},{10,... | collective-permute-start | bytes 2359304 | tf_op jit(solution)/shard_map/ppermute | solution.py:56
  111.7 16.3 %collective-permute-start.17 = (bf16[128,1536]{1,0:T(8,128)(2,1)S(1)}, bf16[128,1536]{1,0:T(8,128)(2,1)S(1)}, u32[]{:S(2)}, u32[]{:S(2)}) collective-permute-start(bf16[128,1536]{1,0:T(8,128)(2,1)S(1)} %slice.135), channel_id=1, source_target_pairs={{0,2},{1,3},{2,4},{3,5},{4,6},{5,7},{6,0},{7,1},{8,10},{9,11},{10,... | collective-permute-start | bytes 1179656 | tf_op jit(solution)/shard_map/ppermute | solution.py:56
  168.9 48.5 %all-to-all-start.1 = ((bf16[8,256,768]{2,1,0:T(8,128)(2,1)}), bf16[8,256,768]{2,1,0:T(8,128)(2,1)S(1)}, u32[]{:S(2)}, u32[]{:S(2)}) async-start(bf16[8,256,768]{2,1,0:T(8,128)(2,1)} %bitcast.73), calls=%async_computation.1 | async-start | bytes 6291456 | tf_op jit(solution)/shard_map/all_to_all | solution.py:120
  172.6 105.8 %reduce-scatter.3.cloned.1.call-start = ((), (), s32[]{:S(2)}) async-start(), calls=%async_computation.10 | async-start | bytes 5308416 | tf_op jit(solution)/shard_map/reduce_scatter | solution.py:135
  219.1 29.4 %all-to-all-start.2 = ((f32[8,32,2048]{2,1,0:T(8,128)}), f32[8,32,2048]{2,1,0:T(8,128)S(1)}, u32[]{:S(2)}, u32[]{:S(2)}) async-start(f32[8,32,2048]{2,1,0:T(8,128)} %bitcast.78), calls=%async_computation.3 | async-start | bytes 4194304 | tf_op jit(solution)/shard_map/all_to_all | solution.py:120
  224.5 92.2 %reduce-scatter.5.cloned.1.call-start = ((), (), s32[]{:S(2)}) async-start(), calls=%async_computation.12 | async-start | bytes 3833856 | tf_op jit(solution)/shard_map/reduce_scatter | solution.py:135
  265.6 32.6 %all-to-all-start.3 = ((bf16[8,256,512]{2,1,0:T(8,128)(2,1)}), bf16[8,256,512]{2,1,0:T(8,128)(2,1)S(1)}, u32[]{:S(2)}, u32[]{:S(2)}) async-start(bf16[8,256,512]{2,1,0:T(8,128)(2,1)} %bitcast.74), calls=%async_computation.4 | async-start | bytes 4194304 | tf_op jit(solution)/shard_map/all_to_all | solution.py:120
  300.9 40.5 %all-to-all-start.4 = ((f32[8,192,384]{2,1,0:T(8,128)}), f32[8,192,384]{2,1,0:T(8,128)}, u32[]{:S(2)}, u32[]{:S(2)}) async-start(f32[8,192,384]{2,1,0:T(8,128)} %broadcast_in_dim.66), calls=%async_computation.6 | async-start | bytes 4718592 | tf_op jit(solution)/shard_map/all_to_all | solution.py:120
  342.9 31.6 %all-to-all-start.5 = ((f32[8,112,512]{2,1,0:T(8,128)}), f32[8,112,512]{2,1,0:T(8,128)S(1)}, u32[]{:S(2)}, u32[]{:S(2)}) async-start(f32[8,112,512]{2,1,0:T(8,128)} %broadcast_in_dim.67), calls=%async_computation.7 | async-start | bytes 3670016 | tf_op jit(solution)/shard_map/all_to_all | solution.py:120
  (38 other events, 429.7 us)
Sparse Core Ops, SparseCore 0:
  31.7 33.3 all-gather.3
  67.4 54.1 all-gather.5
  131.3 94.8 all-gather.7
  228.4 39.9 reduce-scatter.2
  270.7 41.8 reduce-scatter.4

commit v4 on v3

--- a/solution.py
+++ b/solution.py
@@ -816,7 +816,7 @@
         compiler_params=pltpu.CompilerParams(
             dimension_semantics=("arbitrary",), vmem_limit_bytes=VMEM_LIMIT
         ),
-        cost_estimate=FILL,
+        cost_estimate=COST,
         name="z_grad",
     )(rows, full_in)
 
@@ -1244,14 +1244,14 @@
     grad_x, grad_dtraw, grad_bc, grad_sums, grad_heads = run_backward(
         seg_ends, proj, pre, mixed, grad_mixed, states, par
     )
-    low, grad_x = lax.optimization_barrier((low, grad_x))
+    low_rows, low, grad_bc, grad_x = lax.optimization_barrier((low_rows, low, grad_bc, grad_x))
+
+    grad_bc = exchange(grad_bc, "rep").reshape(N_REP, OWN_BC, PACK)
     early_grad = run_early_grad(low, grad_branch, normed)
-    low_rows, early_grad, grad_bc, grad_x = lax.optimization_barrier((low_rows, early_grad, grad_bc, grad_x))
-
-    grad_bc = exchange(grad_bc, "rep").reshape(N_REP, OWN_BC, PACK)
     early = scatter_eight(early_grad)
+    early_grad, low_rows = lax.optimization_barrier((early_grad, low_rows))
     grad_rows = run_z_grad(low_rows, full_in)
-    grad_bc, grad_rows = lax.optimization_barrier((grad_bc, grad_rows))
+    grad_bc, grad_rows, early_grad = lax.optimization_barrier((grad_bc, grad_rows, early_grad))
 
     tail, small_own = run_rest(
         seg_ends, grad_bc, pre, proj, par, grad_x, grad_dtraw, grad_sums, grad_heads, grad_gain, (r * OWN_BC)[None]
@@ -1259,9 +1259,8 @@
     grad_tail = run_tail_grad(normed, tail, small_own)
     tail, grad_tail, low_rows = lax.optimization_barrier((tail, grad_tail, low_rows))
     tail_rows = exchange(tail.reshape(N_REP, ROWS, TAIL), "rep")
+    early, grad_tail = lax.optimization_barrier((early, grad_tail))
     tail_part = scatter_eight(grad_tail)
-    block_out = run_block_out(low_rows, full_out, tokens, own_live)
-    early, block_out = lax.optimization_barrier((early, block_out))
     mine, other = at(early, place.yh), at(early, 1 - place.yh)
     out_mine = move(
         mine[:SHARD_IN], lambda yh, z, c, x, yl: (x // 2, (x % 2) * 2 + yl, z % 2, 2 * c + yh, z // 2)
@@ -1284,8 +1283,9 @@
     grad_gain_in = grad_gain_in + move(grad_gain_in, swap_y_hi)
     tail_part = jnp.concatenate([tail_part, grad_gain_in], 0)
 
-    tail_part, early_parts = lax.optimization_barrier((tail_part, early_parts))
+    tail_part, early_parts, low_rows = lax.optimization_barrier((tail_part, early_parts, low_rows))
     tail_parts = share_rep(tail_part)
+    block_out = run_block_out(low_rows, full_out, tokens, own_live)
 
     grad_out, new_first_out, new_second_out, new_out = run_adam_early(
         lambda i: (i // 2, i % 2), slice(0, SHARD_IN), early_parts, w_out, first_out, second_out

time: 393 us -> 401 us (1.020)
  waiting for transfers between devices: 85.8 us -> 101 us
    ppermute x28, waiting for transfers between devices: 49.8 us -> 65.3 us  [move(): return lax.ppermute(value, ('fsdp', 'rep'), pairs)]
  transfers between devices with their start and end apart: 38 -> 38, of which waited for: 18 -> 17; matrix products, arithmetic and copies ran while one was open for 7% -> 6% of each run, Pallas kernels for 42% -> 41%
where the time goes in v4:
time: 401 us; the launch traced here: 399 us
  Pallas kernels  172 us (43%)
  waiting for transfers between devices  101 us (25%)
  starting transfers between devices  66.2 us (17%)
  local copies, waits for them, and re-layouts  19.1 us (5%)
  other arithmetic  16.3 us (4%)
  between operations  14.5 us (4%)
  blocking collectives  10.2 us (3%)
    ppermute x28, waiting for transfers between devices, move(): return lax.ppermute(value, ('fsdp', 'rep'), pairs)  65.3 us
    ppermute x28, starting transfers between devices, move(): return lax.ppermute(value, ('fsdp', 'rep'), pairs)  45.7 us
    all_to_all x5, waiting for transfers between devices, exchange(): return lax.all_to_all(value, axis, 0, 0, tiled=True)  32.8 us
    pallas_call x1, Pallas kernels, run_backward(): pl.pallas_call(backward_kernel, grid=(CHUNKS,), in_specs=[pl.BlockSpec(me...  32.1 us
    pallas_call x2, Pallas kernels, run_forward(): pl.pallas_call(partial(forward_kernel, part), grid=(HALF,), in_specs=[pl....  24.2 us
    all_to_all x5, starting transfers between devices, exchange(): return lax.all_to_all(value, axis, 0, 0, tiled=True)  20.3 us
    pallas_call x1, Pallas kernels, run_project(): pl.pallas_call(partial(project_kernel, PARTS), grid_spec=pltpu.PrefetchSc...  17.4 us
    pallas_call x1, Pallas kernels, run_out_grad(): pl.pallas_call(out_grad_kernel, grid_spec=pltpu.PrefetchScalarGridSpec(nu...  13.6 us
  transfers between devices with their start and end apart: 38, of which 17 were waited for; matrix products, arithmetic and copies ran while one was open for 6% of the time, Pallas kernels for 41%

profile of v4, /device:TPU:0, one launch (start us, length us, event | category | flops | bytes accessed | tf_op | source)
XLA Modules:
  0.0 399.0 jit_solution(8989832633392848150)
XLA Ops:
  38.8 11.8 %collective-permute-done.7 = bf16[192,1536]{1,0:T(8,128)(2,1)S(1)} collective-permute-done((bf16[192,1536]{1,0:T(8,128)(2,1)S(1)}, bf16[192,1536]{1,0:T(8,128)(2,1)S(1)}, u32[]{:S(2)}, u32[]{:S(2)}) %collective-permute-start.7) | collective-permute-done | bytes 589856 | tf_op jit(solution)/shard_map/ppermute | solution.py:56
  58.1 4.6 %collective-permute-done.11.refs_5_ = bf16[128,1536]{1,0:T(8,128)(2,1)} collective-permute-done((bf16[128,1536]{1,0:T(8,128)(2,1)}, bf16[128,1536]{1,0:T(8,128)(2,1)}, u32[]{:S(2)}, u32[]{:S(2)}) %collective-permute-start.11) | collective-permute-done | bytes 393248 | tf_op jit(solution)/shard_map/ppermute | solution.py:56
  74.3 17.4 %project.1 = (bf16[2048,1536]{1,0:T(8,128)(2,1)}, f32[2048,1152]{1,0:T(8,128)}, bf16[1536,128]{1,0:T(8,128)(2,1)}) custom-call(s32[8]{0:T(128)} %fusion.5.table, bf16[256,1536]{1,0:T(8,128)(2,1)} %tokens.3, bf16[256,1536]{1,0:T(8,128)(2,1)} %collective-permute-done.2.refs_1_, bf16[256,1536]{1,0:T(8,128)(2,1)} %collective-permute-done.1.refs_2_, ...), custom_call_target="tpu_custom_call" | custom-call | flops 1000000 | bytes 100000 | tf_op jit(solution)/shard_map/project/pallas_call | solution.py:578
  97.1 12.1 %scan_forward.2 = (f32[2048,640]{1,0:T(8,128)}, f32[2048,384]{1,0:T(8,128)}, f32[2048,384]{1,0:T(8,128)}, f32[136,640]{1,0:T(8,128)}) custom-call(s32[3]{0:T(128)} %bitcast.92, f32[2048,1152]{1,0:T(8,128)} %get-tuple-element.127.proj.refs_11_.gate_in.conv_in.dt_in, f32[16,640]{1,0:T(8,128)} %concatenate.39.par), custom_call_target="tpu_custom_call" | custom-call | flops 1000000 | bytes 100000 | tf_op jit(solution)/shard_map/scan_forward/pallas_call | solution.py:349
  115.8 12.2 %scan_forward.3 = (f32[2048,640]{1,0:T(8,128)}, f32[2048,384]{1,0:T(8,128)}, f32[2048,384]{1,0:T(8,128)}, f32[136,640]{1,0:T(8,128)}) custom-call(s32[3]{0:T(128)} %bitcast.93, f32[2048,1152]{1,0:T(8,128)} %get-tuple-element.127.proj.refs_11_.gate_in.conv_in.dt_in, ...), custom_call_target="tpu_custom_call", output_to_operand_aliasing={{0}: (3, {}), {1}: (4, {}), {2}: (5, {})} | custom-call | flops 1000000 | bytes 100000 | tf_op jit(solution)/shard_map/scan_forward/pallas_call | solution.py:349
  133.0 13.6 %out_grad.1 = (bf16[2048,1536]{1,0:T(8,128)(2,1)}, f32[2048,384]{1,0:T(8,128)}, f32[8,2048]{1,0:T(8,128)}) custom-call(s32[9]{0:T(128)} %pad_add_fusion.table, bf16[256,1536]{1,0:T(8,128)(2,1)} %copy-done.6, bf16[256,1536]{1,0:T(8,128)(2,1)} %collective-permute-done.10.refs_1_, bf16[256,1536]{1,0:T(8,128)(2,1)} %copy-done.12, bf16[256,1536]{1,0:T(8,128)(2,1)} %copy-done.9, ...), custom_call_target="tpu_custom_call" | custom-call | flops 1000000 | bytes 100000 | tf_op jit(solution)/shard_map/out_grad/pallas_call | solution.py:635
  147.5 10.2 %all_to_all.34 = f32[8,32,128]{2,1,0:T(8,128)S(1)} all-to-all(f32[8,32,128]{2,1,0:T(8,128)S(1)} %broadcast_in_dim.62), channel_id=1, replica_groups=mesh['fsdp'=16,'rep'=8] {'rep'}, dimensions={0} | all-to-all | bytes 262144 | tf_op jit(solution)/shard_map/all_to_all | solution.py:120
  158.4 10.5 %gate_backward.1 = (bf16[2048,768]{1,0:T(8,128)(2,1)}, f32[2048,384]{1,0:T(8,128)}, f32[8,384]{1,0:T(8,128)}) custom-call(f32[2048,384]{1,0:T(8,128)} %get-tuple-element.146.grad_out, f32[2048,384]{1,0:T(8,128)} %get-tuple-element.145.refs_10_.mixed_in, f32[2048,1152]{1,0:T(8,128)} %get-tuple-element.127.proj.refs_11_.gate_in.conv_in.dt_in, ...), custom_call_target="tpu_custom_call" | custom-call | flops 1000000 | bytes 100000 | tf_op jit(solution)/shard_map/gate_backward/pallas_call | solution.py:690
  172.6 32.1 %scan_backward.1 = (bf16[2048,384]{1,0:T(8,128)(2,1)}, bf16[2048,128]{1,0:T(8,128)(2,1)}, f32[256,2048]{1,0:T(8,128)}, f32[8,384]{1,0:T(8,128)}, f32[8,128]{1,0:T(8,128)}) custom-call(s32[3]{0:T(128)} %bitcast.94, f32[2048,1152]{1,0:T(8,128)} %get-tuple-element.127.proj.refs_11_.gate_in.conv_in.dt_in, ...), custom_call_target="tpu_custom_call" | custom-call | flops 1000000 | bytes 100000 | tf_op jit(solution)/shard_map/scan_backward/pallas_call | solution.py:477
  204.7 6.8 %all-to-all-done.1.rows = bf16[8,256,768]{2,1,0:T(8,128)(2,1)S(1)} async-done(((bf16[8,256,768]{2,1,0:T(8,128)(2,1)}), bf16[8,256,768]{2,1,0:T(8,128)(2,1)S(1)}, u32[]{:S(2)}, u32[]{:S(2)}) %all-to-all-start.1) | async-done | bytes 3145760 | tf_op jit(solution)/shard_map/all_to_all | solution.py:120
  211.5 13.6 %early_grad.1 = f32[16,192,384]{2,1,0:T(8,128)} custom-call(bf16[2048,768]{1,0:T(8,128)(2,1)} %get-tuple-element.154.low, bf16[2048,1536]{1,0:T(8,128)(2,1)} %get-tuple-element.155.grad_branch, bf16[2048,1536]{1,0:T(8,128)(2,1)} %get-tuple-element.156.normed), custom_call_target="tpu_custom_call" | custom-call | flops 1000000 | bytes 100000 | tf_op jit(solution)/shard_map/early_grad/pallas_call | solution.py:734
  228.8 7.8 %z_grad.1.grad_z = f32[1536,256]{1,0:T(8,128)} custom-call(bf16[8,256,768]{2,1,0:T(8,128)(2,1)} %copy-done.2, bf16[4,2,2,96,6400]{4,3,2,1,0:T(8,128)(2,1)} %bitcast.66), custom_call_target="tpu_custom_call" | custom-call | flops 1000000 | bytes 100000 | tf_op jit(solution)/shard_map/z_grad/pallas_call | solution.py:807
  236.6 19.0 %all-to-all-done.2.parts = f32[8,32,2048]{2,1,0:T(8,128)S(1)} async-done(((f32[8,32,2048]{2,1,0:T(8,128)}), f32[8,32,2048]{2,1,0:T(8,128)S(1)}, u32[]{:S(2)}, u32[]{:S(2)}) %all-to-all-start.2) | async-done | bytes 2097184 | tf_op jit(solution)/shard_map/all_to_all | solution.py:120
  256.9 6.8 %rest_backward.1 = (bf16[2048,512]{1,0:T(8,128)(2,1)}, f32[8,512]{1,0:T(8,128)}) custom-call(s32[3]{0:T(128)} %bitcast.95, f32[8,32,2048]{2,1,0:T(8,128)} %copy-done.5, f32[2048,640]{1,0:T(8,128)} %get-tuple-element.149.pre_in.pre_b.pre_c, f32[2048,640]{1,0:T(8,128)} %get-tuple-element.149.pre_in.pre_b.pre_c, ...), custom_call_target="tpu_custom_call" | custom-call | flops 1000000 | bytes 100000 | tf_op jit(solution)/shard_map/rest_backward/pallas_call | solution.py:959
  263.7 8.9 %tail_grad.1 = f32[16,104,512]{2,1,0:T(8,128)} custom-call(bf16[2048,1536]{1,0:T(8,128)(2,1)} %get-tuple-element.156.normed, bf16[2048,512]{1,0:T(8,128)(2,1)} %get-tuple-element.173.tail, f32[8,512]{1,0:T(8,128)} %get-tuple-element.169.small), custom_call_target="tpu_custom_call" | custom-call | flops 1000000 | bytes 100000 | tf_op jit(solution)/shard_map/tail_grad/pallas_call | solution.py:1005
  283.4 20.1 %collective-permute-done.20 = f32[96,384]{1,0:T(8,128)S(1)} collective-permute-done((f32[96,384]{1,0:T(8,128)S(1)}, f32[96,384]{1,0:T(8,128)S(1)}, u32[]{:S(2)}, u32[]{:S(2)}) %collective-permute-start.20) | collective-permute-done | bytes 147488 | tf_op jit(solution)/shard_map/ppermute | solution.py:56
  314.1 11.2 %input_grad.1 = (f32[256,1536]{1,0:T(8,128)}, f32[8,512]{1,0:T(8,128)}) custom-call(s32[1]{0:T(128)} %bitcast.22.own_half, f32[1536,256]{1,0:T(8,128)} %z_grad.1.grad_z, bf16[8,256,512]{2,1,0:T(8,128)(2,1)} %copy-done.4, bf16[8,256,512]{2,1,0:T(8,128)(2,1)} %copy-done.4, bf16[4,2,2,96,6400]{4,3,2,1,0:T(8,128)(2,1)} %bitcast.67, ...), custom_call_target="tpu_custom_call" | custom-call | flops 1000000 | bytes 100000 | tf_op jit(solution)/shard_map/input_grad/pallas_call | solution.py:874
  337.8 10.9 %collective-permute-done.27 = f32[8,512]{1,0:T(8,128)S(1)} collective-permute-done((f32[8,512]{1,0:T(8,128)S(1)}, f32[8,512]{1,0:T(8,128)S(1)}, u32[]{:S(2)}, u32[]{:S(2)}) %collective-permute-start.27) | collective-permute-done | bytes 16416 | tf_op jit(solution)/shard_map/ppermute | solution.py:56
  351.2 4.6 %all-to-all-start.5 = ((f32[8,112,512]{2,1,0:T(8,128)}), f32[8,112,512]{2,1,0:T(8,128)S(1)}, u32[]{:S(2)}, u32[]{:S(2)}) async-start(f32[8,112,512]{2,1,0:T(8,128)} %broadcast_in_dim.67), calls=%async_computation.7 | async-start | bytes 3670016 | tf_op jit(solution)/shard_map/all_to_all | solution.py:120
  356.6 8.1 %block_out.1 = f32[256,1536]{1,0:T(8,128)} custom-call(bf16[8,256,768]{2,1,0:T(8,128)(2,1)} %copy-done.2, bf16[4,2,2,192,1536]{4,3,2,1,0:T(8,128)(2,1)} %bitcast.70, bf16[256,1536]{1,0:T(8,128)(2,1)} %tokens.3, f32[256,1]{1,0:T(8,128)} %fusion.1.live), custom_call_target="tpu_custom_call" | custom-call | flops 2400000000 | bytes 20000000 | tf_op jit(solution)/shard_map/block_out/pallas_call | solution.py:767
  364.8 5.7 %adam.2 = (f32[96,6400]{1,0:T(8,128)}, f32[96,6400]{1,0:T(8,128)}, f32[96,6400]{1,0:T(8,128)}, f32[96,6400]{1,0:T(8,128)}) custom-call(f32[8,192,384]{2,1,0:T(8,128)} %all-to-all-done.4.pair, f32[96,6400]{1,0:T(8,128)} %refs_0_.6, f32[96,6400]{1,0:T(8,128)} %refs_1_.4, f32[96,6400]{1,0:T(8,128)} %refs_2_.4), custom_call_target="tpu_custom_call" | custom-call | flops 2400000000 | bytes 20000000 | tf_op jit(solution)/shard_map/adam/pallas_call | solution.py:1043
  370.5 5.3 %adam.3 = (f32[192,1536]{1,0:T(8,128)}, f32[192,1536]{1,0:T(8,128)}, f32[192,1536]{1,0:T(8,128)}, f32[192,1536]{1,0:T(8,128)}) custom-call(f32[8,192,384]{2,1,0:T(8,128)} %all-to-all-done.4.pair, f32[192,1536]{1,0:T(8,128)} %refs_0_.7, f32[192,1536]{1,0:T(8,128)} %refs_1_.5, f32[192,1536]{1,0:T(8,128)} %refs_2_.5), custom_call_target="tpu_custom_call" | custom-call | flops 2400000000 | bytes 20000000 | tf_op jit(solution)/shard_map/adam/pallas_call | solution.py:1043
  375.9 7.1 %all-to-all-done.5.pair.rest = f32[8,112,512]{2,1,0:T(8,128)S(1)} async-done(((f32[8,112,512]{2,1,0:T(8,128)}), f32[8,112,512]{2,1,0:T(8,128)S(1)}, u32[]{:S(2)}, u32[]{:S(2)}) %all-to-all-start.5) | async-done | bytes 1835040 | tf_op jit(solution)/shard_map/all_to_all | solution.py:120
  385.6 6.9 %adam_tail.1 = (f32[96,6400]{1,0:T(8,128)}, f32[96,6400]{1,0:T(8,128)}, f32[96,6400]{1,0:T(8,128)}, f32[96,6400]{1,0:T(8,128)}) custom-call(f32[8,112,512]{2,1,0:T(8,128)} %copy-done.3, f32[8,112,512]{2,1,0:T(8,128)} %copy-done.3, f32[96,6400]{1,0:T(8,128)} %refs_0_.6, ...), custom_call_target="tpu_custom_call", output_to_operand_aliasing={{0}: (5, {}), {1}: (6, {}), {2}: (7, {}), {3}: (8, {})} | custom-call | flops 1000000 | bytes 100000 | tf_op jit(solution)/shard_map/adam_tail/pallas_call | solution.py:1086
  (223 shorter events, 117.3 us)
Async XLA Ops:
  7.2 57.9 %all-gather.4.cloned.1.call-start = ((), (), s32[]{:S(2)}) async-start(), calls=%async_computation.8 | async-start | bytes 4644864 | tf_op jit(solution)/shard_map/all_gather | solution.py:115
  7.3 20.8 %collective-permute-start = (bf16[256,1536]{1,0:T(8,128)(2,1)}, bf16[256,1536]{1,0:T(8,128)(2,1)}, u32[]{:S(2)}, u32[]{:S(2)}) collective-permute-start(bf16[256,1536]{1,0:T(8,128)(2,1)} %tokens.3), channel_id=1, source_target_pairs={{0,2},{1,3},{2,4},{3,5},{4,6},{5,7},{6,0},{7,1},{8,10},{9,11},{10,... | collective-permute-start | bytes 2359304 | tf_op jit(solution)/shard_map/ppermute | solution.py:56
  8.9 19.3 %collective-permute-start.1 = (bf16[256,1536]{1,0:T(8,128)(2,1)}, bf16[256,1536]{1,0:T(8,128)(2,1)}, u32[]{:S(2)}, u32[]{:S(2)}) collective-permute-start(bf16[256,1536]{1,0:T(8,128)(2,1)} %tokens.3), channel_id=1, source_target_pairs={{0,6},{1,7},{2,0},{3,1},{4,2},{5,3},{6,4},{7,5},{8,14},{9,15},{10,... | collective-permute-start | bytes 2359304 | tf_op jit(solution)/shard_map/ppermute | solution.py:56
  10.6 19.0 %collective-permute-start.2 = (bf16[256,1536]{1,0:T(8,128)(2,1)}, bf16[256,1536]{1,0:T(8,128)(2,1)}, u32[]{:S(2)}, u32[]{:S(2)}) collective-permute-start(bf16[256,1536]{1,0:T(8,128)(2,1)} %tokens.3), channel_id=1, source_target_pairs={{0,1},{1,0},{2,3},{3,2},{4,5},{5,4},{6,7},{7,6},{8,9},{9,8},{10,11... | collective-permute-start | bytes 2359304 | tf_op jit(solution)/shard_map/ppermute | solution.py:56
  31.6 101.4 %all-gather.6.cloned.1.call-start = ((), (), s32[]{:S(2)}) async-start(), calls=%async_computation.9 | async-start | bytes 10616832 | tf_op jit(solution)/shard_map/all_gather | solution.py:115
  31.7 19.3 %collective-permute-start.4 = (bf16[256,1536]{1,0:T(8,128)(2,1)}, bf16[256,1536]{1,0:T(8,128)(2,1)S(1)}, u32[]{:S(2)}, u32[]{:S(2)}) collective-permute-start(bf16[256,1536]{1,0:T(8,128)(2,1)} %collective-permute-done.refs_7_), channel_id=1, source_target_pairs={{0,2},{1,3},{2,4},{3,5},{4,6},{5,7},{6,0},{7,1},{8,10},{9,11},{10,... | collective-permute-start | bytes 2359304 | tf_op jit(solution)/shard_map/ppermute | solution.py:56
  32.1 18.8 %collective-permute-start.5 = (bf16[256,1536]{1,0:T(8,128)(2,1)}, bf16[256,1536]{1,0:T(8,128)(2,1)S(1)}, u32[]{:S(2)}, u32[]{:S(2)}) collective-permute-start(bf16[256,1536]{1,0:T(8,128)(2,1)} %collective-permute-done.refs_7_), channel_id=1, source_target_pairs={{0,1},{1,0},{2,3},{3,2},{4,5},{5,4},{6,7},{7,6},{8,9},{9,8},{10,11... | collective-permute-start | bytes 2359304 | tf_op jit(solution)/shard_map/ppermute | solution.py:56
  65.1 163.7 %all-gather.8.cloned.1.call-start = ((), (), s32[]{:S(2)}) async-start(), calls=%async_computation.11 | async-start | bytes 22118400 | tf_op jit(solution)/shard_map/all_gather | solution.py:115
  65.7 26.0 %collective-permute-start.8 = (bf16[256,1536]{1,0:T(8,128)(2,1)S(1)}, bf16[256,1536]{1,0:T(8,128)(2,1)}, u32[]{:S(2)}, u32[]{:S(2)}) collective-permute-start(bf16[256,1536]{1,0:T(8,128)(2,1)S(1)} %multiply_convert_fusion.refs_0_), channel_id=1, source_target_pairs={{0,2},{1,3},{2,4},{3,5},{4,6},{5,7},{6,0},{7,1},{8,10},{9,11},{10,... | collective-permute-start | bytes 2359304 | tf_op jit(solution)/shard_map/ppermute | solution.py:56
  67.2 24.5 %collective-permute-start.9 = (bf16[256,1536]{1,0:T(8,128)(2,1)S(1)}, bf16[256,1536]{1,0:T(8,128)(2,1)S(1)}, u32[]{:S(2)}, u32[]{:S(2)}) collective-permute-start(bf16[256,1536]{1,0:T(8,128)(2,1)S(1)} %multiply_convert_fusion.refs_0_), channel_id=1, source_target_pairs={{0,6},{1,7},{2,0},{3,1},{4,2},{5,3},{6,4},{7,5},{8,14},{9,15},{10,... | collective-permute-start | bytes 2359304 | tf_op jit(solution)/shard_map/ppermute | solution.py:56
  68.9 22.8 %collective-permute-start.10 = (bf16[256,1536]{1,0:T(8,128)(2,1)S(1)}, bf16[256,1536]{1,0:T(8,128)(2,1)}, u32[]{:S(2)}, u32[]{:S(2)}) collective-permute-start(bf16[256,1536]{1,0:T(8,128)(2,1)S(1)} %multiply_convert_fusion.refs_0_), channel_id=1, source_target_pairs={{0,1},{1,0},{2,3},{3,2},{4,5},{5,4},{6,7},{7,6},{8,9},{9,8},{10,11... | collective-permute-start | bytes 2359304 | tf_op jit(solution)/shard_map/ppermute | solution.py:56
  70.4 57.6 %collective-permute-start.16 = (bf16[96,6400]{1,0:T(8,128)(2,1)S(1)}, bf16[96,6400]{1,0:T(8,128)(2,1)}, u32[]{:S(2)}, u32[]{:S(2)}) collective-permute-start(bf16[96,6400]{1,0:T(8,128)(2,1)S(1)} %convert_element_type.48), channel_id=1, source_target_pairs={{0,65},{1,64},{2,67},{3,66},{4,69},{5,68},{6,71},{7,70},{8,73},{9,... | collective-permute-start | bytes 3686408 | tf_op jit(solution)/shard_map/ppermute | solution.py:56
  91.7 19.9 %collective-permute-start.13 = (bf16[256,1536]{1,0:T(8,128)(2,1)}, bf16[256,1536]{1,0:T(8,128)(2,1)}, u32[]{:S(2)}, u32[]{:S(2)}) collective-permute-start(bf16[256,1536]{1,0:T(8,128)(2,1)} %collective-permute-done.8.refs_7_), channel_id=1, source_target_pairs={{0,2},{1,3},{2,4},{3,5},{4,6},{5,7},{6,0},{7,1},{8,10},{9,11},{10,... | collective-permute-start | bytes 2359304 | tf_op jit(solution)/shard_map/ppermute | solution.py:56
  92.6 19.1 %collective-permute-start.14 = (bf16[256,1536]{1,0:T(8,128)(2,1)}, bf16[256,1536]{1,0:T(8,128)(2,1)S(1)}, u32[]{:S(2)}, u32[]{:S(2)}) collective-permute-start(bf16[256,1536]{1,0:T(8,128)(2,1)} %collective-permute-done.8.refs_7_), channel_id=1, source_target_pairs={{0,1},{1,0},{2,3},{3,2},{4,5},{5,4},{6,7},{7,6},{8,9},{9,8},{10,11... | collective-permute-start | bytes 2359304 | tf_op jit(solution)/shard_map/ppermute | solution.py:56
  93.0 18.7 %collective-permute-start.15 = (bf16[256,1536]{1,0:T(8,128)(2,1)}, bf16[256,1536]{1,0:T(8,128)(2,1)S(1)}, u32[]{:S(2)}, u32[]{:S(2)}) collective-permute-start(bf16[256,1536]{1,0:T(8,128)(2,1)} %collective-permute-done.10.refs_1_), channel_id=1, source_target_pairs={{0,6},{1,7},{2,0},{3,1},{4,2},{5,3},{6,4},{7,5},{8,14},{9,15},{10,... | collective-permute-start | bytes 2359304 | tf_op jit(solution)/shard_map/ppermute | solution.py:56
  168.9 42.6 %all-to-all-start.1 = ((bf16[8,256,768]{2,1,0:T(8,128)(2,1)}), bf16[8,256,768]{2,1,0:T(8,128)(2,1)S(1)}, u32[]{:S(2)}, u32[]{:S(2)}) async-start(bf16[8,256,768]{2,1,0:T(8,128)(2,1)} %bitcast.73), calls=%async_computation.1 | async-start | bytes 6291456 | tf_op jit(solution)/shard_map/all_to_all | solution.py:120
  172.6 100.0 %reduce-scatter.3.cloned.1.call-start = ((), (), s32[]{:S(2)}) async-start(), calls=%async_computation.10 | async-start | bytes 5308416 | tf_op jit(solution)/shard_map/reduce_scatter | solution.py:135
  225.1 30.5 %all-to-all-start.2 = ((f32[8,32,2048]{2,1,0:T(8,128)}), f32[8,32,2048]{2,1,0:T(8,128)S(1)}, u32[]{:S(2)}, u32[]{:S(2)}) async-start(f32[8,32,2048]{2,1,0:T(8,128)} %bitcast.78), calls=%async_computation.3 | async-start | bytes 4194304 | tf_op jit(solution)/shard_map/all_to_all | solution.py:120
  228.8 96.5 %reduce-scatter.5.cloned.1.call-start = ((), (), s32[]{:S(2)}) async-start(), calls=%async_computation.12 | async-start | bytes 3833856 | tf_op jit(solution)/shard_map/reduce_scatter | solution.py:135
  272.6 35.0 %all-to-all-start.3 = ((bf16[8,256,512]{2,1,0:T(8,128)(2,1)}), bf16[8,256,512]{2,1,0:T(8,128)(2,1)S(1)}, u32[]{:S(2)}, u32[]{:S(2)}) async-start(bf16[8,256,512]{2,1,0:T(8,128)(2,1)} %bitcast.74), calls=%async_computation.5 | async-start | bytes 4194304 | tf_op jit(solution)/shard_map/all_to_all | solution.py:120
  277.4 26.1 %collective-permute-start.20 = (f32[96,384]{1,0:T(8,128)S(1)}, f32[96,384]{1,0:T(8,128)S(1)}, u32[]{:S(2)}, u32[]{:S(2)}) collective-permute-start(f32[96,384]{1,0:T(8,128)S(1)} %get-tuple-element.221), channel_id=1, source_target_pairs={{0,2},{1,18},{2,34},{3,50},{4,66},{5,82},{6,98},{7,114},{8,6},{9,2... | collective-permute-start | bytes 442376 | tf_op jit(solution)/shard_map/ppermute | solution.py:56
  280.5 27.2 %collective-permute-start.21 = (f32[96,384]{1,0:T(8,128)S(1)}, f32[96,384]{1,0:T(8,128)S(1)}, u32[]{:S(2)}, u32[]{:S(2)}) collective-permute-start(f32[96,384]{1,0:T(8,128)S(1)} %get-tuple-element.220), channel_id=1, source_target_pairs={{0,64},{1,65},{2,66},{3,67},{4,68},{5,69},{6,70},{7,71},{8,72},{9,... | collective-permute-start | bytes 442376 | tf_op jit(solution)/shard_map/ppermute | solution.py:56
  309.7 40.0 %all-to-all-start.4 = ((f32[8,192,384]{2,1,0:T(8,128)}), f32[8,192,384]{2,1,0:T(8,128)}, u32[]{:S(2)}, u32[]{:S(2)}) async-start(f32[8,192,384]{2,1,0:T(8,128)} %broadcast_in_dim.65), calls=%async_computation.6 | async-start | bytes 4718592 | tf_op jit(solution)/shard_map/all_to_all | solution.py:120
  351.2 31.8 %all-to-all-start.5 = ((f32[8,112,512]{2,1,0:T(8,128)}), f32[8,112,512]{2,1,0:T(8,128)S(1)}, u32[]{:S(2)}, u32[]{:S(2)}) async-start(f32[8,112,512]{2,1,0:T(8,128)} %broadcast_in_dim.67), calls=%async_computation.7 | async-start | bytes 3670016 | tf_op jit(solution)/shard_map/all_to_all | solution.py:120
  (39 other events, 403.1 us)
Sparse Core Ops, SparseCore 0:
  31.7 33.3 all-gather.3
  67.4 54.1 all-gather.5
  131.3 94.8 all-gather.7
  228.4 40.0 reduce-scatter.2
  272.7 37.2 reduce-scatter.4

commit v5 on v3

--- a/solution.py
+++ b/solution.py
@@ -1259,9 +1259,8 @@
     grad_tail = run_tail_grad(normed, tail, small_own)
     tail, grad_tail, low_rows = lax.optimization_barrier((tail, grad_tail, low_rows))
     tail_rows = exchange(tail.reshape(N_REP, ROWS, TAIL), "rep")
+    early, grad_tail = lax.optimization_barrier((early, grad_tail))
     tail_part = scatter_eight(grad_tail)
-    block_out = run_block_out(low_rows, full_out, tokens, own_live)
-    early, block_out = lax.optimization_barrier((early, block_out))
     mine, other = at(early, place.yh), at(early, 1 - place.yh)
     out_mine = move(
         mine[:SHARD_IN], lambda yh, z, c, x, yl: (x // 2, (x % 2) * 2 + yl, z % 2, 2 * c + yh, z // 2)
@@ -1284,8 +1283,9 @@
     grad_gain_in = grad_gain_in + move(grad_gain_in, swap_y_hi)
     tail_part = jnp.concatenate([tail_part, grad_gain_in], 0)
 
-    tail_part, early_parts = lax.optimization_barrier((tail_part, early_parts))
+    tail_part, early_parts, low_rows = lax.optimization_barrier((tail_part, early_parts, low_rows))
     tail_parts = share_rep(tail_part)
+    block_out = run_block_out(low_rows, full_out, tokens, own_live)
 
     grad_out, new_first_out, new_second_out, new_out = run_adam_early(
         lambda i: (i // 2, i % 2), slice(0, SHARD_IN), early_parts, w_out, first_out, second_out

time: 393 us -> 401 us (1.020)
  waiting for transfers between devices: 85.8 us -> 92.3 us
    ppermute x28, waiting for transfers between devices: 49.8 us -> 63.7 us  [move(): return lax.ppermute(value, ('fsdp', 'rep'), pairs)]
    all_to_all x5, waiting for transfers between devices: 31.9 us -> 21.6 us  [exchange(): return lax.all_to_all(value, axis, 0, 0, tiled=True)]
  transfers between devices with their start and end apart: 38 -> 38, of which waited for: 18 -> 18; matrix products, arithmetic and copies ran while one was open for 7% -> 6% of each run, Pallas kernels for 42% -> 41%
where the time goes in v5:
time: 401 us; the launch traced here: 398 us
  Pallas kernels  171 us (43%)
  waiting for transfers between devices  92.3 us (23%)
  starting transfers between devices  73.2 us (18%)
  local copies, waits for them, and re-layouts  20.7 us (5%)
  other arithmetic  16.3 us (4%)
  between operations  14.5 us (4%)
  blocking collectives  10.2 us (3%)
    ppermute x28, waiting for transfers between devices, move(): return lax.ppermute(value, ('fsdp', 'rep'), pairs)  63.7 us
    ppermute x28, starting transfers between devices, move(): return lax.ppermute(value, ('fsdp', 'rep'), pairs)  48 us
    pallas_call x1, Pallas kernels, run_backward(): pl.pallas_call(backward_kernel, grid=(CHUNKS,), in_specs=[pl.BlockSpec(me...  32.1 us
    all_to_all x5, starting transfers between devices, exchange(): return lax.all_to_all(value, axis, 0, 0, tiled=True)  25 us
    pallas_call x2, Pallas kernels, run_forward(): pl.pallas_call(partial(forward_kernel, part), grid=(HALF,), in_specs=[pl....  24.2 us
    all_to_all x5, waiting for transfers between devices, exchange(): return lax.all_to_all(value, axis, 0, 0, tiled=True)  21.6 us
    pallas_call x1, Pallas kernels, run_project(): pl.pallas_call(partial(project_kernel, PARTS), grid_spec=pltpu.PrefetchSc...  17.4 us
    pallas_call x1, Pallas kernels, run_out_grad(): pl.pallas_call(out_grad_kernel, grid_spec=pltpu.PrefetchScalarGridSpec(nu...  13.6 us
  transfers between devices with their start and end apart: 38, of which 18 were waited for; matrix products, arithmetic and copies ran while one was open for 6% of the time, Pallas kernels for 41%

profile of v5, /device:TPU:0, one launch (start us, length us, event | category | flops | bytes accessed | tf_op | source)
XLA Modules:
  0.0 398.5 jit_solution(2349155432858402719)
XLA Ops:
  38.8 11.8 %collective-permute-done.7 = bf16[192,1536]{1,0:T(8,128)(2,1)S(1)} collective-permute-done((bf16[192,1536]{1,0:T(8,128)(2,1)S(1)}, bf16[192,1536]{1,0:T(8,128)(2,1)S(1)}, u32[]{:S(2)}, u32[]{:S(2)}) %collective-permute-start.7) | collective-permute-done | bytes 589856 | tf_op jit(solution)/shard_map/ppermute | solution.py:56
  74.3 17.4 %project.1 = (bf16[2048,1536]{1,0:T(8,128)(2,1)}, f32[2048,1152]{1,0:T(8,128)}, bf16[1536,128]{1,0:T(8,128)(2,1)}) custom-call(s32[8]{0:T(128)} %fusion.5.table, bf16[256,1536]{1,0:T(8,128)(2,1)} %tokens.3, bf16[256,1536]{1,0:T(8,128)(2,1)} %collective-permute-done.2.refs_1_, bf16[256,1536]{1,0:T(8,128)(2,1)} %collective-permute-done.1.refs_2_, ...), custom_call_target="tpu_custom_call" | custom-call | flops 1000000 | bytes 100000 | tf_op jit(solution)/shard_map/project/pallas_call | solution.py:578
  97.1 12.1 %scan_forward.2 = (f32[2048,640]{1,0:T(8,128)}, f32[2048,384]{1,0:T(8,128)}, f32[2048,384]{1,0:T(8,128)}, f32[136,640]{1,0:T(8,128)}) custom-call(s32[3]{0:T(128)} %bitcast.92, f32[2048,1152]{1,0:T(8,128)} %get-tuple-element.128.proj.refs_11_.gate_in.conv_in.dt_in, f32[16,640]{1,0:T(8,128)} %concatenate.39.par), custom_call_target="tpu_custom_call" | custom-call | flops 1000000 | bytes 100000 | tf_op jit(solution)/shard_map/scan_forward/pallas_call | solution.py:349
  115.8 12.2 %scan_forward.3 = (f32[2048,640]{1,0:T(8,128)}, f32[2048,384]{1,0:T(8,128)}, f32[2048,384]{1,0:T(8,128)}, f32[136,640]{1,0:T(8,128)}) custom-call(s32[3]{0:T(128)} %bitcast.93, f32[2048,1152]{1,0:T(8,128)} %get-tuple-element.128.proj.refs_11_.gate_in.conv_in.dt_in, ...), custom_call_target="tpu_custom_call", output_to_operand_aliasing={{0}: (3, {}), {1}: (4, {}), {2}: (5, {})} | custom-call | flops 1000000 | bytes 100000 | tf_op jit(solution)/shard_map/scan_forward/pallas_call | solution.py:349
  133.0 13.6 %out_grad.1 = (bf16[2048,1536]{1,0:T(8,128)(2,1)}, f32[2048,384]{1,0:T(8,128)}, f32[8,2048]{1,0:T(8,128)}) custom-call(s32[9]{0:T(128)} %pad_add_fusion.table, bf16[256,1536]{1,0:T(8,128)(2,1)} %copy-done.6, bf16[256,1536]{1,0:T(8,128)(2,1)} %collective-permute-done.10.refs_1_, bf16[256,1536]{1,0:T(8,128)(2,1)} %copy-done.12, bf16[256,1536]{1,0:T(8,128)(2,1)} %copy-done.9, ...), custom_call_target="tpu_custom_call" | custom-call | flops 1000000 | bytes 100000 | tf_op jit(solution)/shard_map/out_grad/pallas_call | solution.py:635
  147.5 10.2 %all_to_all.34 = f32[8,32,128]{2,1,0:T(8,128)S(1)} all-to-all(f32[8,32,128]{2,1,0:T(8,128)S(1)} %broadcast_in_dim.62), channel_id=1, replica_groups=mesh['fsdp'=16,'rep'=8] {'rep'}, dimensions={0} | all-to-all | bytes 262144 | tf_op jit(solution)/shard_map/all_to_all | solution.py:120
  158.4 10.5 %gate_backward.1 = (bf16[2048,768]{1,0:T(8,128)(2,1)}, f32[2048,384]{1,0:T(8,128)}, f32[8,384]{1,0:T(8,128)}) custom-call(f32[2048,384]{1,0:T(8,128)} %get-tuple-element.147.grad_out, f32[2048,384]{1,0:T(8,128)} %get-tuple-element.146.refs_10_.mixed_in, f32[2048,1152]{1,0:T(8,128)} %get-tuple-element.128.proj.refs_11_.gate_in.conv_in.dt_in, ...), custom_call_target="tpu_custom_call" | custom-call | flops 1000000 | bytes 100000 | tf_op jit(solution)/shard_map/gate_backward/pallas_call | solution.py:690
  172.6 32.1 %scan_backward.1 = (bf16[2048,384]{1,0:T(8,128)(2,1)}, bf16[2048,128]{1,0:T(8,128)(2,1)}, f32[256,2048]{1,0:T(8,128)}, f32[8,384]{1,0:T(8,128)}, f32[8,128]{1,0:T(8,128)}) custom-call(s32[3]{0:T(128)} %bitcast.94, f32[2048,1152]{1,0:T(8,128)} %get-tuple-element.128.proj.refs_11_.gate_in.conv_in.dt_in, ...), custom_call_target="tpu_custom_call" | custom-call | flops 1000000 | bytes 100000 | tf_op jit(solution)/shard_map/scan_backward/pallas_call | solution.py:477
  204.7 12.7 %early_grad.1 = f32[16,192,384]{2,1,0:T(8,128)} custom-call(bf16[2048,768]{1,0:T(8,128)(2,1)} %get-tuple-element.154.low, bf16[2048,1536]{1,0:T(8,128)(2,1)} %get-tuple-element.155.grad_branch, bf16[2048,1536]{1,0:T(8,128)(2,1)} %get-tuple-element.156.normed), custom_call_target="tpu_custom_call" | custom-call | flops 1000000 | bytes 100000 | tf_op jit(solution)/shard_map/early_grad/pallas_call | solution.py:734
  219.1 5.4 %all-to-all-start.2 = ((f32[8,32,2048]{2,1,0:T(8,128)}), f32[8,32,2048]{2,1,0:T(8,128)S(1)}, u32[]{:S(2)}, u32[]{:S(2)}) async-start(f32[8,32,2048]{2,1,0:T(8,128)} %bitcast.78), calls=%async_computation.3 | async-start | bytes 4194304 | tf_op jit(solution)/shard_map/all_to_all | solution.py:120
  226.2 7.8 %z_grad.1.grad_z = f32[1536,256]{1,0:T(8,128)} custom-call(bf16[8,256,768]{2,1,0:T(8,128)(2,1)} %copy-done.2, bf16[4,2,2,96,6400]{4,3,2,1,0:T(8,128)(2,1)} %bitcast.66), custom_call_target="tpu_custom_call" | custom-call | flops 2400000000 | bytes 20000000 | tf_op jit(solution)/shard_map/z_grad/pallas_call | solution.py:807
  233.9 14.5 %all-to-all-done.2.parts = f32[8,32,2048]{2,1,0:T(8,128)S(1)} async-done(((f32[8,32,2048]{2,1,0:T(8,128)}), f32[8,32,2048]{2,1,0:T(8,128)S(1)}, u32[]{:S(2)}, u32[]{:S(2)}) %all-to-all-start.2) | async-done | bytes 2097184 | tf_op jit(solution)/shard_map/all_to_all | solution.py:120
  249.8 6.8 %rest_backward.1 = (bf16[2048,512]{1,0:T(8,128)(2,1)}, f32[8,512]{1,0:T(8,128)}) custom-call(s32[3]{0:T(128)} %bitcast.95, f32[8,32,2048]{2,1,0:T(8,128)} %copy-done.5, f32[2048,640]{1,0:T(8,128)} %get-tuple-element.150.pre_in.pre_b.pre_c, f32[2048,640]{1,0:T(8,128)} %get-tuple-element.150.pre_in.pre_b.pre_c, ...), custom_call_target="tpu_custom_call" | custom-call | flops 1000000 | bytes 100000 | tf_op jit(solution)/shard_map/rest_backward/pallas_call | solution.py:959
  256.6 8.9 %tail_grad.1 = f32[16,104,512]{2,1,0:T(8,128)} custom-call(bf16[2048,1536]{1,0:T(8,128)(2,1)} %get-tuple-element.156.normed, bf16[2048,512]{1,0:T(8,128)(2,1)} %get-tuple-element.175.tail, f32[8,512]{1,0:T(8,128)} %get-tuple-element.171.small), custom_call_target="tpu_custom_call" | custom-call | flops 1000000 | bytes 100000 | tf_op jit(solution)/shard_map/tail_grad/pallas_call | solution.py:1005
  268.4 5.2 %all-to-all-start.3 = ((bf16[8,256,512]{2,1,0:T(8,128)(2,1)}), bf16[8,256,512]{2,1,0:T(8,128)(2,1)S(1)}, u32[]{:S(2)}, u32[]{:S(2)}) async-start(bf16[8,256,512]{2,1,0:T(8,128)(2,1)} %bitcast.74), calls=%async_computation.5 | async-start | bytes 4194304 | tf_op jit(solution)/shard_map/all_to_all | solution.py:120
  280.7 19.3 %collective-permute-done.20 = f32[96,384]{1,0:T(8,128)S(1)} collective-permute-done((f32[96,384]{1,0:T(8,128)S(1)}, f32[96,384]{1,0:T(8,128)S(1)}, u32[]{:S(2)}, u32[]{:S(2)}) %collective-permute-start.20) | collective-permute-done | bytes 147488 | tf_op jit(solution)/shard_map/ppermute | solution.py:56
  306.5 5.9 %all-to-all-start.4 = ((f32[8,192,384]{2,1,0:T(8,128)}), f32[8,192,384]{2,1,0:T(8,128)}, u32[]{:S(2)}, u32[]{:S(2)}) async-start(f32[8,192,384]{2,1,0:T(8,128)} %broadcast_in_dim.65), calls=%async_computation.6 | async-start | bytes 4718592 | tf_op jit(solution)/shard_map/all_to_all | solution.py:120
  312.5 11.1 %input_grad.1 = (f32[256,1536]{1,0:T(8,128)}, f32[8,512]{1,0:T(8,128)}) custom-call(s32[1]{0:T(128)} %bitcast.22.own_half, f32[1536,256]{1,0:T(8,128)} %z_grad.1.grad_z, bf16[8,256,512]{2,1,0:T(8,128)(2,1)} %copy-done.4, bf16[8,256,512]{2,1,0:T(8,128)(2,1)} %copy-done.4, bf16[4,2,2,96,6400]{4,3,2,1,0:T(8,128)(2,1)} %bitcast.67, ...), custom_call_target="tpu_custom_call" | custom-call | flops 1000000 | bytes 100000 | tf_op jit(solution)/shard_map/input_grad/pallas_call | solution.py:874
  338.7 9.2 %collective-permute-done.27 = f32[8,512]{1,0:T(8,128)S(1)} collective-permute-done((f32[8,512]{1,0:T(8,128)S(1)}, f32[8,512]{1,0:T(8,128)S(1)}, u32[]{:S(2)}, u32[]{:S(2)}) %collective-permute-start.27) | collective-permute-done | bytes 16416 | tf_op jit(solution)/shard_map/ppermute | solution.py:56
  356.1 8.1 %block_out.1 = f32[256,1536]{1,0:T(8,128)} custom-call(bf16[8,256,768]{2,1,0:T(8,128)(2,1)} %copy-done.2, bf16[4,2,2,192,1536]{4,3,2,1,0:T(8,128)(2,1)} %bitcast.70, bf16[256,1536]{1,0:T(8,128)(2,1)} %tokens.3, f32[256,1]{1,0:T(8,128)} %fusion.1.live), custom_call_target="tpu_custom_call" | custom-call | flops 2400000000 | bytes 20000000 | tf_op jit(solution)/shard_map/block_out/pallas_call | solution.py:767
  364.2 5.7 %adam.2 = (f32[96,6400]{1,0:T(8,128)}, f32[96,6400]{1,0:T(8,128)}, f32[96,6400]{1,0:T(8,128)}, f32[96,6400]{1,0:T(8,128)}) custom-call(f32[8,192,384]{2,1,0:T(8,128)} %all-to-all-done.4.pair, f32[96,6400]{1,0:T(8,128)} %refs_0_.6, f32[96,6400]{1,0:T(8,128)} %refs_1_.4, f32[96,6400]{1,0:T(8,128)} %refs_2_.4), custom_call_target="tpu_custom_call" | custom-call | flops 2400000000 | bytes 20000000 | tf_op jit(solution)/shard_map/adam/pallas_call | solution.py:1043
  370.0 5.3 %adam.3 = (f32[192,1536]{1,0:T(8,128)}, f32[192,1536]{1,0:T(8,128)}, f32[192,1536]{1,0:T(8,128)}, f32[192,1536]{1,0:T(8,128)}) custom-call(f32[8,192,384]{2,1,0:T(8,128)} %all-to-all-done.4.pair, f32[192,1536]{1,0:T(8,128)} %refs_0_.7, f32[192,1536]{1,0:T(8,128)} %refs_1_.5, f32[192,1536]{1,0:T(8,128)} %refs_2_.5), custom_call_target="tpu_custom_call" | custom-call | flops 2400000000 | bytes 20000000 | tf_op jit(solution)/shard_map/adam/pallas_call | solution.py:1043
  375.3 7.1 %all-to-all-done.5.pair.rest = f32[8,112,512]{2,1,0:T(8,128)S(1)} async-done(((f32[8,112,512]{2,1,0:T(8,128)}), f32[8,112,512]{2,1,0:T(8,128)S(1)}, u32[]{:S(2)}, u32[]{:S(2)}) %all-to-all-start.5) | async-done | bytes 1835040 | tf_op jit(solution)/shard_map/all_to_all | solution.py:120
  385.1 6.9 %adam_tail.1 = (f32[96,6400]{1,0:T(8,128)}, f32[96,6400]{1,0:T(8,128)}, f32[96,6400]{1,0:T(8,128)}, f32[96,6400]{1,0:T(8,128)}) custom-call(f32[8,112,512]{2,1,0:T(8,128)} %copy-done.3, f32[8,112,512]{2,1,0:T(8,128)} %copy-done.3, f32[96,6400]{1,0:T(8,128)} %refs_0_.6, ...), custom_call_target="tpu_custom_call", output_to_operand_aliasing={{0}: (5, {}), {1}: (6, {}), {2}: (7, {}), {3}: (8, {})} | custom-call | flops 1000000 | bytes 100000 | tf_op jit(solution)/shard_map/adam_tail/pallas_call | solution.py:1086
  (223 shorter events, 124.2 us)
Async XLA Ops:
  7.2 57.9 %all-gather.4.cloned.1.call-start = ((), (), s32[]{:S(2)}) async-start(), calls=%async_computation.8 | async-start | bytes 4644864 | tf_op jit(solution)/shard_map/all_gather | solution.py:115
  7.3 20.8 %collective-permute-start = (bf16[256,1536]{1,0:T(8,128)(2,1)}, bf16[256,1536]{1,0:T(8,128)(2,1)}, u32[]{:S(2)}, u32[]{:S(2)}) collective-permute-start(bf16[256,1536]{1,0:T(8,128)(2,1)} %tokens.3), channel_id=1, source_target_pairs={{0,2},{1,3},{2,4},{3,5},{4,6},{5,7},{6,0},{7,1},{8,10},{9,11},{10,... | collective-permute-start | bytes 2359304 | tf_op jit(solution)/shard_map/ppermute | solution.py:56
  8.9 19.3 %collective-permute-start.1 = (bf16[256,1536]{1,0:T(8,128)(2,1)}, bf16[256,1536]{1,0:T(8,128)(2,1)}, u32[]{:S(2)}, u32[]{:S(2)}) collective-permute-start(bf16[256,1536]{1,0:T(8,128)(2,1)} %tokens.3), channel_id=1, source_target_pairs={{0,6},{1,7},{2,0},{3,1},{4,2},{5,3},{6,4},{7,5},{8,14},{9,15},{10,... | collective-permute-start | bytes 2359304 | tf_op jit(solution)/shard_map/ppermute | solution.py:56
  10.6 19.0 %collective-permute-start.2 = (bf16[256,1536]{1,0:T(8,128)(2,1)}, bf16[256,1536]{1,0:T(8,128)(2,1)}, u32[]{:S(2)}, u32[]{:S(2)}) collective-permute-start(bf16[256,1536]{1,0:T(8,128)(2,1)} %tokens.3), channel_id=1, source_target_pairs={{0,1},{1,0},{2,3},{3,2},{4,5},{5,4},{6,7},{7,6},{8,9},{9,8},{10,11... | collective-permute-start | bytes 2359304 | tf_op jit(solution)/shard_map/ppermute | solution.py:56
  31.6 101.4 %all-gather.6.cloned.1.call-start = ((), (), s32[]{:S(2)}) async-start(), calls=%async_computation.9 | async-start | bytes 10616832 | tf_op jit(solution)/shard_map/all_gather | solution.py:115
  31.7 19.3 %collective-permute-start.4 = (bf16[256,1536]{1,0:T(8,128)(2,1)}, bf16[256,1536]{1,0:T(8,128)(2,1)S(1)}, u32[]{:S(2)}, u32[]{:S(2)}) collective-permute-start(bf16[256,1536]{1,0:T(8,128)(2,1)} %collective-permute-done.refs_7_), channel_id=1, source_target_pairs={{0,2},{1,3},{2,4},{3,5},{4,6},{5,7},{6,0},{7,1},{8,10},{9,11},{10,... | collective-permute-start | bytes 2359304 | tf_op jit(solution)/shard_map/ppermute | solution.py:56
  32.1 18.8 %collective-permute-start.5 = (bf16[256,1536]{1,0:T(8,128)(2,1)}, bf16[256,1536]{1,0:T(8,128)(2,1)S(1)}, u32[]{:S(2)}, u32[]{:S(2)}) collective-permute-start(bf16[256,1536]{1,0:T(8,128)(2,1)} %collective-permute-done.refs_7_), channel_id=1, source_target_pairs={{0,1},{1,0},{2,3},{3,2},{4,5},{5,4},{6,7},{7,6},{8,9},{9,8},{10,11... | collective-permute-start | bytes 2359304 | tf_op jit(solution)/shard_map/ppermute | solution.py:56
  65.1 161.0 %all-gather.8.cloned.1.call-start = ((), (), s32[]{:S(2)}) async-start(), calls=%async_computation.11 | async-start | bytes 22118400 | tf_op jit(solution)/shard_map/all_gather | solution.py:115
  65.7 26.0 %collective-permute-start.8 = (bf16[256,1536]{1,0:T(8,128)(2,1)S(1)}, bf16[256,1536]{1,0:T(8,128)(2,1)}, u32[]{:S(2)}, u32[]{:S(2)}) collective-permute-start(bf16[256,1536]{1,0:T(8,128)(2,1)S(1)} %multiply_convert_fusion.refs_0_), channel_id=1, source_target_pairs={{0,2},{1,3},{2,4},{3,5},{4,6},{5,7},{6,0},{7,1},{8,10},{9,11},{10,... | collective-permute-start | bytes 2359304 | tf_op jit(solution)/shard_map/ppermute | solution.py:56
  67.2 24.5 %collective-permute-start.9 = (bf16[256,1536]{1,0:T(8,128)(2,1)S(1)}, bf16[256,1536]{1,0:T(8,128)(2,1)S(1)}, u32[]{:S(2)}, u32[]{:S(2)}) collective-permute-start(bf16[256,1536]{1,0:T(8,128)(2,1)S(1)} %multiply_convert_fusion.refs_0_), channel_id=1, source_target_pairs={{0,6},{1,7},{2,0},{3,1},{4,2},{5,3},{6,4},{7,5},{8,14},{9,15},{10,... | collective-permute-start | bytes 2359304 | tf_op jit(solution)/shard_map/ppermute | solution.py:56
  68.9 22.8 %collective-permute-start.10 = (bf16[256,1536]{1,0:T(8,128)(2,1)S(1)}, bf16[256,1536]{1,0:T(8,128)(2,1)}, u32[]{:S(2)}, u32[]{:S(2)}) collective-permute-start(bf16[256,1536]{1,0:T(8,128)(2,1)S(1)} %multiply_convert_fusion.refs_0_), channel_id=1, source_target_pairs={{0,1},{1,0},{2,3},{3,2},{4,5},{5,4},{6,7},{7,6},{8,9},{9,8},{10,11... | collective-permute-start | bytes 2359304 | tf_op jit(solution)/shard_map/ppermute | solution.py:56
  70.4 57.6 %collective-permute-start.16 = (bf16[96,6400]{1,0:T(8,128)(2,1)S(1)}, bf16[96,6400]{1,0:T(8,128)(2,1)}, u32[]{:S(2)}, u32[]{:S(2)}) collective-permute-start(bf16[96,6400]{1,0:T(8,128)(2,1)S(1)} %convert_element_type.48), channel_id=1, source_target_pairs={{0,65},{1,64},{2,67},{3,66},{4,69},{5,68},{6,71},{7,70},{8,73},{9,... | collective-permute-start | bytes 3686408 | tf_op jit(solution)/shard_map/ppermute | solution.py:56
  91.7 19.9 %collective-permute-start.13 = (bf16[256,1536]{1,0:T(8,128)(2,1)}, bf16[256,1536]{1,0:T(8,128)(2,1)}, u32[]{:S(2)}, u32[]{:S(2)}) collective-permute-start(bf16[256,1536]{1,0:T(8,128)(2,1)} %collective-permute-done.8.refs_7_), channel_id=1, source_target_pairs={{0,2},{1,3},{2,4},{3,5},{4,6},{5,7},{6,0},{7,1},{8,10},{9,11},{10,... | collective-permute-start | bytes 2359304 | tf_op jit(solution)/shard_map/ppermute | solution.py:56
  92.6 19.1 %collective-permute-start.14 = (bf16[256,1536]{1,0:T(8,128)(2,1)}, bf16[256,1536]{1,0:T(8,128)(2,1)S(1)}, u32[]{:S(2)}, u32[]{:S(2)}) collective-permute-start(bf16[256,1536]{1,0:T(8,128)(2,1)} %collective-permute-done.8.refs_7_), channel_id=1, source_target_pairs={{0,1},{1,0},{2,3},{3,2},{4,5},{5,4},{6,7},{7,6},{8,9},{9,8},{10,11... | collective-permute-start | bytes 2359304 | tf_op jit(solution)/shard_map/ppermute | solution.py:56
  93.0 18.7 %collective-permute-start.15 = (bf16[256,1536]{1,0:T(8,128)(2,1)}, bf16[256,1536]{1,0:T(8,128)(2,1)S(1)}, u32[]{:S(2)}, u32[]{:S(2)}) collective-permute-start(bf16[256,1536]{1,0:T(8,128)(2,1)} %collective-permute-done.10.refs_1_), channel_id=1, source_target_pairs={{0,6},{1,7},{2,0},{3,1},{4,2},{5,3},{6,4},{7,5},{8,14},{9,15},{10,... | collective-permute-start | bytes 2359304 | tf_op jit(solution)/shard_map/ppermute | solution.py:56
  168.9 48.5 %all-to-all-start.1 = ((bf16[8,256,768]{2,1,0:T(8,128)(2,1)}), bf16[8,256,768]{2,1,0:T(8,128)(2,1)S(1)}, u32[]{:S(2)}, u32[]{:S(2)}) async-start(bf16[8,256,768]{2,1,0:T(8,128)(2,1)} %bitcast.73), calls=%async_computation.1 | async-start | bytes 6291456 | tf_op jit(solution)/shard_map/all_to_all | solution.py:120
  172.6 95.8 %reduce-scatter.3.cloned.1.call-start = ((), (), s32[]{:S(2)}) async-start(), calls=%async_computation.10 | async-start | bytes 5308416 | tf_op jit(solution)/shard_map/reduce_scatter | solution.py:135
  219.1 29.4 %all-to-all-start.2 = ((f32[8,32,2048]{2,1,0:T(8,128)}), f32[8,32,2048]{2,1,0:T(8,128)S(1)}, u32[]{:S(2)}, u32[]{:S(2)}) async-start(f32[8,32,2048]{2,1,0:T(8,128)} %bitcast.78), calls=%async_computation.3 | async-start | bytes 4194304 | tf_op jit(solution)/shard_map/all_to_all | solution.py:120
  224.5 99.1 %reduce-scatter.5.cloned.1.call-start = ((), (), s32[]{:S(2)}) async-start(), calls=%async_computation.12 | async-start | bytes 3833856 | tf_op jit(solution)/shard_map/reduce_scatter | solution.py:135
  268.4 36.0 %all-to-all-start.3 = ((bf16[8,256,512]{2,1,0:T(8,128)(2,1)}), bf16[8,256,512]{2,1,0:T(8,128)(2,1)S(1)}, u32[]{:S(2)}, u32[]{:S(2)}) async-start(bf16[8,256,512]{2,1,0:T(8,128)(2,1)} %bitcast.74), calls=%async_computation.5 | async-start | bytes 4194304 | tf_op jit(solution)/shard_map/all_to_all | solution.py:120
  274.3 25.7 %collective-permute-start.20 = (f32[96,384]{1,0:T(8,128)S(1)}, f32[96,384]{1,0:T(8,128)S(1)}, u32[]{:S(2)}, u32[]{:S(2)}) collective-permute-start(f32[96,384]{1,0:T(8,128)S(1)} %get-tuple-element.223), channel_id=1, source_target_pairs={{0,2},{1,18},{2,34},{3,50},{4,66},{5,82},{6,98},{7,114},{8,6},{9,2... | collective-permute-start | bytes 442376 | tf_op jit(solution)/shard_map/ppermute | solution.py:56
  277.7 26.8 %collective-permute-start.21 = (f32[96,384]{1,0:T(8,128)S(1)}, f32[96,384]{1,0:T(8,128)S(1)}, u32[]{:S(2)}, u32[]{:S(2)}) collective-permute-start(f32[96,384]{1,0:T(8,128)S(1)} %get-tuple-element.222), channel_id=1, source_target_pairs={{0,64},{1,65},{2,66},{3,67},{4,68},{5,69},{6,70},{7,71},{8,72},{9,... | collective-permute-start | bytes 442376 | tf_op jit(solution)/shard_map/ppermute | solution.py:56
  306.5 42.4 %all-to-all-start.4 = ((f32[8,192,384]{2,1,0:T(8,128)}), f32[8,192,384]{2,1,0:T(8,128)}, u32[]{:S(2)}, u32[]{:S(2)}) async-start(f32[8,192,384]{2,1,0:T(8,128)} %broadcast_in_dim.65), calls=%async_computation.6 | async-start | bytes 4718592 | tf_op jit(solution)/shard_map/all_to_all | solution.py:120
  350.4 32.0 %all-to-all-start.5 = ((f32[8,112,512]{2,1,0:T(8,128)}), f32[8,112,512]{2,1,0:T(8,128)S(1)}, u32[]{:S(2)}, u32[]{:S(2)}) async-start(f32[8,112,512]{2,1,0:T(8,128)} %broadcast_in_dim.67), calls=%async_computation.7 | async-start | bytes 3670016 | tf_op jit(solution)/shard_map/all_to_all | solution.py:120
  (39 other events, 395.1 us)
Sparse Core Ops, SparseCore 0:
  31.7 33.3 all-gather.3
  67.4 54.1 all-gather.5
  131.3 94.8 all-gather.7
  228.4 39.9 reduce-scatter.2
  270.7 41.2 reduce-scatter.4

commit v6 on v3

--- a/solution.py
+++ b/solution.py
@@ -1256,12 +1256,11 @@
     tail, small_own = run_rest(
         seg_ends, grad_bc, pre, proj, par, grad_x, grad_dtraw, grad_sums, grad_heads, grad_gain, (r * OWN_BC)[None]
     )
-    grad_tail = run_tail_grad(normed, tail, small_own)
-    tail, grad_tail, low_rows = lax.optimization_barrier((tail, grad_tail, low_rows))
+    tail, small_own, low_rows = lax.optimization_barrier((tail, small_own, low_rows))
     tail_rows = exchange(tail.reshape(N_REP, ROWS, TAIL), "rep")
-    tail_part = scatter_eight(grad_tail)
     block_out = run_block_out(low_rows, full_out, tokens, own_live)
-    early, block_out = lax.optimization_barrier((early, block_out))
+    block_out, early, small_own = lax.optimization_barrier((block_out, early, small_own))
+    tail_part = scatter_eight(run_tail_grad(normed, tail, small_own))
     mine, other = at(early, place.yh), at(early, 1 - place.yh)
     out_mine = move(
         mine[:SHARD_IN], lambda yh, z, c, x, yl: (x // 2, (x % 2) * 2 + yl, z % 2, 2 * c + yh, z // 2)

time: 393 us -> 410 us (1.043)
  waiting for transfers between devices: 85.8 us -> 101 us
    ppermute x28, waiting for transfers between devices: 49.8 us -> 64.1 us  [move(): return lax.ppermute(value, ('fsdp', 'rep'), pairs)]
  transfers between devices with their start and end apart: 38 -> 38, of which waited for: 18 -> 18; matrix products, arithmetic and copies ran while one was open for 7% -> 6% of each run, Pallas kernels for 42% -> 38%
where the time goes in v6:
time: 410 us; the launch traced here: 407 us
  Pallas kernels  171 us (42%)
  waiting for transfers between devices  101 us (25%)
  starting transfers between devices  73.1 us (18%)
  local copies, waits for them, and re-layouts  20.8 us (5%)
  other arithmetic  16.3 us (4%)
  between operations  14.5 us (4%)
  blocking collectives  10.2 us (2%)
    ppermute x28, waiting for transfers between devices, move(): return lax.ppermute(value, ('fsdp', 'rep'), pairs)  64.1 us
    ppermute x28, starting transfers between devices, move(): return lax.ppermute(value, ('fsdp', 'rep'), pairs)  47.5 us
    pallas_call x1, Pallas kernels, run_backward(): pl.pallas_call(backward_kernel, grid=(CHUNKS,), in_specs=[pl.BlockSpec(me...  32.1 us
    all_to_all x5, waiting for transfers between devices, exchange(): return lax.all_to_all(value, axis, 0, 0, tiled=True)  30.6 us
    all_to_all x5, starting transfers between devices, exchange(): return lax.all_to_all(value, axis, 0, 0, tiled=True)  25.2 us
    pallas_call x2, Pallas kernels, run_forward(): pl.pallas_call(partial(forward_kernel, part), grid=(HALF,), in_specs=[pl....  24.2 us
    pallas_call x1, Pallas kernels, run_project(): pl.pallas_call(partial(project_kernel, PARTS), grid_spec=pltpu.PrefetchSc...  17.4 us
    pallas_call x1, Pallas kernels, run_out_grad(): pl.pallas_call(out_grad_kernel, grid_spec=pltpu.PrefetchScalarGridSpec(nu...  13.6 us
  transfers between devices with their start and end apart: 38, of which 18 were waited for; matrix products, arithmetic and copies ran while one was open for 6% of the time, Pallas kernels for 38%

profile of v6, /device:TPU:0, one launch (start us, length us, event | category | flops | bytes accessed | tf_op | source)
XLA Modules:
  0.0 407.5 jit_solution(14986025272217593332)
XLA Ops:
  38.8 11.8 %collective-permute-done.7 = bf16[192,1536]{1,0:T(8,128)(2,1)S(1)} collective-permute-done((bf16[192,1536]{1,0:T(8,128)(2,1)S(1)}, bf16[192,1536]{1,0:T(8,128)(2,1)S(1)}, u32[]{:S(2)}, u32[]{:S(2)}) %collective-permute-start.7) | collective-permute-done | bytes 589856 | tf_op jit(solution)/shard_map/ppermute | solution.py:56
  74.3 17.4 %project.1 = (bf16[2048,1536]{1,0:T(8,128)(2,1)}, f32[2048,1152]{1,0:T(8,128)}, bf16[1536,128]{1,0:T(8,128)(2,1)}) custom-call(s32[8]{0:T(128)} %fusion.5.table, bf16[256,1536]{1,0:T(8,128)(2,1)} %tokens.3, bf16[256,1536]{1,0:T(8,128)(2,1)} %collective-permute-done.2.refs_1_, bf16[256,1536]{1,0:T(8,128)(2,1)} %collective-permute-done.1.refs_2_, ...), custom_call_target="tpu_custom_call" | custom-call | flops 1000000 | bytes 100000 | tf_op jit(solution)/shard_map/project/pallas_call | solution.py:578
  97.1 12.1 %scan_forward.2 = (f32[2048,640]{1,0:T(8,128)}, f32[2048,384]{1,0:T(8,128)}, f32[2048,384]{1,0:T(8,128)}, f32[136,640]{1,0:T(8,128)}) custom-call(s32[3]{0:T(128)} %bitcast.92, f32[2048,1152]{1,0:T(8,128)} %get-tuple-element.128.proj.refs_11_.gate_in.conv_in.dt_in, f32[16,640]{1,0:T(8,128)} %concatenate.39.par), custom_call_target="tpu_custom_call" | custom-call | flops 1000000 | bytes 100000 | tf_op jit(solution)/shard_map/scan_forward/pallas_call | solution.py:349
  115.8 12.2 %scan_forward.3 = (f32[2048,640]{1,0:T(8,128)}, f32[2048,384]{1,0:T(8,128)}, f32[2048,384]{1,0:T(8,128)}, f32[136,640]{1,0:T(8,128)}) custom-call(s32[3]{0:T(128)} %bitcast.93, f32[2048,1152]{1,0:T(8,128)} %get-tuple-element.128.proj.refs_11_.gate_in.conv_in.dt_in, ...), custom_call_target="tpu_custom_call", output_to_operand_aliasing={{0}: (3, {}), {1}: (4, {}), {2}: (5, {})} | custom-call | flops 1000000 | bytes 100000 | tf_op jit(solution)/shard_map/scan_forward/pallas_call | solution.py:349
  133.0 13.6 %out_grad.1 = (bf16[2048,1536]{1,0:T(8,128)(2,1)}, f32[2048,384]{1,0:T(8,128)}, f32[8,2048]{1,0:T(8,128)}) custom-call(s32[9]{0:T(128)} %pad_add_fusion.table, bf16[256,1536]{1,0:T(8,128)(2,1)} %copy-done.6, bf16[256,1536]{1,0:T(8,128)(2,1)} %collective-permute-done.10.refs_1_, bf16[256,1536]{1,0:T(8,128)(2,1)} %copy-done.12, bf16[256,1536]{1,0:T(8,128)(2,1)} %copy-done.9, ...), custom_call_target="tpu_custom_call" | custom-call | flops 1000000 | bytes 100000 | tf_op jit(solution)/shard_map/out_grad/pallas_call | solution.py:635
  147.6 10.2 %all_to_all.34 = f32[8,32,128]{2,1,0:T(8,128)S(1)} all-to-all(f32[8,32,128]{2,1,0:T(8,128)S(1)} %broadcast_in_dim.62), channel_id=1, replica_groups=mesh['fsdp'=16,'rep'=8] {'rep'}, dimensions={0} | all-to-all | bytes 262144 | tf_op jit(solution)/shard_map/all_to_all | solution.py:120
  158.5 10.5 %gate_backward.1 = (bf16[2048,768]{1,0:T(8,128)(2,1)}, f32[2048,384]{1,0:T(8,128)}, f32[8,384]{1,0:T(8,128)}) custom-call(f32[2048,384]{1,0:T(8,128)} %get-tuple-element.147.grad_out, f32[2048,384]{1,0:T(8,128)} %get-tuple-element.146.refs_10_.mixed_in, f32[2048,1152]{1,0:T(8,128)} %get-tuple-element.128.proj.refs_11_.gate_in.conv_in.dt_in, ...), custom_call_target="tpu_custom_call" | custom-call | flops 1000000 | bytes 100000 | tf_op jit(solution)/shard_map/gate_backward/pallas_call | solution.py:690
  172.7 32.1 %scan_backward.1 = (bf16[2048,384]{1,0:T(8,128)(2,1)}, bf16[2048,128]{1,0:T(8,128)(2,1)}, f32[256,2048]{1,0:T(8,128)}, f32[8,384]{1,0:T(8,128)}, f32[8,128]{1,0:T(8,128)}) custom-call(s32[3]{0:T(128)} %bitcast.94, f32[2048,1152]{1,0:T(8,128)} %get-tuple-element.128.proj.refs_11_.gate_in.conv_in.dt_in, ...), custom_call_target="tpu_custom_call" | custom-call | flops 1000000 | bytes 100000 | tf_op jit(solution)/shard_map/scan_backward/pallas_call | solution.py:477
  204.7 12.7 %early_grad.1 = f32[16,192,384]{2,1,0:T(8,128)} custom-call(bf16[2048,768]{1,0:T(8,128)(2,1)} %get-tuple-element.154.low, bf16[2048,1536]{1,0:T(8,128)(2,1)} %get-tuple-element.155.grad_branch, bf16[2048,1536]{1,0:T(8,128)(2,1)} %get-tuple-element.156.normed), custom_call_target="tpu_custom_call" | custom-call | flops 1000000 | bytes 100000 | tf_op jit(solution)/shard_map/early_grad/pallas_call | solution.py:734
  219.1 5.4 %all-to-all-start.2 = ((f32[8,32,2048]{2,1,0:T(8,128)}), f32[8,32,2048]{2,1,0:T(8,128)S(1)}, u32[]{:S(2)}, u32[]{:S(2)}) async-start(f32[8,32,2048]{2,1,0:T(8,128)} %bitcast.78), calls=%async_computation.2 | async-start | bytes 4194304 | tf_op jit(solution)/shard_map/all_to_all | solution.py:120
  226.2 7.8 %z_grad.1.grad_z = f32[1536,256]{1,0:T(8,128)} custom-call(bf16[8,256,768]{2,1,0:T(8,128)(2,1)} %copy-done.2, bf16[4,2,2,96,6400]{4,3,2,1,0:T(8,128)(2,1)} %bitcast.66), custom_call_target="tpu_custom_call" | custom-call | flops 2400000000 | bytes 20000000 | tf_op jit(solution)/shard_map/z_grad/pallas_call | solution.py:807
  233.9 14.6 %all-to-all-done.2.parts = f32[8,32,2048]{2,1,0:T(8,128)S(1)} async-done(((f32[8,32,2048]{2,1,0:T(8,128)}), f32[8,32,2048]{2,1,0:T(8,128)S(1)}, u32[]{:S(2)}, u32[]{:S(2)}) %all-to-all-start.2) | async-done | bytes 2097184 | tf_op jit(solution)/shard_map/all_to_all | solution.py:120
  249.8 6.8 %rest_backward.1 = (bf16[2048,512]{1,0:T(8,128)(2,1)}, f32[8,512]{1,0:T(8,128)}) custom-call(s32[3]{0:T(128)} %bitcast.95, f32[8,32,2048]{2,1,0:T(8,128)} %copy-done.5, f32[2048,640]{1,0:T(8,128)} %get-tuple-element.150.pre_in.pre_b.pre_c, f32[2048,640]{1,0:T(8,128)} %get-tuple-element.150.pre_in.pre_b.pre_c, ...), custom_call_target="tpu_custom_call" | custom-call | flops 1000000 | bytes 100000 | tf_op jit(solution)/shard_map/rest_backward/pallas_call | solution.py:959
  256.7 8.3 %block_out.1 = f32[256,1536]{1,0:T(8,128)} custom-call(bf16[8,256,768]{2,1,0:T(8,128)(2,1)} %copy-done.2, bf16[4,2,2,192,1536]{4,3,2,1,0:T(8,128)(2,1)} %bitcast.70, bf16[256,1536]{1,0:T(8,128)(2,1)} %tokens.3, f32[256,1]{1,0:T(8,128)} %fusion.1.live), custom_call_target="tpu_custom_call" | custom-call | flops 2400000000 | bytes 20000000 | tf_op jit(solution)/shard_map/block_out/pallas_call | solution.py:767
  268.4 8.9 %tail_grad.1 = f32[16,104,512]{2,1,0:T(8,128)} custom-call(bf16[2048,1536]{1,0:T(8,128)(2,1)} %get-tuple-element.156.normed, bf16[2048,512]{1,0:T(8,128)(2,1)} %get-tuple-element.176.tail, f32[8,512]{1,0:T(8,128)} %get-tuple-element.181.small), custom_call_target="tpu_custom_call" | custom-call | flops 1000000 | bytes 100000 | tf_op jit(solution)/shard_map/tail_grad/pallas_call | solution.py:1005
  277.3 5.2 %all-to-all-start.3 = ((bf16[8,256,512]{2,1,0:T(8,128)(2,1)}), bf16[8,256,512]{2,1,0:T(8,128)(2,1)S(1)}, u32[]{:S(2)}, u32[]{:S(2)}) async-start(bf16[8,256,512]{2,1,0:T(8,128)(2,1)} %bitcast.74), calls=%async_computation.4 | async-start | bytes 4194304 | tf_op jit(solution)/shard_map/all_to_all | solution.py:120
  289.6 19.3 %collective-permute-done.20 = f32[96,384]{1,0:T(8,128)S(1)} collective-permute-done((f32[96,384]{1,0:T(8,128)S(1)}, f32[96,384]{1,0:T(8,128)S(1)}, u32[]{:S(2)}, u32[]{:S(2)}) %collective-permute-start.20) | collective-permute-done | bytes 147488 | tf_op jit(solution)/shard_map/ppermute | solution.py:56
  315.5 6.2 %all-to-all-start.4 = ((f32[8,192,384]{2,1,0:T(8,128)}), f32[8,192,384]{2,1,0:T(8,128)}, u32[]{:S(2)}, u32[]{:S(2)}) async-start(f32[8,192,384]{2,1,0:T(8,128)} %broadcast_in_dim.66), calls=%async_computation.6 | async-start | bytes 4718592 | tf_op jit(solution)/shard_map/all_to_all | solution.py:120
  321.6 11.1 %input_grad.1 = (f32[256,1536]{1,0:T(8,128)}, f32[8,512]{1,0:T(8,128)}) custom-call(s32[1]{0:T(128)} %bitcast.21.own_half, f32[1536,256]{1,0:T(8,128)} %z_grad.1.grad_z, bf16[8,256,512]{2,1,0:T(8,128)(2,1)} %copy-done.4, bf16[8,256,512]{2,1,0:T(8,128)(2,1)} %copy-done.4, bf16[4,2,2,96,6400]{4,3,2,1,0:T(8,128)(2,1)} %bitcast.67, ...), custom_call_target="tpu_custom_call" | custom-call | flops 1000000 | bytes 100000 | tf_op jit(solution)/shard_map/input_grad/pallas_call | solution.py:874
  347.4 9.5 %collective-permute-done.27 = f32[8,512]{1,0:T(8,128)S(1)} collective-permute-done((f32[8,512]{1,0:T(8,128)S(1)}, f32[8,512]{1,0:T(8,128)S(1)}, u32[]{:S(2)}, u32[]{:S(2)}) %collective-permute-start.27) | collective-permute-done | bytes 16416 | tf_op jit(solution)/shard_map/ppermute | solution.py:56
  364.2 5.7 %adam.2 = (f32[96,6400]{1,0:T(8,128)}, f32[96,6400]{1,0:T(8,128)}, f32[96,6400]{1,0:T(8,128)}, f32[96,6400]{1,0:T(8,128)}) custom-call(f32[8,192,384]{2,1,0:T(8,128)} %all-to-all-done.4.pair, f32[96,6400]{1,0:T(8,128)} %refs_0_.6, f32[96,6400]{1,0:T(8,128)} %refs_1_.4, f32[96,6400]{1,0:T(8,128)} %refs_2_.4), custom_call_target="tpu_custom_call" | custom-call | flops 2400000000 | bytes 20000000 | tf_op jit(solution)/shard_map/adam/pallas_call | solution.py:1043
  370.0 5.3 %adam.3 = (f32[192,1536]{1,0:T(8,128)}, f32[192,1536]{1,0:T(8,128)}, f32[192,1536]{1,0:T(8,128)}, f32[192,1536]{1,0:T(8,128)}) custom-call(f32[8,192,384]{2,1,0:T(8,128)} %all-to-all-done.4.pair, f32[192,1536]{1,0:T(8,128)} %refs_0_.7, f32[192,1536]{1,0:T(8,128)} %refs_1_.5, f32[192,1536]{1,0:T(8,128)} %refs_2_.5), custom_call_target="tpu_custom_call" | custom-call | flops 2400000000 | bytes 20000000 | tf_op jit(solution)/shard_map/adam/pallas_call | solution.py:1043
  375.3 16.0 %all-to-all-done.5.pair.rest = f32[8,112,512]{2,1,0:T(8,128)S(1)} async-done(((f32[8,112,512]{2,1,0:T(8,128)}), f32[8,112,512]{2,1,0:T(8,128)S(1)}, u32[]{:S(2)}, u32[]{:S(2)}) %all-to-all-start.5) | async-done | bytes 1835040 | tf_op jit(solution)/shard_map/all_to_all | solution.py:120
  394.1 6.9 %adam_tail.1 = (f32[96,6400]{1,0:T(8,128)}, f32[96,6400]{1,0:T(8,128)}, f32[96,6400]{1,0:T(8,128)}, f32[96,6400]{1,0:T(8,128)}) custom-call(f32[8,112,512]{2,1,0:T(8,128)} %copy-done.3, f32[8,112,512]{2,1,0:T(8,128)} %copy-done.3, f32[96,6400]{1,0:T(8,128)} %refs_0_.6, ...), custom_call_target="tpu_custom_call", output_to_operand_aliasing={{0}: (5, {}), {1}: (6, {}), {2}: (7, {}), {3}: (8, {})} | custom-call | flops 1000000 | bytes 100000 | tf_op jit(solution)/shard_map/adam_tail/pallas_call | solution.py:1086
  (223 shorter events, 123.4 us)
Async XLA Ops:
  7.2 57.9 %all-gather.4.cloned.1.call-start = ((), (), s32[]{:S(2)}) async-start(), calls=%async_computation.8 | async-start | bytes 4644864 | tf_op jit(solution)/shard_map/all_gather | solution.py:115
  7.3 20.8 %collective-permute-start = (bf16[256,1536]{1,0:T(8,128)(2,1)}, bf16[256,1536]{1,0:T(8,128)(2,1)}, u32[]{:S(2)}, u32[]{:S(2)}) collective-permute-start(bf16[256,1536]{1,0:T(8,128)(2,1)} %tokens.3), channel_id=1, source_target_pairs={{0,2},{1,3},{2,4},{3,5},{4,6},{5,7},{6,0},{7,1},{8,10},{9,11},{10,... | collective-permute-start | bytes 2359304 | tf_op jit(solution)/shard_map/ppermute | solution.py:56
  8.9 19.3 %collective-permute-start.1 = (bf16[256,1536]{1,0:T(8,128)(2,1)}, bf16[256,1536]{1,0:T(8,128)(2,1)}, u32[]{:S(2)}, u32[]{:S(2)}) collective-permute-start(bf16[256,1536]{1,0:T(8,128)(2,1)} %tokens.3), channel_id=1, source_target_pairs={{0,6},{1,7},{2,0},{3,1},{4,2},{5,3},{6,4},{7,5},{8,14},{9,15},{10,... | collective-permute-start | bytes 2359304 | tf_op jit(solution)/shard_map/ppermute | solution.py:56
  10.6 19.0 %collective-permute-start.2 = (bf16[256,1536]{1,0:T(8,128)(2,1)}, bf16[256,1536]{1,0:T(8,128)(2,1)}, u32[]{:S(2)}, u32[]{:S(2)}) collective-permute-start(bf16[256,1536]{1,0:T(8,128)(2,1)} %tokens.3), channel_id=1, source_target_pairs={{0,1},{1,0},{2,3},{3,2},{4,5},{5,4},{6,7},{7,6},{8,9},{9,8},{10,11... | collective-permute-start | bytes 2359304 | tf_op jit(solution)/shard_map/ppermute | solution.py:56
  31.6 101.4 %all-gather.6.cloned.1.call-start = ((), (), s32[]{:S(2)}) async-start(), calls=%async_computation.9 | async-start | bytes 10616832 | tf_op jit(solution)/shard_map/all_gather | solution.py:115
  31.7 19.3 %collective-permute-start.4 = (bf16[256,1536]{1,0:T(8,128)(2,1)}, bf16[256,1536]{1,0:T(8,128)(2,1)S(1)}, u32[]{:S(2)}, u32[]{:S(2)}) collective-permute-start(bf16[256,1536]{1,0:T(8,128)(2,1)} %collective-permute-done.refs_7_), channel_id=1, source_target_pairs={{0,2},{1,3},{2,4},{3,5},{4,6},{5,7},{6,0},{7,1},{8,10},{9,11},{10,... | collective-permute-start | bytes 2359304 | tf_op jit(solution)/shard_map/ppermute | solution.py:56
  32.1 18.8 %collective-permute-start.5 = (bf16[256,1536]{1,0:T(8,128)(2,1)}, bf16[256,1536]{1,0:T(8,128)(2,1)S(1)}, u32[]{:S(2)}, u32[]{:S(2)}) collective-permute-start(bf16[256,1536]{1,0:T(8,128)(2,1)} %collective-permute-done.refs_7_), channel_id=1, source_target_pairs={{0,1},{1,0},{2,3},{3,2},{4,5},{5,4},{6,7},{7,6},{8,9},{9,8},{10,11... | collective-permute-start | bytes 2359304 | tf_op jit(solution)/shard_map/ppermute | solution.py:56
  65.1 161.0 %all-gather.8.cloned.1.call-start = ((), (), s32[]{:S(2)}) async-start(), calls=%async_computation.10 | async-start | bytes 22118400 | tf_op jit(solution)/shard_map/all_gather | solution.py:115
  65.7 26.0 %collective-permute-start.8 = (bf16[256,1536]{1,0:T(8,128)(2,1)S(1)}, bf16[256,1536]{1,0:T(8,128)(2,1)}, u32[]{:S(2)}, u32[]{:S(2)}) collective-permute-start(bf16[256,1536]{1,0:T(8,128)(2,1)S(1)} %multiply_convert_fusion.refs_0_), channel_id=1, source_target_pairs={{0,2},{1,3},{2,4},{3,5},{4,6},{5,7},{6,0},{7,1},{8,10},{9,11},{10,... | collective-permute-start | bytes 2359304 | tf_op jit(solution)/shard_map/ppermute | solution.py:56
  67.2 24.5 %collective-permute-start.9 = (bf16[256,1536]{1,0:T(8,128)(2,1)S(1)}, bf16[256,1536]{1,0:T(8,128)(2,1)S(1)}, u32[]{:S(2)}, u32[]{:S(2)}) collective-permute-start(bf16[256,1536]{1,0:T(8,128)(2,1)S(1)} %multiply_convert_fusion.refs_0_), channel_id=1, source_target_pairs={{0,6},{1,7},{2,0},{3,1},{4,2},{5,3},{6,4},{7,5},{8,14},{9,15},{10,... | collective-permute-start | bytes 2359304 | tf_op jit(solution)/shard_map/ppermute | solution.py:56
  68.9 22.8 %collective-permute-start.10 = (bf16[256,1536]{1,0:T(8,128)(2,1)S(1)}, bf16[256,1536]{1,0:T(8,128)(2,1)}, u32[]{:S(2)}, u32[]{:S(2)}) collective-permute-start(bf16[256,1536]{1,0:T(8,128)(2,1)S(1)} %multiply_convert_fusion.refs_0_), channel_id=1, source_target_pairs={{0,1},{1,0},{2,3},{3,2},{4,5},{5,4},{6,7},{7,6},{8,9},{9,8},{10,11... | collective-permute-start | bytes 2359304 | tf_op jit(solution)/shard_map/ppermute | solution.py:56
  70.4 57.6 %collective-permute-start.16 = (bf16[96,6400]{1,0:T(8,128)(2,1)S(1)}, bf16[96,6400]{1,0:T(8,128)(2,1)}, u32[]{:S(2)}, u32[]{:S(2)}) collective-permute-start(bf16[96,6400]{1,0:T(8,128)(2,1)S(1)} %convert_element_type.48), channel_id=1, source_target_pairs={{0,65},{1,64},{2,67},{3,66},{4,69},{5,68},{6,71},{7,70},{8,73},{9,... | collective-permute-start | bytes 3686408 | tf_op jit(solution)/shard_map/ppermute | solution.py:56
  91.7 20.0 %collective-permute-start.13 = (bf16[256,1536]{1,0:T(8,128)(2,1)}, bf16[256,1536]{1,0:T(8,128)(2,1)}, u32[]{:S(2)}, u32[]{:S(2)}) collective-permute-start(bf16[256,1536]{1,0:T(8,128)(2,1)} %collective-permute-done.8.refs_7_), channel_id=1, source_target_pairs={{0,2},{1,3},{2,4},{3,5},{4,6},{5,7},{6,0},{7,1},{8,10},{9,11},{10,... | collective-permute-start | bytes 2359304 | tf_op jit(solution)/shard_map/ppermute | solution.py:56
  92.6 19.1 %collective-permute-start.14 = (bf16[256,1536]{1,0:T(8,128)(2,1)}, bf16[256,1536]{1,0:T(8,128)(2,1)S(1)}, u32[]{:S(2)}, u32[]{:S(2)}) collective-permute-start(bf16[256,1536]{1,0:T(8,128)(2,1)} %collective-permute-done.8.refs_7_), channel_id=1, source_target_pairs={{0,1},{1,0},{2,3},{3,2},{4,5},{5,4},{6,7},{7,6},{8,9},{9,8},{10,11... | collective-permute-start | bytes 2359304 | tf_op jit(solution)/shard_map/ppermute | solution.py:56
  93.0 18.7 %collective-permute-start.15 = (bf16[256,1536]{1,0:T(8,128)(2,1)}, bf16[256,1536]{1,0:T(8,128)(2,1)S(1)}, u32[]{:S(2)}, u32[]{:S(2)}) collective-permute-start(bf16[256,1536]{1,0:T(8,128)(2,1)} %collective-permute-done.10.refs_1_), channel_id=1, source_target_pairs={{0,6},{1,7},{2,0},{3,1},{4,2},{5,3},{6,4},{7,5},{8,14},{9,15},{10,... | collective-permute-start | bytes 2359304 | tf_op jit(solution)/shard_map/ppermute | solution.py:56
  168.9 48.5 %all-to-all-start.1 = ((bf16[8,256,768]{2,1,0:T(8,128)(2,1)}), bf16[8,256,768]{2,1,0:T(8,128)(2,1)S(1)}, u32[]{:S(2)}, u32[]{:S(2)}) async-start(bf16[8,256,768]{2,1,0:T(8,128)(2,1)} %bitcast.73), calls=%async_computation.1 | async-start | bytes 6291456 | tf_op jit(solution)/shard_map/all_to_all | solution.py:120
  172.6 95.8 %reduce-scatter.3.cloned.1.call-start = ((), (), s32[]{:S(2)}) async-start(), calls=%async_computation.11 | async-start | bytes 5308416 | tf_op jit(solution)/shard_map/reduce_scatter | solution.py:135
  219.1 29.4 %all-to-all-start.2 = ((f32[8,32,2048]{2,1,0:T(8,128)}), f32[8,32,2048]{2,1,0:T(8,128)S(1)}, u32[]{:S(2)}, u32[]{:S(2)}) async-start(f32[8,32,2048]{2,1,0:T(8,128)} %bitcast.78), calls=%async_computation.2 | async-start | bytes 4194304 | tf_op jit(solution)/shard_map/all_to_all | solution.py:120
  224.5 108.3 %reduce-scatter.5.cloned.1.call-start = ((), (), s32[]{:S(2)}) async-start(), calls=%async_computation.12 | async-start | bytes 3833856 | tf_op jit(solution)/shard_map/reduce_scatter | solution.py:135
  277.3 36.1 %all-to-all-start.3 = ((bf16[8,256,512]{2,1,0:T(8,128)(2,1)}), bf16[8,256,512]{2,1,0:T(8,128)(2,1)S(1)}, u32[]{:S(2)}, u32[]{:S(2)}) async-start(bf16[8,256,512]{2,1,0:T(8,128)(2,1)} %bitcast.74), calls=%async_computation.4 | async-start | bytes 4194304 | tf_op jit(solution)/shard_map/all_to_all | solution.py:120
  283.3 25.7 %collective-permute-start.20 = (f32[96,384]{1,0:T(8,128)S(1)}, f32[96,384]{1,0:T(8,128)S(1)}, u32[]{:S(2)}, u32[]{:S(2)}) collective-permute-start(f32[96,384]{1,0:T(8,128)S(1)} %get-tuple-element.223), channel_id=1, source_target_pairs={{0,2},{1,18},{2,34},{3,50},{4,66},{5,82},{6,98},{7,114},{8,6},{9,2... | collective-permute-start | bytes 442376 | tf_op jit(solution)/shard_map/ppermute | solution.py:56
  286.6 26.8 %collective-permute-start.21 = (f32[96,384]{1,0:T(8,128)S(1)}, f32[96,384]{1,0:T(8,128)S(1)}, u32[]{:S(2)}, u32[]{:S(2)}) collective-permute-start(f32[96,384]{1,0:T(8,128)S(1)} %get-tuple-element.222), channel_id=1, source_target_pairs={{0,64},{1,65},{2,66},{3,67},{4,68},{5,69},{6,70},{7,71},{8,72},{9,... | collective-permute-start | bytes 442376 | tf_op jit(solution)/shard_map/ppermute | solution.py:56
  315.5 42.4 %all-to-all-start.4 = ((f32[8,192,384]{2,1,0:T(8,128)}), f32[8,192,384]{2,1,0:T(8,128)}, u32[]{:S(2)}, u32[]{:S(2)}) async-start(f32[8,192,384]{2,1,0:T(8,128)} %broadcast_in_dim.66), calls=%async_computation.6 | async-start | bytes 4718592 | tf_op jit(solution)/shard_map/all_to_all | solution.py:120
  359.4 32.0 %all-to-all-start.5 = ((f32[8,112,512]{2,1,0:T(8,128)}), f32[8,112,512]{2,1,0:T(8,128)S(1)}, u32[]{:S(2)}, u32[]{:S(2)}) async-start(f32[8,112,512]{2,1,0:T(8,128)} %broadcast_in_dim.67), calls=%async_computation.7 | async-start | bytes 3670016 | tf_op jit(solution)/shard_map/all_to_all | solution.py:120
  (39 other events, 417.6 us)
Sparse Core Ops, SparseCore 0:
  31.7 33.3 all-gather.3
  67.4 54.1 all-gather.5
  131.3 94.8 all-gather.7
  228.4 39.8 reduce-scatter.2
  277.4 41.9 reduce-scatter.4
